TPU v7x, 32 devices: a whole 2x2x4 slice. The times are simulated.
32 devices in a mesh: sec: 4 (over y, core), strip: 8 (over z, x).
Axes of the slice: x: 2, y: 2, z: 4, core: 2. Of those that a mesh axis runs over, the one named last changes fastest.
Arguments:
- positions: float32 [12, 2, 512, 1024], P('sec', None, 'strip'), may hold values from -6 to 6
- velocity: float32 [12, 2, 512, 1024], P('sec', None, 'strip'), may hold values from -4 to 4
- spring_class: int32 [12, 2, 512, 1024], P('sec', None, 'strip'), may hold values from 0 to 7
- match_shift: int32 [12, 2, 64, 8], P('sec', None, 'strip'), may hold values from -3 to 3
- fixed: int32 [12], P('sec'), may hold values 0 or 1
- class_stiffness: float32 [8], replicated, may hold values from 0.1 to 1
- cross_stiffness: float32 [2], replicated, may hold values from 0.2 to 1
Outputs:
- new_positions: float32 [12, 2, 512, 1024], P('sec', None, 'strip')
- new_velocity: float32 [12, 2, 512, 1024], P('sec', None, 'strip')
All inputs are finite; a program needn't handle non-finite values. No bound on the sum of `fixed` on one device may be relied on, other than what follows from the above.
Results may differ from a plain program's by a relative error of at most 0.0003.
Values sent between devices are 32-bit elements; how exact they have to be, the bound alone decides.
No kernel may reach another device: no remote copies, remote signals or barrier semaphores. Data moves between devices by JAX's collectives and lax.ppermute only.
A program may use at most 64 MiB of HBM per device.

v0:
```python
import jax
import jax.numpy as jnp
from jax import lax
from jax.experimental import pallas as pl
from jax.experimental.pallas import tpu as pltpu
from jax.sharding import PartitionSpec as P

ROWS = 8
COLS = 128
CLASSES = 8
DAMPING = 0.9
STEP = 0.35

VMEM = pl.BlockSpec(memory_space=pltpu.VMEM)
ANY = pl.BlockSpec(memory_space=pl.ANY)

INSIDE, SLOW, FAST, TABLE, MOVING = 0, 2, 4, 6, 7


def exchange(value, axis, pairing):
    n = lax.axis_size(axis)
    first = 0 if pairing == "a" else 1
    route = []
    for i in range(first, n - 1, 2):
        route += [(i, i + 1), (i + 1, i)]
    return lax.ppermute(value, axis, route)


def slow_after():
    return lax.rem(lax.axis_index("sec"), 2) == 1


def by_side(body):
    after = slow_after()

    @pl.when(after)
    def _():
        body(True)

    @pl.when(jnp.logical_not(after))
    def _():
        body(False)


def near_of(after, sections):
    return sections - 1 if after else 0


def second_of(after, sections):
    return sections - 2 if after else 1


def pairs_of(after, sections):
    near, second = near_of(after, sections), second_of(after, sections)
    return ((near, 0, 1), (second, 0, 2), (near, 1, 2))


def inverse(value):
    guess = pl.reciprocal(value, approx=True)
    return guess * (2.0 - value * guess)


def flow(ex, ey, half):
    gain = half * (3.0 - inverse(1.0 + ex * ex + ey * ey))
    return gain * ex, gain * ey


def cols_of(cb):
    return slice(cb * COLS, (cb + 1) * COLS)


def rows_of(rb):
    start = rb * ROWS
    return pl.ds(start if isinstance(start, int) else pl.multiple_of(start, ROWS), ROWS)


def tail_rows(rows):
    return -(-(rows // ROWS) // ROWS) * ROWS


def per_tile(width, make):
    return jnp.concatenate([make(cb) for cb in range(width // COLS)], axis=1)


def turned(wide, amounts):
    return per_tile(wide.shape[1], lambda cb: pltpu.roll(wide[:, cols_of(cb)], amounts[cb], 1))


def gathered(wide, index):
    def one(cb):
        full = jnp.broadcast_to(index[:, cols_of(cb)], (ROWS, COLS))
        return jnp.take_along_axis(wide[:, cols_of(cb)], full, axis=1, mode="promise_in_bounds")

    return per_tile(wide.shape[1], one)


def spread(blocks, width):
    return per_tile(width, lambda cb: jnp.broadcast_to(blocks[:, cb : cb + 1], (blocks.shape[0], COLS)))


def lanes(rows, width):
    return lax.broadcasted_iota(jnp.int32, (rows, width), 1) & (COLS - 1)


def put_tail(shift, out, first, width):
    sections, _, rbs, _ = shift.shape
    lane = lanes(rbs, width)
    parts = [
        spread(shift[s, h], width)
        for s, h in ((sections - 1, 0), (sections - 1, 1), (sections - 2, 1))
    ]
    mixed = jnp.where(lane == 0, parts[0], jnp.where(lane == 1, parts[1], parts[2]))
    out[first : first + rbs, :] = mixed.astype(jnp.float32)


def put_index(after, shift, arrived, first, index):
    sections, _, rbs, _ = shift.shape
    width = index.shape[2]
    lane = lanes(rbs, width)
    for j, (own, _, hops) in enumerate(pairs_of(after, sections)):
        if after:
            offset = spread(shift[own, hops - 1], width)
        else:
            blocks = per_tile(
                width,
                lambda cb: jnp.broadcast_to(
                    arrived[first : first + rbs, cb * COLS + j : cb * COLS + j + 1], (rbs, COLS)
                ),
            )
            offset = -blocks.astype(jnp.int32)
        index[j, 0:rbs, :] = (lane + offset) & (COLS - 1)


def put_rims(u, rim_a, rim_b, kv_row):
    sections, _, rows, _ = u.shape
    odd = lax.rem(lax.axis_index("strip"), 2) == 1

    def put(line, first, last):
        rim_a[line : line + 1, :] = jnp.where(odd, first, last)
        rim_b[line : line + 1, :] = jnp.where(odd, last, first)

    for s in range(sections):
        for c in range(2):
            put(2 * s + c, u[s, c, 0:1, :], u[s, c, rows - 1 : rows, :])
        stiff = kv_row(s)
        put(2 * sections + s, stiff, stiff)


def look_up(table, index):
    def one(cb):
        tile = jnp.broadcast_to(index[:, cols_of(cb)], (ROWS, COLS))
        return jnp.take_along_axis(table, tile, axis=1, mode="promise_in_bounds")[: index.shape[0]]

    return per_tile(index.shape[1], one)


def lead_kernel(u, shift, near):
    sections, _, rows, width = u.shape

    def body(after):
        for c in range(2):
            near[c * rows : (c + 1) * rows, :] = u[near_of(after, sections), c]

    by_side(body)
    put_tail(shift, near, 2 * rows, width)


def prepare_kernel(u, cls, shift, stiff, cross, fixed, second, fast, rim_a, rim_b, splat):
    sections, _, rows, width = u.shape
    i, n = lax.axis_index("sec"), lax.axis_size("sec")
    odd = slow_after()

    def body(after):
        for c in range(2):
            second[c * rows : (c + 1) * rows, :] = u[second_of(after, sections), c]
            fast[c * rows : (c + 1) * rows, :] = u[near_of(not after, sections), c]
            fast[(2 + c) * rows : (3 + c) * rows, :] = u[second_of(not after, sections), c]

    by_side(body)
    put_tail(shift, fast, 4 * rows, width)
    tile = (ROWS, COLS)
    lane = lax.broadcasted_iota(jnp.int32, tile, 1)
    slow_there = jnp.where(odd, i < n - 1, i > 0)
    fast_there = jnp.where(odd, i > 0, i < n - 1)
    for h in range(2):
        k = jnp.full(tile, cross[h] * (0.5 * STEP))
        splat[INSIDE + h] = k
        splat[SLOW + h] = jnp.where(slow_there, k, 0.0)
        splat[FAST + h] = jnp.where(fast_there, k, 0.0)
    table = jnp.zeros(tile, jnp.float32)
    for k in range(CLASSES):
        table = jnp.where(lane == k, stiff[k] * (0.5 * STEP), table)
    splat[TABLE] = table
    for s in range(sections):
        splat[MOVING + s] = jnp.full(tile, jnp.where(fixed[s] == 0, 1.0, 0.0))
    put_rims(u, rim_a, rim_b, lambda s: look_up(table, cls[s, 1, rows - 1 : rows, :]))


def wide_splat(splat, k, width):
    tile = splat[k]
    return per_tile(width, lambda cb: tile)


def inside(u, w, total, half_across, half_below, shift, splat, scalars, sem):
    sections, _, rows, width = u.shape
    rbs, cbs = rows // ROWS, width // COLS
    load = pltpu.make_async_copy(shift, scalars, sem)
    load.start()
    last = lax.broadcasted_iota(jnp.int32, (ROWS, width), 1) == width - 1

    def across(rb, carry):
        at = rows_of(rb)
        for s in range(sections):
            x, y = u[s, 0, at, :], u[s, 1, at, :]
            half = jnp.where(last, 0.0, half_across(s, at))
            f = flow(pltpu.roll(x, width - 1, 1) - x, pltpu.roll(y, width - 1, 1) - y, half)
            new = [DAMPING * w[s, c, at, :] + (f[c] - pltpu.roll(f[c], 1, 1)) for c in range(2)]
            for c in range(2):
                total[s, c, at, :] = new[c]
        return carry

    lax.fori_loop(0, rbs, across, 0, unroll=2)
    bottom = lax.broadcasted_iota(jnp.int32, (rows, COLS), 0) == rows - 1

    def below(cb, carry):
        at = pl.ds(pl.multiple_of(cb * COLS, COLS), COLS)
        for s in range(sections):
            x, y = u[s, 0, :, at], u[s, 1, :, at]
            half = jnp.where(bottom, 0.0, half_below(s, at))
            f = flow(pltpu.roll(x, rows - 1, 0) - x, pltpu.roll(y, rows - 1, 0) - y, half)
            new = [total[s, c, :, at] + (f[c] - pltpu.roll(f[c], 1, 0)) for c in range(2)]
            for c in range(2):
                total[s, c, :, at] = new[c]
        return carry

    lax.fori_loop(0, cbs, below, 0)
    load.wait()

    def between(rb, carry):
        at = rows_of(rb)
        add = [[total[s, c, at, :] for c in range(2)] for s in range(sections)]
        for hops in (1, 2):
            half = wide_splat(splat, INSIDE + hops - 1, width)
            for s in range(sections - hops):
                offsets = [scalars[s, hops - 1, rb, cb] for cb in range(cbs)]
                there = [(-o) & (COLS - 1) for o in offsets]
                back = [o & (COLS - 1) for o in offsets]
                e = [turned(u[s + hops, c, at, :], there) - u[s, c, at, :] for c in range(2)]
                f = flow(e[0], e[1], half)
                for c in range(2):
                    add[s][c] = add[s][c] + f[c]
                    add[s + hops][c] = add[s + hops][c] - turned(f[c], back)
        for s in range(sections):
            for c in range(2):
                total[s, c, at, :] = add[s][c]
        return carry

    lax.fori_loop(0, rbs, between, 0, unroll=2)


def first_inside_kernel(u, w, cls, shift, splat, total, half, scalars, sem):
    table = splat[TABLE]

    def half_across(s, at):
        k = look_up(table, cls[s, 0, at, :])
        half[s, 0, at, :] = k
        half[s, 1, at, :] = look_up(table, cls[s, 1, at, :])
        return k

    def half_below(s, at):
        return half[s, 1, :, at]

    inside(u, w, total, half_across, half_below, shift, splat, scalars, sem)


def later_inside_kernel(u, w, half, shift, splat, total, scalars, sem):
    def half_across(s, at):
        return half[s, 0, at, :]

    def half_below(s, at):
        return half[s, 1, :, at]

    inside(u, w, total, half_across, half_below, shift, splat, scalars, sem)


def side_flow(u, own, arrived, first, index, j, half, rb):
    rows = u.shape[2]
    at = rows_of(rb)
    number = index[j, rb : rb + 1, :]
    e = [
        gathered(arrived[pl.ds(first + c * rows + rb * ROWS, ROWS), :], number) - u[own, c, at, :]
        for c in range(2)
    ]
    return flow(e[0], e[1], half)


def rims_and_fast(u, half, fast, rim_a, rim_b, splat, index, total):
    sections, _, rows, width = u.shape
    rbs = rows // ROWS

    def body(slow_is_after):
        for j, (own, block, hops) in enumerate(pairs_of(not slow_is_after, sections)):
            stiff = wide_splat(splat, FAST + hops - 1, width)
            for rb in range(rbs):
                f = side_flow(u, own, fast, 2 * block * rows, index, j, stiff, rb)
                for c in range(2):
                    total[own, c, rows_of(rb), :] += f[c]

    by_side(body)
    strip = lax.axis_index("strip")
    odd = lax.rem(strip, 2) == 1
    has_below = strip < lax.axis_size("strip") - 1

    def below(r):
        return jnp.where(odd, rim_b[r : r + 1, :], rim_a[r : r + 1, :])

    def above(r):
        return jnp.where(odd, rim_a[r : r + 1, :], rim_b[r : r + 1, :])

    last, top = slice(rows - 1, rows), slice(0, 1)
    for s in range(sections):
        stiff = jnp.where(has_below, half[s, 1, last, :], 0.0)
        f = flow(*[below(2 * s + c) - u[s, c, last, :] for c in range(2)], stiff)
        stiff = jnp.where(strip > 0, above(2 * sections + s), 0.0)
        g = flow(*[u[s, c, top, :] - above(2 * s + c) for c in range(2)], stiff)
        for c in range(2):
            total[s, c, last, :] += f[c]
            total[s, c, top, :] -= g[c]


def first_rims_kernel(u, total_in, half, fast, rim_a, rim_b, shift, splat, total, index):
    rows = u.shape[2]
    by_side(lambda after: put_index(not after, shift, fast, 4 * rows, index))
    rims_and_fast(u, half, fast, rim_a, rim_b, splat, index, total)


def later_rims_kernel(u, total_in, half, fast, rim_a, rim_b, index, splat, total):
    rims_and_fast(u, half, fast, rim_a, rim_b, splat, index, total)


def near_kernel(u, total_in, arrived, shift, splat, total, new_u, second, fast, index):
    sections, _, rows, width = u.shape
    rbs = rows // ROWS

    def body(after):
        put_index(after, shift, arrived, 2 * rows, index)
        pairs = pairs_of(after, sections)
        others = [s for s in range(sections) if s != near_of(after, sections)]
        for rb in range(rbs):
            at = rows_of(rb)
            value = {}
            for j in range(2):
                own, _, hops = pairs[j]
                stiff = wide_splat(splat, SLOW + hops - 1, width)
                f = side_flow(u, own, arrived, 0, index, j, stiff, rb)
                value[own] = [total[own, c, at, :] + f[c] for c in range(2)]
            for s in range(sections):
                for c in range(2):
                    v = value[s][c] if s in value else total[s, c, at, :]
                    if s in others:
                        v = v * wide_splat(splat, MOVING + s, width)
                        moved = u[s, c, at, :] + STEP * v
                        new_u[s, c, at, :] = moved
                        if s == second_of(after, sections):
                            second[pl.ds(c * rows + rb * ROWS, ROWS), :] = moved
                        if s == near_of(not after, sections):
                            fast[pl.ds(c * rows + rb * ROWS, ROWS), :] = moved
                        if s == second_of(not after, sections):
                            fast[pl.ds((2 + c) * rows + rb * ROWS, ROWS), :] = moved
                    total[s, c, at, :] = v

    by_side(body)


def far_kernel(
    u, total_in, new_u_in, arrived, half, index, splat, total, new_u, near, rim_a, rim_b
):
    sections, _, rows, width = u.shape

    def body(after):
        own, _, hops = pairs_of(after, sections)[2]
        stiff = wide_splat(splat, SLOW + hops - 1, width)
        moving = wide_splat(splat, MOVING + own, width)
        for rb in range(rows // ROWS):
            at = rows_of(rb)
            f = side_flow(u, own, arrived, 0, index, 2, stiff, rb)
            for c in range(2):
                v = (total[own, c, at, :] + f[c]) * moving
                moved = u[own, c, at, :] + STEP * v
                total[own, c, at, :] = v
                new_u[own, c, at, :] = moved
                near[pl.ds(c * rows + rb * ROWS, ROWS), :] = moved

    by_side(body)
    put_rims(new_u, rim_a, rim_b, lambda s: half[s, 1, rows - 1 : rows, :])


def last_far_kernel(u, total_in, arrived, index, splat, total, out_u, out_w, new_u, new_w, sem):
    sections, _, rows, width = u.shape

    def body(after):
        pairs = pairs_of(after, sections)
        done = [s for s in range(sections) if s not in (pairs[0][0], pairs[1][0])]
        copies = []
        for k, s in enumerate(done):
            moving = splat[MOVING + s][0:1, 0:1]
            for c in range(2):
                v = total[s, c] * moving
                new_w[k, c] = v
                new_u[k, c] = u[s, c] + STEP * v
            copies += [
                pltpu.make_async_copy(new_u.at[k], out_u.at[s], sem.at[2 * k]),
                pltpu.make_async_copy(new_w.at[k], out_w.at[s], sem.at[2 * k + 1]),
            ]
        for copy in copies:
            copy.start()
        own, _, hops = pairs[2]
        stiff = wide_splat(splat, SLOW + hops - 1, width)
        for rb in range(rows // ROWS):
            f = side_flow(u, own, arrived, 0, index, 2, stiff, rb)
            for c in range(2):
                total[own, c, rows_of(rb), :] += f[c]
        for copy in copies:
            copy.wait()

    by_side(body)


def last_near_kernel(
    u, total, arrived, index, splat, out_u_in, out_w_in, out_u, out_w, new_u, new_w, sem
):
    sections, _, rows, width = u.shape

    def body(after):
        copies = []
        for j in range(2):
            own, _, hops = pairs_of(after, sections)[j]
            stiff = wide_splat(splat, SLOW + hops - 1, width)
            moving = wide_splat(splat, MOVING + own, width)
            for rb in range(rows // ROWS):
                at = rows_of(rb)
                f = side_flow(u, own, arrived, 0, index, j, stiff, rb)
                for c in range(2):
                    v = (total[own, c, at, :] + f[c]) * moving
                    new_w[j, c, at, :] = v
                    new_u[j, c, at, :] = u[own, c, at, :] + STEP * v
            for k, (source, target) in enumerate(((new_u, out_u), (new_w, out_w))):
                copy = pltpu.make_async_copy(source.at[j], target.at[own], sem.at[2 * j + k])
                copy.start()
                copies.append(copy)
        for copy in copies:
            copy.wait()

    by_side(body)


def call(kernel, outs, ins, alias=None, scratch=(), in_specs=None, out_specs=None):
    return pl.pallas_call(
        kernel,
        out_shape=outs,
        in_specs=in_specs or [VMEM] * len(ins),
        out_specs=out_specs or [VMEM] * len(outs),
        input_output_aliases=alias or {},
        scratch_shapes=scratch,
        compiler_params=pltpu.CompilerParams(vmem_limit_bytes=16 << 20),
    )(*ins)


def per_device(u, w, cls, shift, fixed, stiff, cross):
    sections, _, rows, width = u.shape
    rbs = rows // ROWS

    def array(*shape, dtype=jnp.float32):
        return jax.ShapeDtypeStruct(shape, dtype)

    full = array(*u.shape)
    one = array(2 * rows, width)
    two = array(4 * rows, width)
    tail = tail_rows(rows)
    rim = array(-(-3 * sections // ROWS) * ROWS, width)
    splat = array(MOVING + sections, ROWS, COLS)
    index = array(3, tail_rows(rows), width, dtype=jnp.int32)
    smem = pl.BlockSpec(memory_space=pltpu.SMEM)
    scalars = [pltpu.SMEM(shift.shape, jnp.int32), pltpu.SemaphoreType.DMA]

    (near,) = call(lead_kernel, [array(2 * rows + tail, width)], [u, shift])
    near = exchange(near, "sec", "b")
    second, fast, rim_a, rim_b, splat = call(
        prepare_kernel,
        [one, array(4 * rows + tail, width), rim, rim, splat],
        [u, cls, shift, stiff, cross, fixed],
        in_specs=[VMEM] * 3 + [smem] * 3,
    )
    fast = exchange(fast, "sec", "a")
    far = exchange(second, "sec", "b")
    rim_a = exchange(rim_a, "strip", "a")
    rim_b = exchange(rim_b, "strip", "b")
    total, half = call(
        first_inside_kernel, [full, full], [u, w, cls, shift, splat], scratch=scalars
    )
    total, fast_index = call(
        first_rims_kernel, [full, index], [u, total, half, fast, rim_a, rim_b, shift, splat], {1: 0}
    )
    total, new_u, second, fast, index = call(
        near_kernel, [full, full, one, two, index], [u, total, near, shift, splat], {1: 0}
    )
    second = exchange(second, "sec", "b")
    fast = exchange(fast, "sec", "a")
    w, u, near, rim_a, rim_b = call(
        far_kernel,
        [full, full, one, rim, rim],
        [u, total, new_u, far, half, index, splat],
        {1: 0, 2: 1},
    )
    near = exchange(near, "sec", "b")
    rim_a = exchange(rim_a, "strip", "a")
    rim_b = exchange(rim_b, "strip", "b")
    (total,) = call(later_inside_kernel, [full], [u, w, half, shift, splat], scratch=scalars)
    (total,) = call(
        later_rims_kernel, [full], [u, total, half, fast, rim_a, rim_b, fast_index, splat], {1: 0}
    )
    done = max(sections - 2, 1)
    total, out_u, out_w = call(
        last_far_kernel,
        [full, full, full],
        [u, total, second, index, splat],
        {1: 0},
        scratch=[pltpu.VMEM((done, 2, rows, width), jnp.float32)] * 2
        + [pltpu.SemaphoreType.DMA((2 * done,))],
        out_specs=[VMEM, ANY, ANY],
    )
    return tuple(
        call(
            last_near_kernel,
            [full, full],
            [u, total, near, index, splat, out_u, out_w],
            {5: 0, 6: 1},
            scratch=[pltpu.VMEM((2, 2, rows, width), jnp.float32)] * 2
            + [pltpu.SemaphoreType.DMA((4,))],
            in_specs=[VMEM] * 5 + [ANY] * 2,
            out_specs=[ANY] * 2,
        )
    )


def solution(mesh):
    block = P("sec", None, "strip", None)
    return jax.shard_map(
        per_device,
        mesh=mesh,
        in_specs=(block, block, block, block, P("sec"), P(), P()),
        out_specs=(block, block),
        check_vma=False,
    )
```

profile of v0, /device:TPU:3, one launch (start us, length us, event | category | flops | bytes accessed | tf_op | source)
XLA Modules:
  0.0 45.6 jit_solution(3056749106788186224)
XLA Ops:
  0.6 0.0 copy-start
  0.6 1.4 %copy-done = f32[3,2,64,1024]{3,2,1,0:T(8,128)S(1)} copy-done((f32[3,2,64,1024]{3,2,1,0:T(8,128)S(1)}, f32[3,2,64,1024]{3,2,1,0:T(8,128)}, u32[]{:S(2)}) %copy-start) | copy-done | bytes 1572888
  2.0 0.0 copy-start.1
  2.0 1.4 %copy-done.1 = s32[3,2,64,1024]{3,2,1,0:T(8,128)S(1)} copy-done((s32[3,2,64,1024]{3,2,1,0:T(8,128)S(1)}, s32[3,2,64,1024]{3,2,1,0:T(8,128)}, u32[]{:S(2)}) %copy-start.1) | copy-done | bytes 1572888
  3.4 0.0 copy-start.4
  3.5 0.7 %copy-done.4 = s32[3,2,8,8]{3,2,1,0:T(8,128)S(1)} copy-done((s32[3,2,8,8]{3,2,1,0:T(8,128)S(1)}, s32[3,2,8,8]{3,2,1,0:T(8,128)}, u32[]{:S(2)}) %copy-start.4) | copy-done | bytes 1560
  4.2 0.0 copy-start.5
  4.2 0.7 %copy-done.5 = f32[8]{0:T(128)S(1)} copy-done((f32[8]{0:T(128)S(1)}, f32[8]{0:T(128)}, u32[]{:S(2)}) %copy-start.5) | copy-done | bytes 56
  4.8 0.0 copy-start.6
  4.8 0.7 %copy-done.6 = f32[2]{0:T(128)S(1)} copy-done((f32[2]{0:T(128)S(1)}, f32[2]{0:T(128)}, u32[]{:S(2)}) %copy-start.6) | copy-done | bytes 32
  5.5 0.0 copy-start.7
  5.5 0.7 %copy-done.7 = s32[3]{0:T(128)S(1)} copy-done((s32[3]{0:T(128)S(1)}, s32[3]{0:T(128)}, u32[]{:S(2)}) %copy-start.7) | copy-done | bytes 36
  6.2 0.0 copy-start.3
  6.2 0.8 %shard_map.86 = (f32[128,1024]{1,0:T(8,128)S(1)}, f32[264,1024]{1,0:T(8,128)S(1)}, f32[16,1024]{1,0:T(8,128)S(1)}, f32[16,1024]{1,0:T(8,128)S(1)}, f32[10,8,128]{2,1,0:T(8,128)S(1)}) custom-call(f32[3,2,64,1024]{3,2,1,0:T(8,128)S(1)} %copy-done, s32[3,2,64,1024]{3,2,1,0:T(8,128)S(1)} %copy-done.1, s32[3,2,8,8]{3,2,1,0:T(8,128)S(1)} %copy-done.4, ...), custom_call_target="tpu_custom_call" | custom-call | tf_op jit(solution)/shard_map/pallas_call | solution.py:458
  7.0 0.0 copy-start.2
  7.0 0.7 %collective-permute-start = (f32[264,1024]{1,0:T(8,128)S(1)}, f32[264,1024]{1,0:T(8,128)S(1)}, u32[]{:S(2)}, u32[]{:S(2)}) collective-permute-start(f32[264,1024]{1,0:T(8,128)S(1)} %get-tuple-element.27), channel_id=1, source_target_pairs={{0,8},{8,0},{16,24},{24,16},{1,9},{9,1},{17,25},{25,17},{2,10},{10... | collective-permute-start | bytes 3244040 | tf_op jit(solution)/shard_map/ppermute | solution.py:26
  7.8 0.1 shard_map.89
  7.9 3.2 %collective-permute-start.3 = (f32[136,1024]{1,0:T(8,128)S(1)}, f32[136,1024]{1,0:T(8,128)S(1)}, u32[]{:S(2)}, u32[]{:S(2)}) collective-permute-start(f32[136,1024]{1,0:T(8,128)S(1)} %shard_map.89), channel_id=1, source_target_pairs={{8,16},{16,8},{9,17},{17,9},{10,18},{18,10},{11,19},{19,11},{12,20... | collective-permute-start | bytes 1671176 | tf_op jit(solution)/shard_map/ppermute | solution.py:26
  11.1 0.3 collective-permute-start.1
  11.4 4.1 %collective-permute-start.2 = (f32[16,1024]{1,0:T(8,128)S(1)}, f32[16,1024]{1,0:T(8,128)S(1)}, u32[]{:S(2)}, u32[]{:S(2)}) collective-permute-start(f32[16,1024]{1,0:T(8,128)S(1)} %get-tuple-element.29), channel_id=1, source_target_pairs={{1,2},{2,1},{3,4},{4,3},{5,6},{6,5},{9,10},{10,9},{11,12},{12,11},... | collective-permute-start | bytes 196616 | tf_op jit(solution)/shard_map/ppermute | solution.py:26
  15.5 2.9 %collective-permute-start.4 = (f32[128,1024]{1,0:T(8,128)S(1)}, f32[128,1024]{1,0:T(8,128)S(1)}, u32[]{:S(2)}, u32[]{:S(2)}) collective-permute-start(f32[128,1024]{1,0:T(8,128)S(1)} %get-tuple-element.33), channel_id=1, source_target_pairs={{8,16},{16,8},{9,17},{17,9},{10,18},{18,10},{11,19},{19,11},{12,20... | collective-permute-start | bytes 1572872 | tf_op jit(solution)/shard_map/ppermute | solution.py:26
  18.5 0.0 copy-done.3
  18.5 0.0 copy-done.2
  18.5 5.6 %shard_map.87 = (f32[3,2,64,1024]{3,2,1,0:T(8,128)S(1)}, f32[3,2,64,1024]{3,2,1,0:T(8,128)S(1)}) custom-call(f32[3,2,64,1024]{3,2,1,0:T(8,128)S(1)} %copy-done, f32[3,2,64,1024]{3,2,1,0:T(8,128)S(1)} %copy-done.3, s32[3,2,64,1024]{3,2,1,0:T(8,128)S(1)} %copy-done.2, s32[3,2,8,8]{3,2,1,0:T(8,128)S(1)} %copy-done.4, f32[10,8,128]{2,1,0:T(8,128)S(1)} %get-tuple-element.24.splat), custom_call_target="tpu_custom_call" | custom-call | tf_op jit(solution)/shard_map/pallas_call | solution.py:458
  24.1 0.0 collective-permute-done.1.rim_a
  24.1 0.0 collective-permute-done.2.rim_b
  24.1 0.0 collective-permute-done.fast
  24.1 1.3 %shard_map.88 = (f32[3,2,64,1024]{3,2,1,0:T(8,128)S(1)}, s32[3,8,1024]{2,1,0:T(8,128)S(1)}) custom-call(f32[3,2,64,1024]{3,2,1,0:T(8,128)S(1)} %copy-done, f32[3,2,64,1024]{3,2,1,0:T(8,128)S(1)} %get-tuple-element.25.total_in, f32[3,2,64,1024]{3,2,1,0:T(8,128)S(1)} %get-tuple-element.26.half, ...), custom_call_target="tpu_custom_call", output_to_operand_aliasing={{0}: (1, {})} | custom-call | tf_op jit(solution)/shard_map/pallas_call | solution.py:458
  25.5 0.0 collective-permute-done.3.arrived
  25.5 1.0 %shard_map.90 = (f32[3,2,64,1024]{3,2,1,0:T(8,128)S(1)}, f32[3,2,64,1024]{3,2,1,0:T(8,128)S(1)}, f32[128,1024]{1,0:T(8,128)S(1)}, f32[256,1024]{1,0:T(8,128)S(1)}, s32[3,8,1024]{2,1,0:T(8,128)S(1)}) custom-call(f32[3,2,64,1024]{3,2,1,0:T(8,128)S(1)} %copy-done, f32[3,2,64,1024]{3,2,1,0:T(8,128)S(1)} %get-tuple-element.30.total_in, ...), custom_call_target="tpu_custom_call", output_to_operand_aliasing={{0}: (1, {})} | custom-call | tf_op jit(solution)/shard_map/pallas_call | solution.py:458
  26.5 0.1 collective-permute-start.5
  26.6 2.6 %collective-permute-start.8 = (f32[128,1024]{1,0:T(8,128)S(1)}, f32[128,1024]{1,0:T(8,128)S(1)}, u32[]{:S(2)}, u32[]{:S(2)}) collective-permute-start(f32[128,1024]{1,0:T(8,128)S(1)} %get-tuple-element.41), channel_id=1, source_target_pairs={{8,16},{16,8},{9,17},{17,9},{10,18},{18,10},{11,19},{19,11},{12,20... | collective-permute-start | bytes 1572872 | tf_op jit(solution)/shard_map/ppermute | solution.py:26
  29.2 0.0 collective-permute-done.4.arrived
  29.2 0.5 %shard_map.91 = (f32[3,2,64,1024]{3,2,1,0:T(8,128)S(1)}, f32[3,2,64,1024]{3,2,1,0:T(8,128)S(1)}, f32[128,1024]{1,0:T(8,128)S(1)}, f32[16,1024]{1,0:T(8,128)S(1)}, f32[16,1024]{1,0:T(8,128)S(1)}) custom-call(f32[3,2,64,1024]{3,2,1,0:T(8,128)S(1)} %copy-done, ...), custom_call_target="tpu_custom_call", output_to_operand_aliasing={{0}: (1, {}), {1}: (2, {})} | custom-call | tf_op jit(solution)/shard_map/pallas_call | solution.py:458
  29.7 2.9 %collective-permute-start.9 = (f32[128,1024]{1,0:T(8,128)S(1)}, f32[128,1024]{1,0:T(8,128)S(1)}, u32[]{:S(2)}, u32[]{:S(2)}) collective-permute-start(f32[128,1024]{1,0:T(8,128)S(1)} %get-tuple-element.43), channel_id=1, source_target_pairs={{8,16},{16,8},{9,17},{17,9},{10,18},{18,10},{11,19},{19,11},{12,20... | collective-permute-start | bytes 1572872 | tf_op jit(solution)/shard_map/ppermute | solution.py:26
  32.7 0.1 collective-permute-start.6
  32.8 4.4 %collective-permute-start.7 = (f32[16,1024]{1,0:T(8,128)S(1)}, f32[16,1024]{1,0:T(8,128)S(1)}, u32[]{:S(2)}, u32[]{:S(2)}) collective-permute-start(f32[16,1024]{1,0:T(8,128)S(1)} %get-tuple-element.39), channel_id=1, source_target_pairs={{1,2},{2,1},{3,4},{4,3},{5,6},{6,5},{9,10},{10,9},{11,12},{12,11},... | collective-permute-start | bytes 196616 | tf_op jit(solution)/shard_map/ppermute | solution.py:26
  37.1 3.9 %shard_map.92.total_in = f32[3,2,64,1024]{3,2,1,0:T(8,128)S(1)} custom-call(f32[3,2,64,1024]{3,2,1,0:T(8,128)S(1)} %get-tuple-element.35.u, f32[3,2,64,1024]{3,2,1,0:T(8,128)S(1)} %get-tuple-element.36.w, f32[3,2,64,1024]{3,2,1,0:T(8,128)S(1)} %get-tuple-element.26.half, s32[3,2,8,8]{3,2,1,0:T(8,128)S(1)} %copy-done.4, f32[10,8,128]{2,1,0:T(8,128)S(1)} %get-tuple-element.24.splat), custom_call_target="tpu_custom_call" | custom-call | tf_op jit(solution)/shard_map/pallas_call | solution.py:458
  41.0 0.0 collective-permute-done.6.rim_a
  41.0 0.0 collective-permute-done.7.rim_b
  41.0 0.0 collective-permute-done.5.fast
  41.0 1.2 %shard_map.93.total_in = f32[3,2,64,1024]{3,2,1,0:T(8,128)S(1)} custom-call(f32[3,2,64,1024]{3,2,1,0:T(8,128)S(1)} %get-tuple-element.35.u, f32[3,2,64,1024]{3,2,1,0:T(8,128)S(1)} %shard_map.92.total_in, f32[3,2,64,1024]{3,2,1,0:T(8,128)S(1)} %get-tuple-element.26.half, f32[256,1024]{1,0:T(8,128)S(1)} %collective-permute-done.5.fast, ...), custom_call_target="tpu_custom_call", output_to_operand_aliasing={{}: (1, {})} | custom-call | tf_op jit(solution)/shard_map/pallas_call | solution.py:458
  42.3 0.0 collective-permute-done.8.arrived
  42.3 1.5 %shard_map.94 = (f32[3,2,64,1024]{3,2,1,0:T(8,128)S(1)}, f32[3,2,64,1024]{3,2,1,0:T(8,128)}, f32[3,2,64,1024]{3,2,1,0:T(8,128)}) custom-call(f32[3,2,64,1024]{3,2,1,0:T(8,128)S(1)} %get-tuple-element.35.u, f32[3,2,64,1024]{3,2,1,0:T(8,128)S(1)} %shard_map.93.total_in, ...), custom_call_target="tpu_custom_call", output_to_operand_aliasing={{0}: (1, {})} | custom-call | tf_op jit(solution)/shard_map/pallas_call | solution.py:458
  43.8 0.0 collective-permute-done.9.arrived
  43.8 1.8 %shard_map.95 = (f32[3,2,64,1024]{3,2,1,0:T(8,128)}, f32[3,2,64,1024]{3,2,1,0:T(8,128)}) custom-call(f32[3,2,64,1024]{3,2,1,0:T(8,128)S(1)} %get-tuple-element.35.u, f32[3,2,64,1024]{3,2,1,0:T(8,128)S(1)} %get-tuple-element.42.total, f32[128,1024]{1,0:T(8,128)S(1)} %collective-permute-done.9.arrived, ...), custom_call_target="tpu_custom_call", output_to_operand_aliasing={{0}: (5, {}), {1}: (6, {})} | custom-call | tf_op jit(solution)/shard_map/pallas_call | solution.py:458
Async XLA Ops:
  0.6 1.4 %copy-start = (f32[3,2,64,1024]{3,2,1,0:T(8,128)S(1)}, f32[3,2,64,1024]{3,2,1,0:T(8,128)}, u32[]{:S(2)}) copy-start(f32[3,2,64,1024]{3,2,1,0:T(8,128)} %u.11) | copy-start | bytes 4718596
  2.0 1.4 %copy-start.1 = (s32[3,2,64,1024]{3,2,1,0:T(8,128)S(1)}, s32[3,2,64,1024]{3,2,1,0:T(8,128)}, u32[]{:S(2)}) copy-start(s32[3,2,64,1024]{3,2,1,0:T(8,128)} %cls.3) | copy-start | bytes 4718596
  3.4 0.7 %copy-start.4 = (s32[3,2,8,8]{3,2,1,0:T(8,128)S(1)}, s32[3,2,8,8]{3,2,1,0:T(8,128)}, u32[]{:S(2)}) copy-start(s32[3,2,8,8]{3,2,1,0:T(8,128)} %shift.11) | copy-start | bytes 4612
  4.2 0.7 %copy-start.5 = (f32[8]{0:T(128)S(1)}, f32[8]{0:T(128)}, u32[]{:S(2)}) copy-start(f32[8]{0:T(128)} %stiff.1) | copy-start | bytes 100
  4.8 0.7 %copy-start.6 = (f32[2]{0:T(128)S(1)}, f32[2]{0:T(128)}, u32[]{:S(2)}) copy-start(f32[2]{0:T(128)} %cross.1) | copy-start | bytes 28
  5.5 0.7 %copy-start.7 = (s32[3]{0:T(128)S(1)}, s32[3]{0:T(128)}, u32[]{:S(2)}) copy-start(s32[3]{0:T(128)} %fixed.1) | copy-start | bytes 40
  6.2 12.3 %copy-start.3 = (f32[3,2,64,1024]{3,2,1,0:T(8,128)S(1)}, f32[3,2,64,1024]{3,2,1,0:T(8,128)}, u32[]{:S(2)}) copy-start(f32[3,2,64,1024]{3,2,1,0:T(8,128)} %w.1) | copy-start | bytes 4718596
  7.0 11.5 %copy-start.2 = (s32[3,2,64,1024]{3,2,1,0:T(8,128)S(1)}, s32[3,2,64,1024]{3,2,1,0:T(8,128)}, u32[]{:S(2)}) copy-start(s32[3,2,64,1024]{3,2,1,0:T(8,128)} %cls.3) | copy-start | bytes 4718596
  7.0 17.1 %collective-permute-start = (f32[264,1024]{1,0:T(8,128)S(1)}, f32[264,1024]{1,0:T(8,128)S(1)}, u32[]{:S(2)}, u32[]{:S(2)}) collective-permute-start(f32[264,1024]{1,0:T(8,128)S(1)} %get-tuple-element.27), channel_id=1, source_target_pairs={{0,8},{8,0},{16,24},{24,16},{1,9},{9,1},{17,25},{25,17},{2,10},{10... | collective-permute-start | bytes 3244040 | tf_op jit(solution)/shard_map/ppermute | solution.py:26
  7.9 17.6 %collective-permute-start.3 = (f32[136,1024]{1,0:T(8,128)S(1)}, f32[136,1024]{1,0:T(8,128)S(1)}, u32[]{:S(2)}, u32[]{:S(2)}) collective-permute-start(f32[136,1024]{1,0:T(8,128)S(1)} %shard_map.89), channel_id=1, source_target_pairs={{8,16},{16,8},{9,17},{17,9},{10,18},{18,10},{11,19},{19,11},{12,20... | collective-permute-start | bytes 1671176 | tf_op jit(solution)/shard_map/ppermute | solution.py:26
  11.1 13.0 %collective-permute-start.1 = (f32[16,1024]{1,0:T(8,128)S(1)}, f32[16,1024]{1,0:T(8,128)S(1)}, u32[]{:S(2)}, u32[]{:S(2)}) collective-permute-start(f32[16,1024]{1,0:T(8,128)S(1)} %get-tuple-element.28), channel_id=1, source_target_pairs={{0,1},{1,0},{2,3},{3,2},{4,5},{5,4},{6,7},{7,6},{8,9},{9,8},{10,11... | collective-permute-start | bytes 196616 | tf_op jit(solution)/shard_map/ppermute | solution.py:26
  11.4 12.7 %collective-permute-start.2 = (f32[16,1024]{1,0:T(8,128)S(1)}, f32[16,1024]{1,0:T(8,128)S(1)}, u32[]{:S(2)}, u32[]{:S(2)}) collective-permute-start(f32[16,1024]{1,0:T(8,128)S(1)} %get-tuple-element.29), channel_id=1, source_target_pairs={{1,2},{2,1},{3,4},{4,3},{5,6},{6,5},{9,10},{10,9},{11,12},{12,11},... | collective-permute-start | bytes 196616 | tf_op jit(solution)/shard_map/ppermute | solution.py:26
  15.5 13.7 %collective-permute-start.4 = (f32[128,1024]{1,0:T(8,128)S(1)}, f32[128,1024]{1,0:T(8,128)S(1)}, u32[]{:S(2)}, u32[]{:S(2)}) collective-permute-start(f32[128,1024]{1,0:T(8,128)S(1)} %get-tuple-element.33), channel_id=1, source_target_pairs={{8,16},{16,8},{9,17},{17,9},{10,18},{18,10},{11,19},{19,11},{12,20... | collective-permute-start | bytes 1572872 | tf_op jit(solution)/shard_map/ppermute | solution.py:26
  26.5 14.5 %collective-permute-start.5 = (f32[256,1024]{1,0:T(8,128)S(1)}, f32[256,1024]{1,0:T(8,128)S(1)}, u32[]{:S(2)}, u32[]{:S(2)}) collective-permute-start(f32[256,1024]{1,0:T(8,128)S(1)} %get-tuple-element.37), channel_id=1, source_target_pairs={{0,8},{8,0},{16,24},{24,16},{1,9},{9,1},{17,25},{25,17},{2,10},{10... | collective-permute-start | bytes 3145736 | tf_op jit(solution)/shard_map/ppermute | solution.py:26
  26.6 15.7 %collective-permute-start.8 = (f32[128,1024]{1,0:T(8,128)S(1)}, f32[128,1024]{1,0:T(8,128)S(1)}, u32[]{:S(2)}, u32[]{:S(2)}) collective-permute-start(f32[128,1024]{1,0:T(8,128)S(1)} %get-tuple-element.41), channel_id=1, source_target_pairs={{8,16},{16,8},{9,17},{17,9},{10,18},{18,10},{11,19},{19,11},{12,20... | collective-permute-start | bytes 1572872 | tf_op jit(solution)/shard_map/ppermute | solution.py:26
  29.7 14.0 %collective-permute-start.9 = (f32[128,1024]{1,0:T(8,128)S(1)}, f32[128,1024]{1,0:T(8,128)S(1)}, u32[]{:S(2)}, u32[]{:S(2)}) collective-permute-start(f32[128,1024]{1,0:T(8,128)S(1)} %get-tuple-element.43), channel_id=1, source_target_pairs={{8,16},{16,8},{9,17},{17,9},{10,18},{18,10},{11,19},{19,11},{12,20... | collective-permute-start | bytes 1572872 | tf_op jit(solution)/shard_map/ppermute | solution.py:26
  32.7 8.3 %collective-permute-start.6 = (f32[16,1024]{1,0:T(8,128)S(1)}, f32[16,1024]{1,0:T(8,128)S(1)}, u32[]{:S(2)}, u32[]{:S(2)}) collective-permute-start(f32[16,1024]{1,0:T(8,128)S(1)} %get-tuple-element.38), channel_id=1, source_target_pairs={{0,1},{1,0},{2,3},{3,2},{4,5},{5,4},{6,7},{7,6},{8,9},{9,8},{10,11... | collective-permute-start | bytes 196616 | tf_op jit(solution)/shard_map/ppermute | solution.py:26
  32.8 8.3 %collective-permute-start.7 = (f32[16,1024]{1,0:T(8,128)S(1)}, f32[16,1024]{1,0:T(8,128)S(1)}, u32[]{:S(2)}, u32[]{:S(2)}) collective-permute-start(f32[16,1024]{1,0:T(8,128)S(1)} %get-tuple-element.39), channel_id=1, source_target_pairs={{1,2},{2,1},{3,4},{4,3},{5,6},{6,5},{9,10},{10,9},{11,12},{12,11},... | collective-permute-start | bytes 196616 | tf_op jit(solution)/shard_map/ppermute | solution.py:26
where the time goes:
time: 46 us; the launch traced here: 45.6 us
  starting transfers between devices  21.4 us (47%)
  Pallas kernels  17.8 us (39%)
  local copies, waits for them, and re-layouts  5.52 us (12%)
  between operations  0.87 us (2%)
    ppermute x10, starting transfers between devices, exchange(): return lax.ppermute(value, axis, route)  21.4 us
    pallas_call x10, Pallas kernels, call(): pl.pallas_call(kernel, out_shape=outs, in_specs=in_specs or [VMEM] * len(...  17.8 us
    unnamed x16, local copies, waits for them, and re-layouts  5.52 us
  transfers between devices with their start and end apart: 10, of which 0 were waited for; matrix products, arithmetic and copies ran while one was open for 0% of the time, Pallas kernels for 33%

commit v1 on v0

v1 whole, which is shorter than its diff:
```python
import jax
import jax.numpy as jnp
from jax import lax
from jax.experimental import pallas as pl
from jax.experimental.pallas import tpu as pltpu
from jax.sharding import PartitionSpec as P

ROWS = 8
COLS = 128
CLASSES = 8
DAMPING = 0.9
STEP = 0.35

VMEM = pl.BlockSpec(memory_space=pltpu.VMEM)
ANY = pl.BlockSpec(memory_space=pl.ANY)
LEAD_LIMIT = 64 << 20

INSIDE, SLOW, FAST, TABLE, MOVING = 0, 2, 4, 6, 7


def exchange(value, axis, pairing):
    n = lax.axis_size(axis)
    first = 0 if pairing == "a" else 1
    route = []
    for i in range(first, n - 1, 2):
        route += [(i, i + 1), (i + 1, i)]
    return lax.ppermute(value, axis, route)


def slow_after():
    return lax.rem(lax.axis_index("sec"), 2) == 1


def by_side(body):
    after = slow_after()

    @pl.when(after)
    def _():
        body(True)

    @pl.when(jnp.logical_not(after))
    def _():
        body(False)


def near_of(after, sections):
    return sections - 1 if after else 0


def second_of(after, sections):
    return sections - 2 if after else 1


def pairs_of(after, sections):
    near, second = near_of(after, sections), second_of(after, sections)
    return ((near, 0, 1), (second, 0, 2), (near, 1, 2))


def inverse(value):
    guess = pl.reciprocal(value, approx=True)
    return guess * (2.0 - value * guess)


def flow(ex, ey, half):
    gain = half * (3.0 - inverse(1.0 + ex * ex + ey * ey))
    return gain * ex, gain * ey


def cols_of(cb):
    return slice(cb * COLS, (cb + 1) * COLS)


def rows_of(rb):
    start = rb * ROWS
    return pl.ds(start if isinstance(start, int) else pl.multiple_of(start, ROWS), ROWS)


def tail_rows(rows):
    return -(-(rows // ROWS) // ROWS) * ROWS


def per_tile(width, make):
    return jnp.concatenate([make(cb) for cb in range(width // COLS)], axis=1)


def turned(wide, amounts):
    return per_tile(wide.shape[1], lambda cb: pltpu.roll(wide[:, cols_of(cb)], amounts[cb], 1))


def gathered(wide, index):
    def one(cb):
        full = jnp.broadcast_to(index[:, cols_of(cb)], (ROWS, COLS))
        return jnp.take_along_axis(wide[:, cols_of(cb)], full, axis=1, mode="promise_in_bounds")

    return per_tile(wide.shape[1], one)


def spread(blocks, width):
    return per_tile(width, lambda cb: jnp.broadcast_to(blocks[:, cb : cb + 1], (blocks.shape[0], COLS)))


def lanes(rows, width):
    return lax.broadcasted_iota(jnp.int32, (rows, width), 1) & (COLS - 1)


def put_tail(shift, out, first, width):
    sections, _, rbs, _ = shift.shape
    lane = lanes(rbs, width)
    parts = [
        spread(shift[s, h], width)
        for s, h in ((sections - 1, 0), (sections - 1, 1), (sections - 2, 1))
    ]
    mixed = jnp.where(lane == 0, parts[0], jnp.where(lane == 1, parts[1], parts[2]))
    out[first : first + rbs, :] = mixed.astype(jnp.float32)


def put_index(after, shift, arrived, first, index):
    sections, _, rbs, _ = shift.shape
    width = index.shape[2]
    lane = lanes(rbs, width)
    for j, (own, _, hops) in enumerate(pairs_of(after, sections)):
        if after:
            offset = spread(shift[own, hops - 1], width)
        else:
            blocks = per_tile(
                width,
                lambda cb: jnp.broadcast_to(
                    arrived[first : first + rbs, cb * COLS + j : cb * COLS + j + 1], (rbs, COLS)
                ),
            )
            offset = -blocks.astype(jnp.int32)
        index[j, 0:rbs, :] = (lane + offset) & (COLS - 1)


def put_rims(first_of, last_of, kv_of, rim_a, rim_b, sections):
    odd = lax.rem(lax.axis_index("strip"), 2) == 1

    def put(line, first, last):
        rim_a[line : line + 1, :] = jnp.where(odd, first, last)
        rim_b[line : line + 1, :] = jnp.where(odd, last, first)

    for s in range(sections):
        for c in range(2):
            put(2 * s + c, first_of(s, c), last_of(s, c))
        stiff = kv_of(s)
        put(2 * sections + s, stiff, stiff)


def look_up(table, index):
    def one(cb):
        tile = jnp.broadcast_to(index[:, cols_of(cb)], (ROWS, COLS))
        return jnp.take_along_axis(table, tile, axis=1, mode="promise_in_bounds")[: index.shape[0]]

    return per_tile(index.shape[1], one)


def put_splat(stiff, cross, fixed, splat):
    sections = fixed.shape[0]
    i, n = lax.axis_index("sec"), lax.axis_size("sec")
    odd = slow_after()
    tile = (ROWS, COLS)
    lane = lax.broadcasted_iota(jnp.int32, tile, 1)
    slow_there = jnp.where(odd, i < n - 1, i > 0)
    fast_there = jnp.where(odd, i > 0, i < n - 1)
    for h in range(2):
        k = jnp.full(tile, cross[h] * (0.5 * STEP))
        splat[INSIDE + h] = k
        splat[SLOW + h] = jnp.where(slow_there, k, 0.0)
        splat[FAST + h] = jnp.where(fast_there, k, 0.0)
    table = jnp.zeros(tile, jnp.float32)
    for k in range(CLASSES):
        table = jnp.where(lane == k, stiff[k] * (0.5 * STEP), table)
    splat[TABLE] = table
    for s in range(sections):
        splat[MOVING + s] = jnp.full(tile, jnp.where(fixed[s] == 0, 1.0, 0.0))


def lead_kernel(
    u, cls, shift, stiff, cross, fixed, slow, fast, rim_a, rim_b, splat,
    shift_here, stiff_here, cross_here, fixed_here, first_here, last_here, cls_here,
    tail_here, rim_a_here, rim_b_here, splat_here, sem,
):
    sections, _, rows, width = u.shape

    def copies(first, pairs):
        return [
            pltpu.make_async_copy(source, target, sem.at[first + k])
            for k, (source, target) in enumerate(pairs)
        ]

    def blocks(after):
        pairs = []
        for out, side in ((slow, after), (fast, not after)):
            for k, own in enumerate((near_of(side, sections), second_of(side, sections))):
                for c in range(2):
                    pairs.append((u.at[own, c], out.at[pl.ds((2 * k + c) * rows, rows)]))
        return copies(0, pairs)

    bottom = pl.ds(rows - ROWS, ROWS)
    small = copies(
        8,
        (
            (shift, shift_here),
            (stiff, stiff_here),
            (cross, cross_here),
            (fixed, fixed_here),
            (u.at[:, :, pl.ds(0, ROWS)], first_here),
            (u.at[:, :, bottom], last_here),
            (cls.at[:, 1, bottom], cls_here),
        ),
    )
    for copy in small:
        copy.start()
    by_side(lambda after: [copy.start() for copy in blocks(after)])
    for copy in small:
        copy.wait()
    put_tail(shift_here, tail_here, 0, width)
    put_splat(stiff_here, cross_here, fixed_here, splat_here)
    table = splat_here[TABLE]
    put_rims(
        lambda s, c: first_here[s, c, 0:1, :],
        lambda s, c: last_here[s, c, ROWS - 1 : ROWS, :],
        lambda s: look_up(table, cls_here[s, ROWS - 1 : ROWS, :]),
        rim_a_here,
        rim_b_here,
        sections,
    )
    after_blocks = pl.ds(4 * rows, tail_here.shape[0])
    results = copies(
        15,
        (
            (tail_here, slow.at[after_blocks]),
            (tail_here, fast.at[after_blocks]),
            (rim_a_here, rim_a),
            (rim_b_here, rim_b),
            (splat_here, splat),
        ),
    )
    for copy in results:
        copy.start()
    by_side(lambda after: [copy.wait() for copy in blocks(after)])
    for copy in results:
        copy.wait()


def hand_on_kernel(*refs):
    pass


def wide_splat(splat, k, width):
    tile = splat[k]
    return per_tile(width, lambda cb: tile)


def chosen(values, index):
    for bit in range(3):
        on = (index & (1 << bit)) != 0
        values = [jnp.where(on, values[k + 1], values[k]) for k in range(0, len(values), 2)]
    return values[0]


def inside(u, w, total, half_across, half_below, shift, splat, scalars, sem):
    sections, _, rows, width = u.shape
    rbs, cbs = rows // ROWS, width // COLS
    load = pltpu.make_async_copy(shift, scalars, sem)
    load.start()
    bottom = lax.broadcasted_iota(jnp.int32, (rows, COLS), 0) == rows - 1

    def below(cb, carry):
        at = pl.ds(pl.multiple_of(cb * COLS, COLS), COLS)
        for s in range(sections):
            x, y = u[s, 0, :, at], u[s, 1, :, at]
            half = jnp.where(bottom, 0.0, half_below(s, at))
            f = flow(pltpu.roll(x, rows - 1, 0) - x, pltpu.roll(y, rows - 1, 0) - y, half)
            new = [f[c] - pltpu.roll(f[c], 1, 0) for c in range(2)]
            if w is not None:
                new = [DAMPING * w[s, c, :, at] + new[c] for c in range(2)]
            for c in range(2):
                total[s, c, :, at] = new[c]
        return carry

    lax.fori_loop(0, cbs, below, 0)
    load.wait()
    last = lax.broadcasted_iota(jnp.int32, (ROWS, width), 1) == width - 1

    def row(rb, carry):
        at = rows_of(rb)
        add = [[total[s, c, at, :] for c in range(2)] for s in range(sections)]
        for s in range(sections):
            x, y = u[s, 0, at, :], u[s, 1, at, :]
            half = jnp.where(last, 0.0, half_across(s, at))
            f = flow(pltpu.roll(x, width - 1, 1) - x, pltpu.roll(y, width - 1, 1) - y, half)
            for c in range(2):
                add[s][c] = add[s][c] + (f[c] - pltpu.roll(f[c], 1, 1))
        for hops in (1, 2):
            half = wide_splat(splat, INSIDE + hops - 1, width)
            for s in range(sections - hops):
                offsets = [scalars[s, hops - 1, rb, cb] for cb in range(cbs)]
                there = [(-o) & (COLS - 1) for o in offsets]
                back = [o & (COLS - 1) for o in offsets]
                e = [turned(u[s + hops, c, at, :], there) - u[s, c, at, :] for c in range(2)]
                f = flow(e[0], e[1], half)
                for c in range(2):
                    add[s][c] = add[s][c] + f[c]
                    add[s + hops][c] = add[s + hops][c] - turned(f[c], back)
        for s in range(sections):
            for c in range(2):
                total[s, c, at, :] = add[s][c]
        return carry

    lax.fori_loop(0, rbs, row, 0)


def first_inside_kernel(u, cls, shift, splat, total, half, scalars, sem):
    table = splat[TABLE]
    values = [jnp.broadcast_to(table[:, k : k + 1], (ROWS, COLS)) for k in range(CLASSES)]
    rows = u.shape[2]

    def half_across(s, at):
        index = cls[s, 0, at, :]
        k = per_tile(index.shape[1], lambda cb: chosen(values, index[:, cols_of(cb)]))
        half[s, 0, at, :] = k
        return k

    def half_below(s, at):
        index = cls[s, 1, :, at]
        k = jnp.concatenate(
            [look_up(table, index[r : r + ROWS]) for r in range(0, rows, ROWS)], axis=0
        )
        half[s, 1, :, at] = k
        return k

    inside(u, None, total, half_across, half_below, shift, splat, scalars, sem)


def later_inside_kernel(u, w, half, shift, splat, total, scalars, sem):
    def half_across(s, at):
        return half[s, 0, at, :]

    def half_below(s, at):
        return half[s, 1, :, at]

    inside(u, w, total, half_across, half_below, shift, splat, scalars, sem)


def side_flow(u, own, arrived, first, index, j, half, rb):
    rows = u.shape[2]
    at = rows_of(rb)
    number = index[j, rb : rb + 1, :]
    e = [
        gathered(arrived[pl.ds(first + c * rows + rb * ROWS, ROWS), :], number) - u[own, c, at, :]
        for c in range(2)
    ]
    return flow(e[0], e[1], half)


def rim_flows(u, half, rim_a, rim_b, total, sections):
    rows = u.shape[2]
    strip = lax.axis_index("strip")
    odd = lax.rem(strip, 2) == 1
    has_below = strip < lax.axis_size("strip") - 1

    def below(r):
        return jnp.where(odd, rim_b[r : r + 1, :], rim_a[r : r + 1, :])

    def above(r):
        return jnp.where(odd, rim_a[r : r + 1, :], rim_b[r : r + 1, :])

    count = u.shape[0]
    last, top = slice(rows - 1, rows), slice(0, 1)
    for s in sections:
        stiff = jnp.where(has_below, half[s, 1, last, :], 0.0)
        f = flow(*[below(2 * s + c) - u[s, c, last, :] for c in range(2)], stiff)
        stiff = jnp.where(strip > 0, above(2 * count + s), 0.0)
        g = flow(*[u[s, c, top, :] - above(2 * s + c) for c in range(2)], stiff)
        for c in range(2):
            total[s, c, last, :] += f[c]
            total[s, c, top, :] -= g[c]


def fast_flows(u, after, fast, index, splat, total, which):
    sections, _, rows, width = u.shape
    for j in which:
        own, block, hops = pairs_of(after, sections)[j]
        stiff = wide_splat(splat, FAST + hops - 1, width)
        for rb in range(rows // ROWS):
            f = side_flow(u, own, fast, 2 * block * rows, index, j, stiff, rb)
            for c in range(2):
                total[own, c, rows_of(rb), :] += f[c]


def first_rims_kernel(u, w, total_in, half, fast, rim_a, rim_b, shift, splat, total, index):
    sections, _, rows, _ = u.shape

    def damp(rb, carry):
        at = rows_of(rb)
        new = [total[s, c, at, :] + DAMPING * w[s, c, at, :] for s in range(sections) for c in range(2)]
        for k, value in enumerate(new):
            total[k // 2, k % 2, at, :] = value
        return carry

    lax.fori_loop(0, rows // ROWS, damp, 0)

    def body(after):
        put_index(not after, shift, fast, 4 * rows, index)
        fast_flows(u, not after, fast, index, splat, total, range(3))

    by_side(body)
    rim_flows(u, half, rim_a, rim_b, total, range(sections))


def later_rims_kernel(
    u, total_in, half, fast, rim_a, rim_b, index, splat, total, out_u, out_w, new_u, new_w, sem
):
    sections, _, rows, width = u.shape

    def body(after):
        near = (near_of(after, sections), second_of(after, sections))
        done = [s for s in range(sections) if s not in near]
        fast_flows(u, not after, fast, index, splat, total, (0, 2))
        rim_flows(u, half, rim_a, rim_b, total, done)
        copies = []
        for k, s in enumerate(done):
            moving = wide_splat(splat, MOVING + s, width)
            for rb in range(rows // ROWS):
                at = rows_of(rb)
                for c in range(2):
                    v = total[s, c, at, :] * moving
                    new_w[k, c, at, :] = v
                    new_u[k, c, at, :] = u[s, c, at, :] + STEP * v
            copies += [
                pltpu.make_async_copy(new_u.at[k], out_u.at[s], sem.at[2 * k]),
                pltpu.make_async_copy(new_w.at[k], out_w.at[s], sem.at[2 * k + 1]),
            ]
        for copy in copies:
            copy.start()
        fast_flows(u, not after, fast, index, splat, total, (1,))
        rim_flows(u, half, rim_a, rim_b, total, near)
        for copy in copies:
            copy.wait()

    by_side(body)


def slow_values(u, after, arrived, index, splat, total, j, rb):
    sections, _, rows, width = u.shape
    own = pairs_of(after, sections)[j][0]
    value = [total[own, c, rows_of(rb), :] for c in range(2)]
    for p, (section, block, hops) in enumerate(pairs_of(after, sections)):
        if section == own:
            stiff = wide_splat(splat, SLOW + hops - 1, width)
            f = side_flow(u, own, arrived, 2 * block * rows, index, p, stiff, rb)
            value = [value[c] + f[c] for c in range(2)]
    return value


def step_kernel(
    u, total, arrived, half, shift, splat, new_u, new_w, slow, fast, index, rim_a, rim_b
):
    sections, _, rows, width = u.shape

    def body(after):
        put_index(after, shift, arrived, 4 * rows, index)
        slow_edge = (near_of(after, sections), second_of(after, sections))
        fast_edge = (near_of(not after, sections), second_of(not after, sections))
        for s in range(sections):
            moving = wide_splat(splat, MOVING + s, width)
            for rb in range(rows // ROWS):
                at = rows_of(rb)
                if s in slow_edge:
                    value = slow_values(u, after, arrived, index, splat, total, slow_edge.index(s), rb)
                else:
                    value = [total[s, c, at, :] for c in range(2)]
                for c in range(2):
                    v = value[c] * moving
                    moved = u[s, c, at, :] + STEP * v
                    new_w[s, c, at, :] = v
                    new_u[s, c, at, :] = moved
                    for edge, out in ((slow_edge, slow), (fast_edge, fast)):
                        if s in edge:
                            first = (2 * edge.index(s) + c) * rows
                            out[pl.ds(first + rb * ROWS, ROWS), :] = moved

    by_side(body)
    last = slice(rows - 1, rows)
    put_rims(
        lambda s, c: new_u[s, c, 0:1, :],
        lambda s, c: new_u[s, c, last, :],
        lambda s: half[s, 1, last, :],
        rim_a,
        rim_b,
        sections,
    )


def last_kernel(u, total, arrived, index, splat, out_u_in, out_w_in, out_u, out_w, new_u, new_w, sem):
    sections, _, rows, width = u.shape
    rbs = rows // ROWS
    part = rbs // 2 if rbs % 2 == 0 else rbs

    def body(after):
        copies = []
        for j in range(2):
            own = pairs_of(after, sections)[j][0]
            moving = wide_splat(splat, MOVING + own, width)
            for rb in range(rbs):
                at = rows_of(rb)
                value = slow_values(u, after, arrived, index, splat, total, j, rb)
                for c in range(2):
                    v = value[c] * moving
                    new_w[j, c, at, :] = v
                    new_u[j, c, at, :] = u[own, c, at, :] + STEP * v
                if (rb + 1) % part == 0:
                    block = pl.ds((rb + 1 - part) * ROWS, part * ROWS)
                    for source, target in ((new_u, out_u), (new_w, out_w)):
                        copy = pltpu.make_async_copy(
                            source.at[j, :, block], target.at[own, :, block], sem.at[len(copies)]
                        )
                        copy.start()
                        copies.append(copy)
        for copy in copies:
            copy.wait()

    by_side(body)


def call(kernel, outs, ins, alias=None, scratch=(), in_specs=None, out_specs=None, limit=16 << 20, cost=None):
    return pl.pallas_call(
        kernel,
        out_shape=outs,
        in_specs=in_specs or [VMEM] * len(ins),
        out_specs=out_specs or [VMEM] * len(outs),
        input_output_aliases=alias or {},
        scratch_shapes=scratch,
        cost_estimate=cost,
        compiler_params=pltpu.CompilerParams(vmem_limit_bytes=limit),
    )(*ins)


def per_device(u, w, cls, shift, fixed, stiff, cross):
    sections, _, rows, width = u.shape

    def array(*shape, dtype=jnp.float32):
        return jax.ShapeDtypeStruct(shape, dtype)

    full = array(*u.shape)
    tail = array(tail_rows(rows), width)
    two = array(4 * rows, width)
    two_tail = array(4 * rows + tail.shape[0], width)
    rim = array(-(-3 * sections // ROWS) * ROWS, width)
    splat = array(MOVING + sections, ROWS, COLS)
    index = array(3, tail.shape[0], width, dtype=jnp.int32)
    scalars = [pltpu.SMEM(shift.shape, jnp.int32), pltpu.SemaphoreType.DMA]

    ends = pltpu.VMEM((sections, 2, ROWS, width), jnp.float32)
    slow, fast, rim_a, rim_b, splat = call(
        lead_kernel,
        [two_tail, two_tail, rim, rim, splat],
        [u, cls, shift, stiff, cross, fixed],
        scratch=[
            pltpu.VMEM(shift.shape, jnp.int32),
            pltpu.SMEM(stiff.shape, jnp.float32),
            pltpu.SMEM(cross.shape, jnp.float32),
            pltpu.SMEM(fixed.shape, jnp.int32),
            ends,
            ends,
            pltpu.VMEM((sections, ROWS, width), jnp.int32),
            pltpu.VMEM(tail.shape, jnp.float32),
            pltpu.VMEM(rim.shape, jnp.float32),
            pltpu.VMEM(rim.shape, jnp.float32),
            pltpu.VMEM(splat.shape, jnp.float32),
            pltpu.SemaphoreType.DMA((20,)),
        ],
        in_specs=[ANY] * 6,
        out_specs=[ANY] * 5,
        limit=LEAD_LIMIT,
    )
    slow, fast, rim_a, rim_b = call(
        hand_on_kernel,
        [two_tail, two_tail, rim, rim],
        [slow, fast, rim_a, rim_b],
        {k: k for k in range(4)},
        in_specs=[ANY] * 4,
        out_specs=[ANY] * 4,
    )
    slow = exchange(slow, "sec", "b")
    fast = exchange(fast, "sec", "a")
    rim_a = exchange(rim_a, "strip", "a")
    rim_b = exchange(rim_b, "strip", "b")
    total, half = call(
        first_inside_kernel, [full, full], [u, cls, shift, splat], scratch=scalars
    )
    total, fast_index = call(
        first_rims_kernel,
        [full, index],
        [u, w, total, half, fast, rim_a, rim_b, shift, splat],
        {2: 0},
    )
    u, w, slow, fast, index, rim_a, rim_b = call(
        step_kernel,
        [full, full, two, two, index, rim, rim],
        [u, total, slow, half, shift, splat],
    )
    slow = exchange(slow, "sec", "b")
    fast = exchange(fast, "sec", "a")
    rim_a = exchange(rim_a, "strip", "a")
    rim_b = exchange(rim_b, "strip", "b")
    (total,) = call(later_inside_kernel, [full], [u, w, half, shift, splat], scratch=scalars)
    done = max(sections - 2, 1)
    total, out_u, out_w = call(
        later_rims_kernel,
        [full, full, full],
        [u, total, half, fast, rim_a, rim_b, fast_index, splat],
        {1: 0},
        scratch=[pltpu.VMEM((done, 2, rows, width), jnp.float32)] * 2
        + [pltpu.SemaphoreType.DMA((2 * done,))],
        out_specs=[VMEM, ANY, ANY],
    )
    return tuple(
        call(
            last_kernel,
            [full, full],
            [u, total, slow, index, splat, out_u, out_w],
            {5: 0, 6: 1},
            scratch=[pltpu.VMEM((2, 2, rows, width), jnp.float32)] * 2
            + [pltpu.SemaphoreType.DMA((8,))],
            in_specs=[VMEM] * 5 + [ANY] * 2,
            out_specs=[ANY] * 2,
        )
    )


def solution(mesh):
    block = P("sec", None, "strip", None)
    return jax.shard_map(
        per_device,
        mesh=mesh,
        in_specs=(block, block, block, block, P("sec"), P(), P()),
        out_specs=(block, block),
        check_vma=False,
    )
```

time: 46 us -> 106 us (2.30)
  Pallas kernels: 17.8 us -> 79.8 us
  starting transfers between devices: 21.4 us -> 16.9 us
  waiting for transfers between devices: 0.03 us -> 3.55 us
  local copies, waits for them, and re-layouts: 5.52 us -> 3.84 us
    pallas_call x10 -> x8, Pallas kernels: 17.8 us -> 79.8 us  [call(): pl.pallas_call(kernel, out_shape=outs, in_specs=in_specs or [VMEM] * len(...]
    ppermute x10 -> x8, starting transfers between devices: 21.4 us -> 16.9 us  [exchange(): return lax.ppermute(value, axis, route)]
    ppermute x10 -> x8, waiting for transfers between devices: 0.03 us -> 3.55 us  [exchange(): return lax.ppermute(value, axis, route)]
    unnamed x16 -> x18, local copies, waits for them, and re-layouts: 5.52 us -> 3.84 us
  transfers between devices with their start and end apart: 10 -> 8, of which waited for: 0 -> 2; matrix products, arithmetic and copies ran while one was open for 0% -> 0% of each run, Pallas kernels for 33% -> 11%
where the time goes in v1:
time: 106 us; the launch traced here: 105 us
  Pallas kernels  79.8 us (75%)
  starting transfers between devices  16.9 us (16%)
  local copies, waits for them, and re-layouts  3.84 us (4%)
  waiting for transfers between devices  3.55 us (3%)
    pallas_call x8, Pallas kernels, call(): pl.pallas_call(kernel, out_shape=outs, in_specs=in_specs or [VMEM] * len(...  79.8 us
    ppermute x8, starting transfers between devices, exchange(): return lax.ppermute(value, axis, route)  16.9 us
    unnamed x18, local copies, waits for them, and re-layouts  3.84 us
    ppermute x8, waiting for transfers between devices, exchange(): return lax.ppermute(value, axis, route)  3.55 us
  transfers between devices with their start and end apart: 8, of which 2 were waited for; matrix products, arithmetic and copies ran while one was open for 0% of the time, Pallas kernels for 11%

profile of v1, /device:TPU:3, one launch (start us, length us, event | category | flops | bytes accessed | tf_op | source)
XLA Modules:
  0.0 104.9 jit_solution(1643835888692457048)
XLA Ops:
  0.6 64.8 %shard_map.86 = (f32[264,1024]{1,0:T(8,128)}, f32[264,1024]{1,0:T(8,128)}, f32[16,1024]{1,0:T(8,128)}, f32[16,1024]{1,0:T(8,128)}, f32[10,8,128]{2,1,0:T(8,128)}) custom-call(f32[3,2,64,1024]{3,2,1,0:T(8,128)} %u.7, s32[3,2,64,1024]{3,2,1,0:T(8,128)} %cls.3, s32[3,2,8,8]{3,2,1,0:T(8,128)} %shift.9, f32[8]{0:T(128)} %stiff.1, f32[2]{0:T(128)} %cross.1, s32[3]{0:T(128)} %fixed.1), custom_call_target="tpu_custom_call" | custom-call | tf_op jit(solution)/shard_map/pallas_call | solution.py:528
  65.5 0.0 copy-start
  65.5 0.0 copy-start.3
  65.5 0.0 copy-start.4
  65.5 0.0 copy-start.5
  65.5 0.9 copy-done.5
  66.5 0.0 copy-start.7
  66.5 0.8 copy-done.7
  67.3 0.0 copy-start.6
  67.3 0.6 copy-done.6
  67.9 0.0 copy-start.8
  67.9 0.7 collective-permute-start
  68.6 0.0 copy-done.8
  68.6 3.6 %collective-permute-start.3 = (f32[264,1024]{1,0:T(8,128)}, f32[264,1024]{1,0:T(8,128)S(1)}, u32[]{:S(2)}, u32[]{:S(2)}) collective-permute-start(f32[264,1024]{1,0:T(8,128)} %get-tuple-element.36), channel_id=1, source_target_pairs={{8,16},{16,8},{9,17},{17,9},{10,18},{18,10},{11,19},{19,11},{12,20... | collective-permute-start | bytes 3244040 | tf_op jit(solution)/shard_map/ppermute | solution.py:27
  72.3 0.3 collective-permute-start.1
  72.6 4.1 %collective-permute-start.2 = (f32[16,1024]{1,0:T(8,128)}, f32[16,1024]{1,0:T(8,128)S(1)}, u32[]{:S(2)}, u32[]{:S(2)}) collective-permute-start(f32[16,1024]{1,0:T(8,128)} %copy-done.8), channel_id=1, source_target_pairs={{1,2},{2,1},{3,4},{4,3},{5,6},{6,5},{9,10},{10,9},{11,12},{12,11},... | collective-permute-start | bytes 196616 | tf_op jit(solution)/shard_map/ppermute | solution.py:27
  76.7 0.0 copy-done
  76.7 0.0 copy-done.3
  76.7 0.0 copy-done.4
  76.7 0.0 copy-start.1
  76.8 1.4 %copy-done.1 = s32[3,2,64,1024]{3,2,1,0:T(8,128)S(1)} copy-done((s32[3,2,64,1024]{3,2,1,0:T(8,128)S(1)}, s32[3,2,64,1024]{3,2,1,0:T(8,128)}, u32[]{:S(2)}) %copy-start.1) | copy-done | bytes 1572888
  78.2 0.0 copy-start.2
  78.2 4.2 %shard_map.87 = (f32[3,2,64,1024]{3,2,1,0:T(8,128)S(1)}, f32[3,2,64,1024]{3,2,1,0:T(8,128)S(1)}) custom-call(f32[3,2,64,1024]{3,2,1,0:T(8,128)S(1)} %copy-done, s32[3,2,64,1024]{3,2,1,0:T(8,128)S(1)} %copy-done.1, s32[3,2,8,8]{3,2,1,0:T(8,128)S(1)} %copy-done.4, f32[10,8,128]{2,1,0:T(8,128)S(1)} %copy-done.3), custom_call_target="tpu_custom_call" | custom-call | tf_op jit(solution)/shard_map/pallas_call | solution.py:528
  82.3 0.0 collective-permute-done.1.rim_a
  82.4 0.0 collective-permute-done.2.rim_b
  82.4 0.0 collective-permute-done.fast
  82.4 0.0 copy-done.2
  82.4 1.6 %shard_map.89 = (f32[3,2,64,1024]{3,2,1,0:T(8,128)S(1)}, s32[3,8,1024]{2,1,0:T(8,128)S(1)}) custom-call(f32[3,2,64,1024]{3,2,1,0:T(8,128)S(1)} %copy-done, f32[3,2,64,1024]{3,2,1,0:T(8,128)S(1)} %copy-done.2, f32[3,2,64,1024]{3,2,1,0:T(8,128)S(1)} %get-tuple-element.26.total_in, ...), custom_call_target="tpu_custom_call", output_to_operand_aliasing={{0}: (2, {})} | custom-call | tf_op jit(solution)/shard_map/pallas_call | solution.py:528
  83.9 1.4 %collective-permute-done.3.arrived = f32[264,1024]{1,0:T(8,128)S(1)} collective-permute-done((f32[264,1024]{1,0:T(8,128)}, f32[264,1024]{1,0:T(8,128)S(1)}, u32[]{:S(2)}, u32[]{:S(2)}) %collective-permute-start.3) | collective-permute-done | bytes 1081376 | tf_op jit(solution)/shard_map/ppermute | solution.py:27
  85.3 1.4 %shard_map.90 = (f32[3,2,64,1024]{3,2,1,0:T(8,128)S(1)}, f32[3,2,64,1024]{3,2,1,0:T(8,128)S(1)}, f32[256,1024]{1,0:T(8,128)S(1)}, f32[256,1024]{1,0:T(8,128)S(1)...) custom-call(f32[3,2,64,1024]{3,2,1,0:T(8,128)S(1)} %copy-done, ...), custom_call_target="tpu_custom_call" | custom-call | tf_op jit(solution)/shard_map/pallas_call | solution.py:528
  86.7 0.1 collective-permute-start.4
  86.8 3.6 %collective-permute-start.7 = (f32[256,1024]{1,0:T(8,128)S(1)}, f32[256,1024]{1,0:T(8,128)S(1)}, u32[]{:S(2)}, u32[]{:S(2)}) collective-permute-start(f32[256,1024]{1,0:T(8,128)S(1)} %get-tuple-element.44), channel_id=1, source_target_pairs={{8,16},{16,8},{9,17},{17,9},{10,18},{18,10},{11,19},{19,11},{12,20... | collective-permute-start | bytes 3145736 | tf_op jit(solution)/shard_map/ppermute | solution.py:27
  90.4 0.3 collective-permute-start.5
  90.7 4.1 %collective-permute-start.6 = (f32[16,1024]{1,0:T(8,128)S(1)}, f32[16,1024]{1,0:T(8,128)S(1)}, u32[]{:S(2)}, u32[]{:S(2)}) collective-permute-start(f32[16,1024]{1,0:T(8,128)S(1)} %get-tuple-element.41), channel_id=1, source_target_pairs={{1,2},{2,1},{3,4},{4,3},{5,6},{6,5},{9,10},{10,9},{11,12},{12,11},... | collective-permute-start | bytes 196616 | tf_op jit(solution)/shard_map/ppermute | solution.py:27
  94.9 3.9 %shard_map.91.total_in = f32[3,2,64,1024]{3,2,1,0:T(8,128)S(1)} custom-call(f32[3,2,64,1024]{3,2,1,0:T(8,128)S(1)} %get-tuple-element.37.u, f32[3,2,64,1024]{3,2,1,0:T(8,128)S(1)} %get-tuple-element.38.w, f32[3,2,64,1024]{3,2,1,0:T(8,128)S(1)} %get-tuple-element.27.half, s32[3,2,8,8]{3,2,1,0:T(8,128)S(1)} %copy-done.4, f32[10,8,128]{2,1,0:T(8,128)S(1)} %copy-done.3), custom_call_target="tpu_custom_call" | custom-call | tf_op jit(solution)/shard_map/pallas_call | solution.py:528
  98.8 0.0 collective-permute-done.5.rim_a
  98.8 0.0 collective-permute-done.6.rim_b
  98.8 0.0 collective-permute-done.4.fast
  98.8 1.9 %shard_map.92 = (f32[3,2,64,1024]{3,2,1,0:T(8,128)S(1)}, f32[3,2,64,1024]{3,2,1,0:T(8,128)}, f32[3,2,64,1024]{3,2,1,0:T(8,128)}) custom-call(f32[3,2,64,1024]{3,2,1,0:T(8,128)S(1)} %get-tuple-element.37.u, f32[3,2,64,1024]{3,2,1,0:T(8,128)S(1)} %shard_map.91.total_in, ...), custom_call_target="tpu_custom_call", output_to_operand_aliasing={{0}: (1, {})} | custom-call | tf_op jit(solution)/shard_map/pallas_call | solution.py:528
  100.7 2.2 %collective-permute-done.7.arrived = f32[256,1024]{1,0:T(8,128)S(1)} collective-permute-done((f32[256,1024]{1,0:T(8,128)S(1)}, f32[256,1024]{1,0:T(8,128)S(1)}, u32[]{:S(2)}, u32[]{:S(2)}) %collective-permute-start.7) | collective-permute-done | bytes 1048608 | tf_op jit(solution)/shard_map/ppermute | solution.py:27
  102.9 2.1 %shard_map.93 = (f32[3,2,64,1024]{3,2,1,0:T(8,128)}, f32[3,2,64,1024]{3,2,1,0:T(8,128)}) custom-call(f32[3,2,64,1024]{3,2,1,0:T(8,128)S(1)} %get-tuple-element.37.u, f32[3,2,64,1024]{3,2,1,0:T(8,128)S(1)} %get-tuple-element.43.total, f32[256,1024]{1,0:T(8,128)S(1)} %collective-permute-done.7.arrived, ...), custom_call_target="tpu_custom_call", output_to_operand_aliasing={{0}: (5, {}), {1}: (6, {})} | custom-call | tf_op jit(solution)/shard_map/pallas_call | solution.py:528
  (1 shorter events, 0.0 us)
Async XLA Ops:
  65.5 11.2 %copy-start = (f32[3,2,64,1024]{3,2,1,0:T(8,128)S(1)}, f32[3,2,64,1024]{3,2,1,0:T(8,128)}, u32[]{:S(2)}) copy-start(f32[3,2,64,1024]{3,2,1,0:T(8,128)} %u.7) | copy-start | bytes 4718596
  65.5 11.2 %copy-start.3 = (f32[10,8,128]{2,1,0:T(8,128)S(1)}, f32[10,8,128]{2,1,0:T(8,128)}, u32[]{:S(2)}) copy-start(f32[10,8,128]{2,1,0:T(8,128)} %get-tuple-element.25.splat) | copy-start | bytes 122884
  65.5 11.2 %copy-start.4 = (s32[3,2,8,8]{3,2,1,0:T(8,128)S(1)}, s32[3,2,8,8]{3,2,1,0:T(8,128)}, u32[]{:S(2)}) copy-start(s32[3,2,8,8]{3,2,1,0:T(8,128)} %shift.9) | copy-start | bytes 4612
  65.5 1.0 copy-start.5
  66.5 0.8 copy-start.7
  67.3 0.6 copy-start.6
  67.9 0.7 copy-start.8
  67.9 14.4 %collective-permute-start = (f32[264,1024]{1,0:T(8,128)}, f32[264,1024]{1,0:T(8,128)S(1)}, u32[]{:S(2)}, u32[]{:S(2)}) collective-permute-start(f32[264,1024]{1,0:T(8,128)} %get-tuple-element.32), channel_id=1, source_target_pairs={{0,8},{8,0},{16,24},{24,16},{1,9},{9,1},{17,25},{25,17},{2,10},{10... | collective-permute-start | bytes 3244040 | tf_op jit(solution)/shard_map/ppermute | solution.py:27
  68.6 16.7 %collective-permute-start.3 = (f32[264,1024]{1,0:T(8,128)}, f32[264,1024]{1,0:T(8,128)S(1)}, u32[]{:S(2)}, u32[]{:S(2)}) collective-permute-start(f32[264,1024]{1,0:T(8,128)} %get-tuple-element.36), channel_id=1, source_target_pairs={{8,16},{16,8},{9,17},{17,9},{10,18},{18,10},{11,19},{19,11},{12,20... | collective-permute-start | bytes 3244040 | tf_op jit(solution)/shard_map/ppermute | solution.py:27
  72.3 10.1 %collective-permute-start.1 = (f32[16,1024]{1,0:T(8,128)}, f32[16,1024]{1,0:T(8,128)S(1)}, u32[]{:S(2)}, u32[]{:S(2)}) collective-permute-start(f32[16,1024]{1,0:T(8,128)} %copy-done.6), channel_id=1, source_target_pairs={{0,1},{1,0},{2,3},{3,2},{4,5},{5,4},{6,7},{7,6},{8,9},{9,8},{10,11... | collective-permute-start | bytes 196616 | tf_op jit(solution)/shard_map/ppermute | solution.py:27
  72.6 9.8 %collective-permute-start.2 = (f32[16,1024]{1,0:T(8,128)}, f32[16,1024]{1,0:T(8,128)S(1)}, u32[]{:S(2)}, u32[]{:S(2)}) collective-permute-start(f32[16,1024]{1,0:T(8,128)} %copy-done.8), channel_id=1, source_target_pairs={{1,2},{2,1},{3,4},{4,3},{5,6},{6,5},{9,10},{10,9},{11,12},{12,11},... | collective-permute-start | bytes 196616 | tf_op jit(solution)/shard_map/ppermute | solution.py:27
  76.7 1.4 %copy-start.1 = (s32[3,2,64,1024]{3,2,1,0:T(8,128)S(1)}, s32[3,2,64,1024]{3,2,1,0:T(8,128)}, u32[]{:S(2)}) copy-start(s32[3,2,64,1024]{3,2,1,0:T(8,128)} %cls.3) | copy-start | bytes 4718596
  78.2 4.2 %copy-start.2 = (f32[3,2,64,1024]{3,2,1,0:T(8,128)S(1)}, f32[3,2,64,1024]{3,2,1,0:T(8,128)}, u32[]{:S(2)}) copy-start(f32[3,2,64,1024]{3,2,1,0:T(8,128)} %w.1) | copy-start | bytes 4718596
  86.7 12.1 %collective-permute-start.4 = (f32[256,1024]{1,0:T(8,128)S(1)}, f32[256,1024]{1,0:T(8,128)S(1)}, u32[]{:S(2)}, u32[]{:S(2)}) collective-permute-start(f32[256,1024]{1,0:T(8,128)S(1)} %get-tuple-element.39), channel_id=1, source_target_pairs={{0,8},{8,0},{16,24},{24,16},{1,9},{9,1},{17,25},{25,17},{2,10},{10... | collective-permute-start | bytes 3145736 | tf_op jit(solution)/shard_map/ppermute | solution.py:27
  86.8 16.1 %collective-permute-start.7 = (f32[256,1024]{1,0:T(8,128)S(1)}, f32[256,1024]{1,0:T(8,128)S(1)}, u32[]{:S(2)}, u32[]{:S(2)}) collective-permute-start(f32[256,1024]{1,0:T(8,128)S(1)} %get-tuple-element.44), channel_id=1, source_target_pairs={{8,16},{16,8},{9,17},{17,9},{10,18},{18,10},{11,19},{19,11},{12,20... | collective-permute-start | bytes 3145736 | tf_op jit(solution)/shard_map/ppermute | solution.py:27
  90.4 8.4 %collective-permute-start.5 = (f32[16,1024]{1,0:T(8,128)S(1)}, f32[16,1024]{1,0:T(8,128)S(1)}, u32[]{:S(2)}, u32[]{:S(2)}) collective-permute-start(f32[16,1024]{1,0:T(8,128)S(1)} %get-tuple-element.40), channel_id=1, source_target_pairs={{0,1},{1,0},{2,3},{3,2},{4,5},{5,4},{6,7},{7,6},{8,9},{9,8},{10,11... | collective-permute-start | bytes 196616 | tf_op jit(solution)/shard_map/ppermute | solution.py:27
  90.7 8.1 %collective-permute-start.6 = (f32[16,1024]{1,0:T(8,128)S(1)}, f32[16,1024]{1,0:T(8,128)S(1)}, u32[]{:S(2)}, u32[]{:S(2)}) collective-permute-start(f32[16,1024]{1,0:T(8,128)S(1)} %get-tuple-element.41), channel_id=1, source_target_pairs={{1,2},{2,1},{3,4},{4,3},{5,6},{6,5},{9,10},{10,9},{11,12},{12,11},... | collective-permute-start | bytes 196616 | tf_op jit(solution)/shard_map/ppermute | solution.py:27

commit v2 on v1

--- a/solution.py
+++ b/solution.py
@@ -13,7 +13,6 @@
 
 VMEM = pl.BlockSpec(memory_space=pltpu.VMEM)
 ANY = pl.BlockSpec(memory_space=pl.ANY)
-LEAD_LIMIT = 64 << 20
 
 INSIDE, SLOW, FAST, TABLE, MOVING = 0, 2, 4, 6, 7
 
@@ -103,32 +102,15 @@
     return lax.broadcasted_iota(jnp.int32, (rows, width), 1) & (COLS - 1)
 
 
-def put_tail(shift, out, first, width):
-    sections, _, rbs, _ = shift.shape
-    lane = lanes(rbs, width)
-    parts = [
-        spread(shift[s, h], width)
-        for s, h in ((sections - 1, 0), (sections - 1, 1), (sections - 2, 1))
-    ]
-    mixed = jnp.where(lane == 0, parts[0], jnp.where(lane == 1, parts[1], parts[2]))
-    out[first : first + rbs, :] = mixed.astype(jnp.float32)
-
-
-def put_index(after, shift, arrived, first, index):
+def put_index(after, shift, before, index):
     sections, _, rbs, _ = shift.shape
     width = index.shape[2]
     lane = lanes(rbs, width)
-    for j, (own, _, hops) in enumerate(pairs_of(after, sections)):
+    for j, (own, block, hops) in enumerate(pairs_of(after, sections)):
         if after:
             offset = spread(shift[own, hops - 1], width)
         else:
-            blocks = per_tile(
-                width,
-                lambda cb: jnp.broadcast_to(
-                    arrived[first : first + rbs, cb * COLS + j : cb * COLS + j + 1], (rbs, COLS)
-                ),
-            )
-            offset = -blocks.astype(jnp.int32)
+            offset = -spread(before[sections - 1 - block, hops - 1], width)
         index[j, 0:rbs, :] = (lane + offset) & (COLS - 1)
 
 
@@ -175,76 +157,31 @@
         splat[MOVING + s] = jnp.full(tile, jnp.where(fixed[s] == 0, 1.0, 0.0))
 
 
-def lead_kernel(
-    u, cls, shift, stiff, cross, fixed, slow, fast, rim_a, rim_b, splat,
-    shift_here, stiff_here, cross_here, fixed_here, first_here, last_here, cls_here,
-    tail_here, rim_a_here, rim_b_here, splat_here, sem,
-):
-    sections, _, rows, width = u.shape
-
-    def copies(first, pairs):
-        return [
-            pltpu.make_async_copy(source, target, sem.at[first + k])
-            for k, (source, target) in enumerate(pairs)
-        ]
-
-    def blocks(after):
-        pairs = []
+def lead_kernel(u, slow, fast):
+    sections, _, rows, _ = u.shape
+
+    def body(after):
         for out, side in ((slow, after), (fast, not after)):
             for k, own in enumerate((near_of(side, sections), second_of(side, sections))):
                 for c in range(2):
-                    pairs.append((u.at[own, c], out.at[pl.ds((2 * k + c) * rows, rows)]))
-        return copies(0, pairs)
-
-    bottom = pl.ds(rows - ROWS, ROWS)
-    small = copies(
-        8,
-        (
-            (shift, shift_here),
-            (stiff, stiff_here),
-            (cross, cross_here),
-            (fixed, fixed_here),
-            (u.at[:, :, pl.ds(0, ROWS)], first_here),
-            (u.at[:, :, bottom], last_here),
-            (cls.at[:, 1, bottom], cls_here),
-        ),
-    )
-    for copy in small:
-        copy.start()
-    by_side(lambda after: [copy.start() for copy in blocks(after)])
-    for copy in small:
-        copy.wait()
-    put_tail(shift_here, tail_here, 0, width)
-    put_splat(stiff_here, cross_here, fixed_here, splat_here)
-    table = splat_here[TABLE]
+                    out[(2 * k + c) * rows : (2 * k + c + 1) * rows, :] = u[own, c]
+
+    by_side(body)
+
+
+def prepare_kernel(u, cls, before, stiff, cross, fixed, rim_a, rim_b, splat):
+    sections, _, rows, _ = u.shape
+    last = slice(rows - 1, rows)
+    put_splat(stiff, cross, fixed, splat)
+    table = splat[TABLE]
     put_rims(
-        lambda s, c: first_here[s, c, 0:1, :],
-        lambda s, c: last_here[s, c, ROWS - 1 : ROWS, :],
-        lambda s: look_up(table, cls_here[s, ROWS - 1 : ROWS, :]),
-        rim_a_here,
-        rim_b_here,
+        lambda s, c: u[s, c, 0:1, :],
+        lambda s, c: u[s, c, last, :],
+        lambda s: look_up(table, cls[s, 1, last, :]),
+        rim_a,
+        rim_b,
         sections,
     )
-    after_blocks = pl.ds(4 * rows, tail_here.shape[0])
-    results = copies(
-        15,
-        (
-            (tail_here, slow.at[after_blocks]),
-            (tail_here, fast.at[after_blocks]),
-            (rim_a_here, rim_a),
-            (rim_b_here, rim_b),
-            (splat_here, splat),
-        ),
-    )
-    for copy in results:
-        copy.start()
-    by_side(lambda after: [copy.wait() for copy in blocks(after)])
-    for copy in results:
-        copy.wait()
-
-
-def hand_on_kernel(*refs):
-    pass
 
 
 def wide_splat(splat, k, width):
@@ -389,7 +326,7 @@
                 total[own, c, rows_of(rb), :] += f[c]
 
 
-def first_rims_kernel(u, w, total_in, half, fast, rim_a, rim_b, shift, splat, total, index):
+def first_rims_kernel(u, w, total_in, half, fast, rim_a, rim_b, shift, before, splat, total, index):
     sections, _, rows, _ = u.shape
 
     def damp(rb, carry):
@@ -402,7 +339,7 @@
     lax.fori_loop(0, rows // ROWS, damp, 0)
 
     def body(after):
-        put_index(not after, shift, fast, 4 * rows, index)
+        put_index(not after, shift, before, index)
         fast_flows(u, not after, fast, index, splat, total, range(3))
 
     by_side(body)
@@ -455,12 +392,13 @@
 
 
 def step_kernel(
-    u, total, arrived, half, shift, splat, new_u, new_w, slow, fast, index, rim_a, rim_b
+    u, total, arrived, half, shift, before, splat,
+    new_u, new_w, slow, fast, index, rim_a, rim_b,
 ):
     sections, _, rows, width = u.shape
 
     def body(after):
-        put_index(after, shift, arrived, 4 * rows, index)
+        put_index(after, shift, before, index)
         slow_edge = (near_of(after, sections), second_of(after, sections))
         fast_edge = (near_of(not after, sections), second_of(not after, sections))
         for s in range(sections):
@@ -544,47 +482,24 @@
         return jax.ShapeDtypeStruct(shape, dtype)
 
     full = array(*u.shape)
-    tail = array(tail_rows(rows), width)
     two = array(4 * rows, width)
-    two_tail = array(4 * rows + tail.shape[0], width)
     rim = array(-(-3 * sections // ROWS) * ROWS, width)
     splat = array(MOVING + sections, ROWS, COLS)
-    index = array(3, tail.shape[0], width, dtype=jnp.int32)
+    index = array(3, tail_rows(rows), width, dtype=jnp.int32)
     scalars = [pltpu.SMEM(shift.shape, jnp.int32), pltpu.SemaphoreType.DMA]
-
-    ends = pltpu.VMEM((sections, 2, ROWS, width), jnp.float32)
-    slow, fast, rim_a, rim_b, splat = call(
-        lead_kernel,
-        [two_tail, two_tail, rim, rim, splat],
-        [u, cls, shift, stiff, cross, fixed],
-        scratch=[
-            pltpu.VMEM(shift.shape, jnp.int32),
-            pltpu.SMEM(stiff.shape, jnp.float32),
-            pltpu.SMEM(cross.shape, jnp.float32),
-            pltpu.SMEM(fixed.shape, jnp.int32),
-            ends,
-            ends,
-            pltpu.VMEM((sections, ROWS, width), jnp.int32),
-            pltpu.VMEM(tail.shape, jnp.float32),
-            pltpu.VMEM(rim.shape, jnp.float32),
-            pltpu.VMEM(rim.shape, jnp.float32),
-            pltpu.VMEM(splat.shape, jnp.float32),
-            pltpu.SemaphoreType.DMA((20,)),
-        ],
-        in_specs=[ANY] * 6,
-        out_specs=[ANY] * 5,
-        limit=LEAD_LIMIT,
-    )
-    slow, fast, rim_a, rim_b = call(
-        hand_on_kernel,
-        [two_tail, two_tail, rim, rim],
-        [slow, fast, rim_a, rim_b],
-        {k: k for k in range(4)},
-        in_specs=[ANY] * 4,
-        out_specs=[ANY] * 4,
-    )
+    smem = pl.BlockSpec(memory_space=pltpu.SMEM)
+
+    n = lax.axis_size("sec")
+    before = lax.ppermute(shift, "sec", [(i, i + 1) for i in range(n - 1)])
+    slow, fast = call(lead_kernel, [two, two], [u])
     slow = exchange(slow, "sec", "b")
     fast = exchange(fast, "sec", "a")
+    rim_a, rim_b, splat = call(
+        prepare_kernel,
+        [rim, rim, splat],
+        [u, cls, before, stiff, cross, fixed],
+        in_specs=[VMEM] * 3 + [smem] * 3,
+    )
     rim_a = exchange(rim_a, "strip", "a")
     rim_b = exchange(rim_b, "strip", "b")
     total, half = call(
@@ -593,13 +508,13 @@
     total, fast_index = call(
         first_rims_kernel,
         [full, index],
-        [u, w, total, half, fast, rim_a, rim_b, shift, splat],
+        [u, w, total, half, fast, rim_a, rim_b, shift, before, splat],
         {2: 0},
     )
     u, w, slow, fast, index, rim_a, rim_b = call(
         step_kernel,
         [full, full, two, two, index, rim, rim],
-        [u, total, slow, half, shift, splat],
+        [u, total, slow, half, shift, before, splat],
     )
     slow = exchange(slow, "sec", "b")
     fast = exchange(fast, "sec", "a")

time: 106 us -> 50.4 us (0.48)
  Pallas kernels: 79.8 us -> 15.8 us
  waiting for transfers between devices: 3.55 us -> 11.7 us
  starting transfers between devices: 16.9 us -> 20.3 us
  local copies, waits for them, and re-layouts: 3.84 us -> 1.43 us
    pallas_call x8, Pallas kernels: 79.8 us -> 15.8 us  [call(): pl.pallas_call(kernel, out_shape=outs, in_specs=in_specs or [VMEM] * len(...]
    ppermute x0 -> x1, waiting for transfers between devices: none -> 9.48 us  [per_device(): before = lax.ppermute(shift, 'sec', [(i, i + 1) for i in range(n - 1)])]
    ppermute x0 -> x1, starting transfers between devices: none -> 2.5 us  [per_device(): before = lax.ppermute(shift, 'sec', [(i, i + 1) for i in range(n - 1)])]
    unnamed x18 -> x14, local copies, waits for them, and re-layouts: 3.84 us -> 1.43 us
    ppermute x8, waiting for transfers between devices: 3.55 us -> 2.22 us  [exchange(): return lax.ppermute(value, axis, route)]
  transfers between devices with their start and end apart: 8 -> 9, of which waited for: 2 -> 2; matrix products, arithmetic and copies ran while one was open for 0% -> 0% of each run, Pallas kernels for 11% -> 24%
where the time goes in v2:
time: 50.4 us; the launch traced here: 50.1 us
  starting transfers between devices  20.3 us (40%)
  Pallas kernels  15.8 us (31%)
  waiting for transfers between devices  11.7 us (23%)
  local copies, waits for them, and re-layouts  1.43 us (3%)
  between operations  0.84 us (2%)
    ppermute x8, starting transfers between devices, exchange(): return lax.ppermute(value, axis, route)  17.8 us
    pallas_call x8, Pallas kernels, call(): pl.pallas_call(kernel, out_shape=outs, in_specs=in_specs or [VMEM] * len(...  15.8 us
    ppermute x1, waiting for transfers between devices, per_device(): before = lax.ppermute(shift, 'sec', [(i, i + 1) for i in range(n - 1)])  9.48 us
    ppermute x1, starting transfers between devices, per_device(): before = lax.ppermute(shift, 'sec', [(i, i + 1) for i in range(n - 1)])  2.5 us
    ppermute x8, waiting for transfers between devices, exchange(): return lax.ppermute(value, axis, route)  2.22 us
    unnamed x14, local copies, waits for them, and re-layouts  1.43 us
  transfers between devices with their start and end apart: 9, of which 2 were waited for; matrix products, arithmetic and copies ran while one was open for 0% of the time, Pallas kernels for 24%

profile of v2, /device:TPU:3, one launch (start us, length us, event | category | flops | bytes accessed | tf_op | source)
XLA Modules:
  0.0 50.1 jit_solution(6661449420972187477)
XLA Ops:
  0.6 0.0 copy-start
  0.6 1.4 %copy-done = f32[3,2,64,1024]{3,2,1,0:T(8,128)S(1)} copy-done((f32[3,2,64,1024]{3,2,1,0:T(8,128)S(1)}, f32[3,2,64,1024]{3,2,1,0:T(8,128)}, u32[]{:S(2)}) %copy-start) | copy-done | bytes 1572888
  2.0 0.0 copy-start.1
  2.0 0.0 copy-start.4
  2.0 0.0 copy-start.5
  2.0 0.0 copy-start.6
  2.1 0.2 shard_map.88
  2.2 0.7 %collective-permute-start.1 = (f32[256,1024]{1,0:T(8,128)S(1)}, f32[256,1024]{1,0:T(8,128)S(1)}, u32[]{:S(2)}, u32[]{:S(2)}) collective-permute-start(f32[256,1024]{1,0:T(8,128)S(1)} %get-tuple-element.24), channel_id=1, source_target_pairs={{0,8},{8,0},{16,24},{24,16},{1,9},{9,1},{17,25},{25,17},{2,10},{10... | collective-permute-start | bytes 3145736 | tf_op jit(solution)/shard_map/ppermute | solution.py:26
  3.0 0.0 copy-start.3
  3.0 3.2 %collective-permute-start.4 = (f32[256,1024]{1,0:T(8,128)S(1)}, f32[256,1024]{1,0:T(8,128)S(1)}, u32[]{:S(2)}, u32[]{:S(2)}) collective-permute-start(f32[256,1024]{1,0:T(8,128)S(1)} %get-tuple-element.28), channel_id=1, source_target_pairs={{8,16},{16,8},{9,17},{17,9},{10,18},{18,10},{11,19},{19,11},{12,20... | collective-permute-start | bytes 3145736 | tf_op jit(solution)/shard_map/ppermute | solution.py:26
  6.2 2.5 %collective-permute-start = (s32[3,2,8,8]{3,2,1,0:T(8,128)}, s32[3,2,8,8]{3,2,1,0:T(8,128)S(1)}, u32[]{:S(2)}, u32[]{:S(2)}) collective-permute-start(s32[3,2,8,8]{3,2,1,0:T(8,128)} %shift.7), channel_id=1, source_target_pairs={{0,8},{8,16},{16,24},{1,9},{9,17},{17,25},{2,10},{10,18},{18,26},{... | collective-permute-start | bytes 4616 | tf_op jit(solution)/shard_map/ppermute | solution.py:493
  8.7 9.5 %collective-permute-done.before = s32[3,2,8,8]{3,2,1,0:T(8,128)S(1)} collective-permute-done((s32[3,2,8,8]{3,2,1,0:T(8,128)}, s32[3,2,8,8]{3,2,1,0:T(8,128)S(1)}, u32[]{:S(2)}, u32[]{:S(2)}) %collective-permute-start) | collective-permute-done | bytes 1568 | tf_op jit(solution)/shard_map/ppermute | solution.py:493
  18.1 0.0 copy-done.1
  18.1 0.0 copy-done.4
  18.1 0.0 copy-done.5
  18.1 0.0 copy-done.6
  18.2 0.7 %shard_map.86 = (f32[16,1024]{1,0:T(8,128)S(1)}, f32[16,1024]{1,0:T(8,128)S(1)}, f32[10,8,128]{2,1,0:T(8,128)S(1)}) custom-call(f32[3,2,64,1024]{3,2,1,0:T(8,128)S(1)} %copy-done, s32[3,2,64,1024]{3,2,1,0:T(8,128)S(1)} %copy-done.1, s32[3,2,8,8]{3,2,1,0:T(8,128)S(1)} %collective-permute-done.before, f32[8]{0:T(128)S(1)} %copy-done.4, f32[2]{0:T(128)S(1)} %copy-done.5, ...), custom_call_target="tpu_custom_call" | custom-call | tf_op jit(solution)/shard_map/pallas_call | solution.py:466
  18.8 0.3 collective-permute-start.2
  19.2 4.1 %collective-permute-start.3 = (f32[16,1024]{1,0:T(8,128)S(1)}, f32[16,1024]{1,0:T(8,128)S(1)}, u32[]{:S(2)}, u32[]{:S(2)}) collective-permute-start(f32[16,1024]{1,0:T(8,128)S(1)} %get-tuple-element.26), channel_id=1, source_target_pairs={{1,2},{2,1},{3,4},{4,3},{5,6},{6,5},{9,10},{10,9},{11,12},{12,11},... | collective-permute-start | bytes 196616 | tf_op jit(solution)/shard_map/ppermute | solution.py:26
  23.3 0.0 copy-done.3
  23.3 0.0 copy-start.2
  23.3 4.2 %shard_map.87 = (f32[3,2,64,1024]{3,2,1,0:T(8,128)S(1)}, f32[3,2,64,1024]{3,2,1,0:T(8,128)S(1)}) custom-call(f32[3,2,64,1024]{3,2,1,0:T(8,128)S(1)} %copy-done, s32[3,2,64,1024]{3,2,1,0:T(8,128)S(1)} %copy-done.1, s32[3,2,8,8]{3,2,1,0:T(8,128)S(1)} %copy-done.3, f32[10,8,128]{2,1,0:T(8,128)S(1)} %get-tuple-element.21.splat), custom_call_target="tpu_custom_call" | custom-call | tf_op jit(solution)/shard_map/pallas_call | solution.py:466
  27.5 0.0 collective-permute-done.2.rim_a
  27.5 0.0 collective-permute-done.3.rim_b
  27.5 0.0 collective-permute-done.1.fast
  27.5 0.0 copy-done.2
  27.6 1.6 %shard_map.89 = (f32[3,2,64,1024]{3,2,1,0:T(8,128)S(1)}, s32[3,8,1024]{2,1,0:T(8,128)S(1)}) custom-call(f32[3,2,64,1024]{3,2,1,0:T(8,128)S(1)} %copy-done, f32[3,2,64,1024]{3,2,1,0:T(8,128)S(1)} %copy-done.2, f32[3,2,64,1024]{3,2,1,0:T(8,128)S(1)} %get-tuple-element.22.total_in, ...), custom_call_target="tpu_custom_call", output_to_operand_aliasing={{0}: (2, {})} | custom-call | tf_op jit(solution)/shard_map/pallas_call | solution.py:466
  29.2 0.0 collective-permute-done.4.arrived
  29.2 1.4 %shard_map.90 = (f32[3,2,64,1024]{3,2,1,0:T(8,128)S(1)}, f32[3,2,64,1024]{3,2,1,0:T(8,128)S(1)}, f32[256,1024]{1,0:T(8,128)S(1)}, f32[256,1024]{1,0:T(8,128)S(1)...) custom-call(f32[3,2,64,1024]{3,2,1,0:T(8,128)S(1)} %copy-done, ...), custom_call_target="tpu_custom_call" | custom-call | tf_op jit(solution)/shard_map/pallas_call | solution.py:466
  30.6 0.1 collective-permute-start.5
  30.7 5.0 %collective-permute-start.8 = (f32[256,1024]{1,0:T(8,128)S(1)}, f32[256,1024]{1,0:T(8,128)S(1)}, u32[]{:S(2)}, u32[]{:S(2)}) collective-permute-start(f32[256,1024]{1,0:T(8,128)S(1)} %get-tuple-element.36), channel_id=1, source_target_pairs={{8,16},{16,8},{9,17},{17,9},{10,18},{18,10},{11,19},{19,11},{12,20... | collective-permute-start | bytes 3145736 | tf_op jit(solution)/shard_map/ppermute | solution.py:26
  35.6 0.1 collective-permute-start.6
  35.7 4.4 %collective-permute-start.7 = (f32[16,1024]{1,0:T(8,128)S(1)}, f32[16,1024]{1,0:T(8,128)S(1)}, u32[]{:S(2)}, u32[]{:S(2)}) collective-permute-start(f32[16,1024]{1,0:T(8,128)S(1)} %get-tuple-element.33), channel_id=1, source_target_pairs={{1,2},{2,1},{3,4},{4,3},{5,6},{6,5},{9,10},{10,9},{11,12},{12,11},... | collective-permute-start | bytes 196616 | tf_op jit(solution)/shard_map/ppermute | solution.py:26
  40.1 3.9 %shard_map.91.total_in = f32[3,2,64,1024]{3,2,1,0:T(8,128)S(1)} custom-call(f32[3,2,64,1024]{3,2,1,0:T(8,128)S(1)} %get-tuple-element.29.u, f32[3,2,64,1024]{3,2,1,0:T(8,128)S(1)} %get-tuple-element.30.w, f32[3,2,64,1024]{3,2,1,0:T(8,128)S(1)} %get-tuple-element.23.half, s32[3,2,8,8]{3,2,1,0:T(8,128)S(1)} %copy-done.3, f32[10,8,128]{2,1,0:T(8,128)S(1)} %get-tuple-element.21.splat), custom_call_target="tpu_custom_call" | custom-call | tf_op jit(solution)/shard_map/pallas_call | solution.py:466
  44.0 0.0 collective-permute-done.6.rim_a
  44.0 0.0 collective-permute-done.7.rim_b
  44.0 0.0 collective-permute-done.5.fast
  44.1 1.8 %shard_map.92 = (f32[3,2,64,1024]{3,2,1,0:T(8,128)S(1)}, f32[3,2,64,1024]{3,2,1,0:T(8,128)}, f32[3,2,64,1024]{3,2,1,0:T(8,128)}) custom-call(f32[3,2,64,1024]{3,2,1,0:T(8,128)S(1)} %get-tuple-element.29.u, f32[3,2,64,1024]{3,2,1,0:T(8,128)S(1)} %shard_map.91.total_in, ...), custom_call_target="tpu_custom_call", output_to_operand_aliasing={{0}: (1, {})} | custom-call | tf_op jit(solution)/shard_map/pallas_call | solution.py:466
  45.9 2.2 %collective-permute-done.8.arrived = f32[256,1024]{1,0:T(8,128)S(1)} collective-permute-done((f32[256,1024]{1,0:T(8,128)S(1)}, f32[256,1024]{1,0:T(8,128)S(1)}, u32[]{:S(2)}, u32[]{:S(2)}) %collective-permute-start.8) | collective-permute-done | bytes 1048608 | tf_op jit(solution)/shard_map/ppermute | solution.py:26
  48.1 2.0 %shard_map.93 = (f32[3,2,64,1024]{3,2,1,0:T(8,128)}, f32[3,2,64,1024]{3,2,1,0:T(8,128)}) custom-call(f32[3,2,64,1024]{3,2,1,0:T(8,128)S(1)} %get-tuple-element.29.u, f32[3,2,64,1024]{3,2,1,0:T(8,128)S(1)} %get-tuple-element.35.total, f32[256,1024]{1,0:T(8,128)S(1)} %collective-permute-done.8.arrived, ...), custom_call_target="tpu_custom_call", output_to_operand_aliasing={{0}: (5, {}), {1}: (6, {})} | custom-call | tf_op jit(solution)/shard_map/pallas_call | solution.py:466
Async XLA Ops:
  0.6 1.4 %copy-start = (f32[3,2,64,1024]{3,2,1,0:T(8,128)S(1)}, f32[3,2,64,1024]{3,2,1,0:T(8,128)}, u32[]{:S(2)}) copy-start(f32[3,2,64,1024]{3,2,1,0:T(8,128)} %u.9) | copy-start | bytes 4718596
  2.0 16.1 %copy-start.1 = (s32[3,2,64,1024]{3,2,1,0:T(8,128)S(1)}, s32[3,2,64,1024]{3,2,1,0:T(8,128)}, u32[]{:S(2)}) copy-start(s32[3,2,64,1024]{3,2,1,0:T(8,128)} %cls.3) | copy-start | bytes 4718596
  2.0 16.1 %copy-start.4 = (f32[8]{0:T(128)S(1)}, f32[8]{0:T(128)}, u32[]{:S(2)}) copy-start(f32[8]{0:T(128)} %stiff.1) | copy-start | bytes 100
  2.0 16.1 %copy-start.5 = (f32[2]{0:T(128)S(1)}, f32[2]{0:T(128)}, u32[]{:S(2)}) copy-start(f32[2]{0:T(128)} %cross.1) | copy-start | bytes 28
  2.0 16.1 %copy-start.6 = (s32[3]{0:T(128)S(1)}, s32[3]{0:T(128)}, u32[]{:S(2)}) copy-start(s32[3]{0:T(128)} %fixed.1) | copy-start | bytes 40
  2.2 25.3 %collective-permute-start.1 = (f32[256,1024]{1,0:T(8,128)S(1)}, f32[256,1024]{1,0:T(8,128)S(1)}, u32[]{:S(2)}, u32[]{:S(2)}) collective-permute-start(f32[256,1024]{1,0:T(8,128)S(1)} %get-tuple-element.24), channel_id=1, source_target_pairs={{0,8},{8,0},{16,24},{24,16},{1,9},{9,1},{17,25},{25,17},{2,10},{10... | collective-permute-start | bytes 3145736 | tf_op jit(solution)/shard_map/ppermute | solution.py:26
  3.0 20.3 %copy-start.3 = (s32[3,2,8,8]{3,2,1,0:T(8,128)S(1)}, s32[3,2,8,8]{3,2,1,0:T(8,128)}, u32[]{:S(2)}) copy-start(s32[3,2,8,8]{3,2,1,0:T(8,128)} %shift.7) | copy-start | bytes 4612
  3.0 26.2 %collective-permute-start.4 = (f32[256,1024]{1,0:T(8,128)S(1)}, f32[256,1024]{1,0:T(8,128)S(1)}, u32[]{:S(2)}, u32[]{:S(2)}) collective-permute-start(f32[256,1024]{1,0:T(8,128)S(1)} %get-tuple-element.28), channel_id=1, source_target_pairs={{8,16},{16,8},{9,17},{17,9},{10,18},{18,10},{11,19},{19,11},{12,20... | collective-permute-start | bytes 3145736 | tf_op jit(solution)/shard_map/ppermute | solution.py:26
  6.2 12.0 %collective-permute-start = (s32[3,2,8,8]{3,2,1,0:T(8,128)}, s32[3,2,8,8]{3,2,1,0:T(8,128)S(1)}, u32[]{:S(2)}, u32[]{:S(2)}) collective-permute-start(s32[3,2,8,8]{3,2,1,0:T(8,128)} %shift.7), channel_id=1, source_target_pairs={{0,8},{8,16},{16,24},{1,9},{9,17},{17,25},{2,10},{10,18},{18,26},{... | collective-permute-start | bytes 4616 | tf_op jit(solution)/shard_map/ppermute | solution.py:493
  18.8 8.7 %collective-permute-start.2 = (f32[16,1024]{1,0:T(8,128)S(1)}, f32[16,1024]{1,0:T(8,128)S(1)}, u32[]{:S(2)}, u32[]{:S(2)}) collective-permute-start(f32[16,1024]{1,0:T(8,128)S(1)} %get-tuple-element.25), channel_id=1, source_target_pairs={{0,1},{1,0},{2,3},{3,2},{4,5},{5,4},{6,7},{7,6},{8,9},{9,8},{10,11... | collective-permute-start | bytes 196616 | tf_op jit(solution)/shard_map/ppermute | solution.py:26
  19.2 8.4 %collective-permute-start.3 = (f32[16,1024]{1,0:T(8,128)S(1)}, f32[16,1024]{1,0:T(8,128)S(1)}, u32[]{:S(2)}, u32[]{:S(2)}) collective-permute-start(f32[16,1024]{1,0:T(8,128)S(1)} %get-tuple-element.26), channel_id=1, source_target_pairs={{1,2},{2,1},{3,4},{4,3},{5,6},{6,5},{9,10},{10,9},{11,12},{12,11},... | collective-permute-start | bytes 196616 | tf_op jit(solution)/shard_map/ppermute | solution.py:26
  23.3 4.3 %copy-start.2 = (f32[3,2,64,1024]{3,2,1,0:T(8,128)S(1)}, f32[3,2,64,1024]{3,2,1,0:T(8,128)}, u32[]{:S(2)}) copy-start(f32[3,2,64,1024]{3,2,1,0:T(8,128)} %w.1) | copy-start | bytes 4718596
  30.6 13.5 %collective-permute-start.5 = (f32[256,1024]{1,0:T(8,128)S(1)}, f32[256,1024]{1,0:T(8,128)S(1)}, u32[]{:S(2)}, u32[]{:S(2)}) collective-permute-start(f32[256,1024]{1,0:T(8,128)S(1)} %get-tuple-element.31), channel_id=1, source_target_pairs={{0,8},{8,0},{16,24},{24,16},{1,9},{9,1},{17,25},{25,17},{2,10},{10... | collective-permute-start | bytes 3145736 | tf_op jit(solution)/shard_map/ppermute | solution.py:26
  30.7 17.4 %collective-permute-start.8 = (f32[256,1024]{1,0:T(8,128)S(1)}, f32[256,1024]{1,0:T(8,128)S(1)}, u32[]{:S(2)}, u32[]{:S(2)}) collective-permute-start(f32[256,1024]{1,0:T(8,128)S(1)} %get-tuple-element.36), channel_id=1, source_target_pairs={{8,16},{16,8},{9,17},{17,9},{10,18},{18,10},{11,19},{19,11},{12,20... | collective-permute-start | bytes 3145736 | tf_op jit(solution)/shard_map/ppermute | solution.py:26
  35.6 8.4 %collective-permute-start.6 = (f32[16,1024]{1,0:T(8,128)S(1)}, f32[16,1024]{1,0:T(8,128)S(1)}, u32[]{:S(2)}, u32[]{:S(2)}) collective-permute-start(f32[16,1024]{1,0:T(8,128)S(1)} %get-tuple-element.32), channel_id=1, source_target_pairs={{0,1},{1,0},{2,3},{3,2},{4,5},{5,4},{6,7},{7,6},{8,9},{9,8},{10,11... | collective-permute-start | bytes 196616 | tf_op jit(solution)/shard_map/ppermute | solution.py:26
  35.7 8.3 %collective-permute-start.7 = (f32[16,1024]{1,0:T(8,128)S(1)}, f32[16,1024]{1,0:T(8,128)S(1)}, u32[]{:S(2)}, u32[]{:S(2)}) collective-permute-start(f32[16,1024]{1,0:T(8,128)S(1)} %get-tuple-element.33), channel_id=1, source_target_pairs={{1,2},{2,1},{3,4},{4,3},{5,6},{6,5},{9,10},{10,9},{11,12},{12,11},... | collective-permute-start | bytes 196616 | tf_op jit(solution)/shard_map/ppermute | solution.py:26

commit v3 on v2

--- a/solution.py
+++ b/solution.py
@@ -102,15 +102,32 @@
     return lax.broadcasted_iota(jnp.int32, (rows, width), 1) & (COLS - 1)
 
 
-def put_index(after, shift, before, index):
+def put_tail(shift, out, first, width):
+    sections, _, rbs, _ = shift.shape
+    lane = lanes(rbs, width)
+    parts = [
+        spread(shift[s, h], width)
+        for s, h in ((sections - 1, 0), (sections - 1, 1), (sections - 2, 1))
+    ]
+    mixed = jnp.where(lane == 0, parts[0], jnp.where(lane == 1, parts[1], parts[2]))
+    out[first : first + rbs, :] = mixed.astype(jnp.float32)
+
+
+def put_index(after, shift, arrived, first, index):
     sections, _, rbs, _ = shift.shape
     width = index.shape[2]
     lane = lanes(rbs, width)
-    for j, (own, block, hops) in enumerate(pairs_of(after, sections)):
+    for j, (own, _, hops) in enumerate(pairs_of(after, sections)):
         if after:
             offset = spread(shift[own, hops - 1], width)
         else:
-            offset = -spread(before[sections - 1 - block, hops - 1], width)
+            blocks = per_tile(
+                width,
+                lambda cb: jnp.broadcast_to(
+                    arrived[first : first + rbs, cb * COLS + j : cb * COLS + j + 1], (rbs, COLS)
+                ),
+            )
+            offset = -blocks.astype(jnp.int32)
         index[j, 0:rbs, :] = (lane + offset) & (COLS - 1)
 
 
@@ -157,8 +174,8 @@
         splat[MOVING + s] = jnp.full(tile, jnp.where(fixed[s] == 0, 1.0, 0.0))
 
 
-def lead_kernel(u, slow, fast):
-    sections, _, rows, _ = u.shape
+def lead_kernel(u, shift, slow, fast):
+    sections, _, rows, width = u.shape
 
     def body(after):
         for out, side in ((slow, after), (fast, not after)):
@@ -167,9 +184,12 @@
                     out[(2 * k + c) * rows : (2 * k + c + 1) * rows, :] = u[own, c]
 
     by_side(body)
-
-
-def prepare_kernel(u, cls, before, stiff, cross, fixed, rim_a, rim_b, splat):
+    put_tail(shift, slow, 4 * rows, width)
+    after_blocks = slice(4 * rows, slow.shape[0])
+    fast[after_blocks, :] = slow[after_blocks, :]
+
+
+def prepare_kernel(u, cls, arrived, stiff, cross, fixed, rim_a, rim_b, splat):
     sections, _, rows, _ = u.shape
     last = slice(rows - 1, rows)
     put_splat(stiff, cross, fixed, splat)
@@ -326,7 +346,7 @@
                 total[own, c, rows_of(rb), :] += f[c]
 
 
-def first_rims_kernel(u, w, total_in, half, fast, rim_a, rim_b, shift, before, splat, total, index):
+def first_rims_kernel(u, w, total_in, half, fast, rim_a, rim_b, shift, splat, total, index):
     sections, _, rows, _ = u.shape
 
     def damp(rb, carry):
@@ -339,7 +359,7 @@
     lax.fori_loop(0, rows // ROWS, damp, 0)
 
     def body(after):
-        put_index(not after, shift, before, index)
+        put_index(not after, shift, fast, 4 * rows, index)
         fast_flows(u, not after, fast, index, splat, total, range(3))
 
     by_side(body)
@@ -392,13 +412,13 @@
 
 
 def step_kernel(
-    u, total, arrived, half, shift, before, splat,
+    u, total, arrived, half, shift, splat,
     new_u, new_w, slow, fast, index, rim_a, rim_b,
 ):
     sections, _, rows, width = u.shape
 
     def body(after):
-        put_index(after, shift, before, index)
+        put_index(after, shift, arrived, 4 * rows, index)
         slow_edge = (near_of(after, sections), second_of(after, sections))
         fast_edge = (near_of(not after, sections), second_of(not after, sections))
         for s in range(sections):
@@ -489,16 +509,15 @@
     scalars = [pltpu.SMEM(shift.shape, jnp.int32), pltpu.SemaphoreType.DMA]
     smem = pl.BlockSpec(memory_space=pltpu.SMEM)
 
-    n = lax.axis_size("sec")
-    before = lax.ppermute(shift, "sec", [(i, i + 1) for i in range(n - 1)])
-    slow, fast = call(lead_kernel, [two, two], [u])
+    two_tail = array(4 * rows + index.shape[1], width)
+    slow, fast = call(lead_kernel, [two_tail, two_tail], [u, shift])
     slow = exchange(slow, "sec", "b")
     fast = exchange(fast, "sec", "a")
     rim_a, rim_b, splat = call(
         prepare_kernel,
         [rim, rim, splat],
-        [u, cls, before, stiff, cross, fixed],
-        in_specs=[VMEM] * 3 + [smem] * 3,
+        [u, cls, fast, stiff, cross, fixed],
+        in_specs=[VMEM] * 2 + [ANY] + [smem] * 3,
     )
     rim_a = exchange(rim_a, "strip", "a")
     rim_b = exchange(rim_b, "strip", "b")
@@ -508,13 +527,13 @@
     total, fast_index = call(
         first_rims_kernel,
         [full, index],
-        [u, w, total, half, fast, rim_a, rim_b, shift, before, splat],
+        [u, w, total, half, fast, rim_a, rim_b, shift, splat],
         {2: 0},
     )
     u, w, slow, fast, index, rim_a, rim_b = call(
         step_kernel,
         [full, full, two, two, index, rim, rim],
-        [u, total, slow, half, shift, before, splat],
+        [u, total, slow, half, shift, splat],
     )
     slow = exchange(slow, "sec", "b")
     fast = exchange(fast, "sec", "a")

time: 50.4 us -> 40.5 us (0.80)
  waiting for transfers between devices: 11.7 us -> 4.96 us
  starting transfers between devices: 20.3 us -> 16.1 us
  local copies, waits for them, and re-layouts: 1.43 us -> 2.16 us
    ppermute x1 -> x0, waiting for transfers between devices: 9.48 us -> none  [per_device(): before = lax.ppermute(shift, 'sec', [(i, i + 1) for i in range(n - 1)])]
    ppermute x8, waiting for transfers between devices: 2.22 us -> 4.96 us  [exchange(): return lax.ppermute(value, axis, route)]
    ppermute x1 -> x0, starting transfers between devices: 2.5 us -> none  [per_device(): before = lax.ppermute(shift, 'sec', [(i, i + 1) for i in range(n - 1)])]
    ppermute x8, starting transfers between devices: 17.8 us -> 16.1 us  [exchange(): return lax.ppermute(value, axis, route)]
    unnamed x14, local copies, waits for them, and re-layouts: 1.43 us -> 2.16 us
  transfers between devices with their start and end apart: 9 -> 8, of which waited for: 2 -> 2; matrix products, arithmetic and copies ran while one was open for 0% -> 0% of each run, Pallas kernels for 24% -> 31%
where the time goes in v3:
time: 40.5 us; the launch traced here: 39.8 us
  starting transfers between devices  16.1 us (40%)
  Pallas kernels  15.8 us (39%)
  waiting for transfers between devices  4.96 us (12%)
  local copies, waits for them, and re-layouts  2.16 us (5%)
  between operations  0.83 us (2%)
    ppermute x8, starting transfers between devices, exchange(): return lax.ppermute(value, axis, route)  16.1 us
    pallas_call x8, Pallas kernels, call(): pl.pallas_call(kernel, out_shape=outs, in_specs=in_specs or [VMEM] * len(...  15.8 us
    ppermute x8, waiting for transfers between devices, exchange(): return lax.ppermute(value, axis, route)  4.96 us
    unnamed x14, local copies, waits for them, and re-layouts  2.16 us
  transfers between devices with their start and end apart: 8, of which 2 were waited for; matrix products, arithmetic and copies ran while one was open for 0% of the time, Pallas kernels for 31%

profile of v3, /device:TPU:3, one launch (start us, length us, event | category | flops | bytes accessed | tf_op | source)
XLA Modules:
  0.0 39.8 jit_solution(6735977118176097673)
XLA Ops:
  0.6 0.0 copy-start
  0.6 1.4 %copy-done = f32[3,2,64,1024]{3,2,1,0:T(8,128)S(1)} copy-done((f32[3,2,64,1024]{3,2,1,0:T(8,128)S(1)}, f32[3,2,64,1024]{3,2,1,0:T(8,128)}, u32[]{:S(2)}) %copy-start) | copy-done | bytes 1572888
  2.0 0.0 copy-start.3
  2.0 0.7 %copy-done.3 = s32[3,2,8,8]{3,2,1,0:T(8,128)S(1)} copy-done((s32[3,2,8,8]{3,2,1,0:T(8,128)S(1)}, s32[3,2,8,8]{3,2,1,0:T(8,128)}, u32[]{:S(2)}) %copy-start.3) | copy-done | bytes 1560
  2.8 0.0 copy-start.1
  2.8 0.0 copy-start.4
  2.8 0.0 copy-start.5
  2.8 0.0 copy-start.6
  2.8 0.3 shard_map.86
  3.0 0.7 %collective-permute-start = (f32[264,1024]{1,0:T(8,128)S(1)}, f32[264,1024]{1,0:T(8,128)S(1)}, u32[]{:S(2)}, u32[]{:S(2)}) collective-permute-start(f32[264,1024]{1,0:T(8,128)S(1)} %get-tuple-element.21), channel_id=1, source_target_pairs={{0,8},{8,0},{16,24},{24,16},{1,9},{9,1},{17,25},{25,17},{2,10},{10... | collective-permute-start | bytes 3244040 | tf_op jit(solution)/shard_map/ppermute | solution.py:26
  3.8 3.2 %collective-permute-start.3 = (f32[264,1024]{1,0:T(8,128)S(1)}, f32[264,1024]{1,0:T(8,128)S(1)}, u32[]{:S(2)}, u32[]{:S(2)}) collective-permute-start(f32[264,1024]{1,0:T(8,128)S(1)} %get-tuple-element.28), channel_id=1, source_target_pairs={{8,16},{16,8},{9,17},{17,9},{10,18},{18,10},{11,19},{19,11},{12,20... | collective-permute-start | bytes 3244040 | tf_op jit(solution)/shard_map/ppermute | solution.py:26
  7.0 0.0 collective-permute-done.arrived.fast
  7.0 0.0 copy-done.1
  7.0 0.0 copy-done.4
  7.0 0.0 copy-done.5
  7.0 0.0 copy-done.6
  7.0 0.7 %shard_map.87 = (f32[16,1024]{1,0:T(8,128)S(1)}, f32[16,1024]{1,0:T(8,128)S(1)}, f32[10,8,128]{2,1,0:T(8,128)S(1)}) custom-call(f32[3,2,64,1024]{3,2,1,0:T(8,128)S(1)} %copy-done, s32[3,2,64,1024]{3,2,1,0:T(8,128)S(1)} %copy-done.1, f32[264,1024]{1,0:T(8,128)S(1)} %collective-permute-done.arrived.fast, f32[8]{0:T(128)S(1)} %copy-done.4, f32[2]{0:T(128)S(1)} %copy-done.5, ...), custom_call_target="tpu_custom_call" | custom-call | tf_op jit(solution)/shard_map/pallas_call | solution.py:486
  7.7 0.3 collective-permute-start.1
  8.0 4.1 %collective-permute-start.2 = (f32[16,1024]{1,0:T(8,128)S(1)}, f32[16,1024]{1,0:T(8,128)S(1)}, u32[]{:S(2)}, u32[]{:S(2)}) collective-permute-start(f32[16,1024]{1,0:T(8,128)S(1)} %get-tuple-element.26), channel_id=1, source_target_pairs={{1,2},{2,1},{3,4},{4,3},{5,6},{6,5},{9,10},{10,9},{11,12},{12,11},... | collective-permute-start | bytes 196616 | tf_op jit(solution)/shard_map/ppermute | solution.py:26
  12.2 0.0 copy-start.2
  12.2 4.2 %shard_map.88 = (f32[3,2,64,1024]{3,2,1,0:T(8,128)S(1)}, f32[3,2,64,1024]{3,2,1,0:T(8,128)S(1)}) custom-call(f32[3,2,64,1024]{3,2,1,0:T(8,128)S(1)} %copy-done, s32[3,2,64,1024]{3,2,1,0:T(8,128)S(1)} %copy-done.1, s32[3,2,8,8]{3,2,1,0:T(8,128)S(1)} %copy-done.3, f32[10,8,128]{2,1,0:T(8,128)S(1)} %get-tuple-element.22.splat), custom_call_target="tpu_custom_call" | custom-call | tf_op jit(solution)/shard_map/pallas_call | solution.py:486
  16.4 0.0 collective-permute-done.1.rim_a
  16.4 0.0 collective-permute-done.2.rim_b
  16.4 0.0 copy-done.2
  16.4 1.5 %shard_map.89 = (f32[3,2,64,1024]{3,2,1,0:T(8,128)S(1)}, s32[3,8,1024]{2,1,0:T(8,128)S(1)}) custom-call(f32[3,2,64,1024]{3,2,1,0:T(8,128)S(1)} %copy-done, f32[3,2,64,1024]{3,2,1,0:T(8,128)S(1)} %copy-done.2, f32[3,2,64,1024]{3,2,1,0:T(8,128)S(1)} %get-tuple-element.23.total_in, ...), custom_call_target="tpu_custom_call", output_to_operand_aliasing={{0}: (2, {})} | custom-call | tf_op jit(solution)/shard_map/pallas_call | solution.py:486
  17.9 2.3 %collective-permute-done.3.arrived = f32[264,1024]{1,0:T(8,128)S(1)} collective-permute-done((f32[264,1024]{1,0:T(8,128)S(1)}, f32[264,1024]{1,0:T(8,128)S(1)}, u32[]{:S(2)}, u32[]{:S(2)}) %collective-permute-start.3) | collective-permute-done | bytes 1081376 | tf_op jit(solution)/shard_map/ppermute | solution.py:26
  20.2 1.3 %shard_map.90 = (f32[3,2,64,1024]{3,2,1,0:T(8,128)S(1)}, f32[3,2,64,1024]{3,2,1,0:T(8,128)S(1)}, f32[256,1024]{1,0:T(8,128)S(1)}, f32[256,1024]{1,0:T(8,128)S(1)...) custom-call(f32[3,2,64,1024]{3,2,1,0:T(8,128)S(1)} %copy-done, ...), custom_call_target="tpu_custom_call" | custom-call | tf_op jit(solution)/shard_map/pallas_call | solution.py:486
  21.6 0.1 collective-permute-start.4
  21.7 3.2 %collective-permute-start.7 = (f32[256,1024]{1,0:T(8,128)S(1)}, f32[256,1024]{1,0:T(8,128)S(1)}, u32[]{:S(2)}, u32[]{:S(2)}) collective-permute-start(f32[256,1024]{1,0:T(8,128)S(1)} %get-tuple-element.36), channel_id=1, source_target_pairs={{8,16},{16,8},{9,17},{17,9},{10,18},{18,10},{11,19},{19,11},{12,20... | collective-permute-start | bytes 3145736 | tf_op jit(solution)/shard_map/ppermute | solution.py:26
  24.9 0.3 collective-permute-start.5
  25.2 4.1 %collective-permute-start.6 = (f32[16,1024]{1,0:T(8,128)S(1)}, f32[16,1024]{1,0:T(8,128)S(1)}, u32[]{:S(2)}, u32[]{:S(2)}) collective-permute-start(f32[16,1024]{1,0:T(8,128)S(1)} %get-tuple-element.33), channel_id=1, source_target_pairs={{1,2},{2,1},{3,4},{4,3},{5,6},{6,5},{9,10},{10,9},{11,12},{12,11},... | collective-permute-start | bytes 196616 | tf_op jit(solution)/shard_map/ppermute | solution.py:26
  29.3 3.9 %shard_map.91.total_in = f32[3,2,64,1024]{3,2,1,0:T(8,128)S(1)} custom-call(f32[3,2,64,1024]{3,2,1,0:T(8,128)S(1)} %get-tuple-element.29.u, f32[3,2,64,1024]{3,2,1,0:T(8,128)S(1)} %get-tuple-element.30.w, f32[3,2,64,1024]{3,2,1,0:T(8,128)S(1)} %get-tuple-element.24.half, s32[3,2,8,8]{3,2,1,0:T(8,128)S(1)} %copy-done.3, f32[10,8,128]{2,1,0:T(8,128)S(1)} %get-tuple-element.22.splat), custom_call_target="tpu_custom_call" | custom-call | tf_op jit(solution)/shard_map/pallas_call | solution.py:486
  33.3 0.0 collective-permute-done.5.rim_a
  33.3 0.0 collective-permute-done.6.rim_b
  33.3 0.0 collective-permute-done.4.fast
  33.3 1.9 %shard_map.92 = (f32[3,2,64,1024]{3,2,1,0:T(8,128)S(1)}, f32[3,2,64,1024]{3,2,1,0:T(8,128)}, f32[3,2,64,1024]{3,2,1,0:T(8,128)}) custom-call(f32[3,2,64,1024]{3,2,1,0:T(8,128)S(1)} %get-tuple-element.29.u, f32[3,2,64,1024]{3,2,1,0:T(8,128)S(1)} %shard_map.91.total_in, ...), custom_call_target="tpu_custom_call", output_to_operand_aliasing={{0}: (1, {})} | custom-call | tf_op jit(solution)/shard_map/pallas_call | solution.py:486
  35.2 2.6 %collective-permute-done.7.arrived = f32[256,1024]{1,0:T(8,128)S(1)} collective-permute-done((f32[256,1024]{1,0:T(8,128)S(1)}, f32[256,1024]{1,0:T(8,128)S(1)}, u32[]{:S(2)}, u32[]{:S(2)}) %collective-permute-start.7) | collective-permute-done | bytes 1048608 | tf_op jit(solution)/shard_map/ppermute | solution.py:26
  37.8 2.1 %shard_map.93 = (f32[3,2,64,1024]{3,2,1,0:T(8,128)}, f32[3,2,64,1024]{3,2,1,0:T(8,128)}) custom-call(f32[3,2,64,1024]{3,2,1,0:T(8,128)S(1)} %get-tuple-element.29.u, f32[3,2,64,1024]{3,2,1,0:T(8,128)S(1)} %get-tuple-element.35.total, f32[256,1024]{1,0:T(8,128)S(1)} %collective-permute-done.7.arrived, ...), custom_call_target="tpu_custom_call", output_to_operand_aliasing={{0}: (5, {}), {1}: (6, {})} | custom-call | tf_op jit(solution)/shard_map/pallas_call | solution.py:486
Async XLA Ops:
  0.6 1.4 %copy-start = (f32[3,2,64,1024]{3,2,1,0:T(8,128)S(1)}, f32[3,2,64,1024]{3,2,1,0:T(8,128)}, u32[]{:S(2)}) copy-start(f32[3,2,64,1024]{3,2,1,0:T(8,128)} %u.9) | copy-start | bytes 4718596
  2.0 0.7 %copy-start.3 = (s32[3,2,8,8]{3,2,1,0:T(8,128)S(1)}, s32[3,2,8,8]{3,2,1,0:T(8,128)}, u32[]{:S(2)}) copy-start(s32[3,2,8,8]{3,2,1,0:T(8,128)} %shift.9) | copy-start | bytes 4612
  2.8 4.2 %copy-start.1 = (s32[3,2,64,1024]{3,2,1,0:T(8,128)S(1)}, s32[3,2,64,1024]{3,2,1,0:T(8,128)}, u32[]{:S(2)}) copy-start(s32[3,2,64,1024]{3,2,1,0:T(8,128)} %cls.3) | copy-start | bytes 4718596
  2.8 4.2 %copy-start.4 = (f32[8]{0:T(128)S(1)}, f32[8]{0:T(128)}, u32[]{:S(2)}) copy-start(f32[8]{0:T(128)} %stiff.1) | copy-start | bytes 100
  2.8 4.2 %copy-start.5 = (f32[2]{0:T(128)S(1)}, f32[2]{0:T(128)}, u32[]{:S(2)}) copy-start(f32[2]{0:T(128)} %cross.1) | copy-start | bytes 28
  2.8 4.2 %copy-start.6 = (s32[3]{0:T(128)S(1)}, s32[3]{0:T(128)}, u32[]{:S(2)}) copy-start(s32[3]{0:T(128)} %fixed.1) | copy-start | bytes 40
  3.0 3.9 %collective-permute-start = (f32[264,1024]{1,0:T(8,128)S(1)}, f32[264,1024]{1,0:T(8,128)S(1)}, u32[]{:S(2)}, u32[]{:S(2)}) collective-permute-start(f32[264,1024]{1,0:T(8,128)S(1)} %get-tuple-element.21), channel_id=1, source_target_pairs={{0,8},{8,0},{16,24},{24,16},{1,9},{9,1},{17,25},{25,17},{2,10},{10... | collective-permute-start | bytes 3244040 | tf_op jit(solution)/shard_map/ppermute | solution.py:26
  3.8 16.5 %collective-permute-start.3 = (f32[264,1024]{1,0:T(8,128)S(1)}, f32[264,1024]{1,0:T(8,128)S(1)}, u32[]{:S(2)}, u32[]{:S(2)}) collective-permute-start(f32[264,1024]{1,0:T(8,128)S(1)} %get-tuple-element.28), channel_id=1, source_target_pairs={{8,16},{16,8},{9,17},{17,9},{10,18},{18,10},{11,19},{19,11},{12,20... | collective-permute-start | bytes 3244040 | tf_op jit(solution)/shard_map/ppermute | solution.py:26
  7.7 8.6 %collective-permute-start.1 = (f32[16,1024]{1,0:T(8,128)S(1)}, f32[16,1024]{1,0:T(8,128)S(1)}, u32[]{:S(2)}, u32[]{:S(2)}) collective-permute-start(f32[16,1024]{1,0:T(8,128)S(1)} %get-tuple-element.25), channel_id=1, source_target_pairs={{0,1},{1,0},{2,3},{3,2},{4,5},{5,4},{6,7},{7,6},{8,9},{9,8},{10,11... | collective-permute-start | bytes 196616 | tf_op jit(solution)/shard_map/ppermute | solution.py:26
  8.0 8.3 %collective-permute-start.2 = (f32[16,1024]{1,0:T(8,128)S(1)}, f32[16,1024]{1,0:T(8,128)S(1)}, u32[]{:S(2)}, u32[]{:S(2)}) collective-permute-start(f32[16,1024]{1,0:T(8,128)S(1)} %get-tuple-element.26), channel_id=1, source_target_pairs={{1,2},{2,1},{3,4},{4,3},{5,6},{6,5},{9,10},{10,9},{11,12},{12,11},... | collective-permute-start | bytes 196616 | tf_op jit(solution)/shard_map/ppermute | solution.py:26
  12.2 4.2 %copy-start.2 = (f32[3,2,64,1024]{3,2,1,0:T(8,128)S(1)}, f32[3,2,64,1024]{3,2,1,0:T(8,128)}, u32[]{:S(2)}) copy-start(f32[3,2,64,1024]{3,2,1,0:T(8,128)} %w.1) | copy-start | bytes 4718596
  21.6 11.7 %collective-permute-start.4 = (f32[256,1024]{1,0:T(8,128)S(1)}, f32[256,1024]{1,0:T(8,128)S(1)}, u32[]{:S(2)}, u32[]{:S(2)}) collective-permute-start(f32[256,1024]{1,0:T(8,128)S(1)} %get-tuple-element.31), channel_id=1, source_target_pairs={{0,8},{8,0},{16,24},{24,16},{1,9},{9,1},{17,25},{25,17},{2,10},{10... | collective-permute-start | bytes 3145736 | tf_op jit(solution)/shard_map/ppermute | solution.py:26
  21.7 16.1 %collective-permute-start.7 = (f32[256,1024]{1,0:T(8,128)S(1)}, f32[256,1024]{1,0:T(8,128)S(1)}, u32[]{:S(2)}, u32[]{:S(2)}) collective-permute-start(f32[256,1024]{1,0:T(8,128)S(1)} %get-tuple-element.36), channel_id=1, source_target_pairs={{8,16},{16,8},{9,17},{17,9},{10,18},{18,10},{11,19},{19,11},{12,20... | collective-permute-start | bytes 3145736 | tf_op jit(solution)/shard_map/ppermute | solution.py:26
  24.9 8.4 %collective-permute-start.5 = (f32[16,1024]{1,0:T(8,128)S(1)}, f32[16,1024]{1,0:T(8,128)S(1)}, u32[]{:S(2)}, u32[]{:S(2)}) collective-permute-start(f32[16,1024]{1,0:T(8,128)S(1)} %get-tuple-element.32), channel_id=1, source_target_pairs={{0,1},{1,0},{2,3},{3,2},{4,5},{5,4},{6,7},{7,6},{8,9},{9,8},{10,11... | collective-permute-start | bytes 196616 | tf_op jit(solution)/shard_map/ppermute | solution.py:26
  25.2 8.1 %collective-permute-start.6 = (f32[16,1024]{1,0:T(8,128)S(1)}, f32[16,1024]{1,0:T(8,128)S(1)}, u32[]{:S(2)}, u32[]{:S(2)}) collective-permute-start(f32[16,1024]{1,0:T(8,128)S(1)} %get-tuple-element.33), channel_id=1, source_target_pairs={{1,2},{2,1},{3,4},{4,3},{5,6},{6,5},{9,10},{10,9},{11,12},{12,11},... | collective-permute-start | bytes 196616 | tf_op jit(solution)/shard_map/ppermute | solution.py:26

commit v4 on v3

--- a/solution.py
+++ b/solution.py
@@ -1,3 +1,5 @@
+import functools
+
 import jax
 import jax.numpy as jnp
 from jax import lax
@@ -300,12 +302,12 @@
     inside(u, w, total, half_across, half_below, shift, splat, scalars, sem)
 
 
-def side_flow(u, own, arrived, first, index, j, half, rb):
-    rows = u.shape[2]
+def side_flow(u, own, arrived, block, height, base, index, j, half, rb):
     at = rows_of(rb)
     number = index[j, rb : rb + 1, :]
     e = [
-        gathered(arrived[pl.ds(first + c * rows + rb * ROWS, ROWS), :], number) - u[own, c, at, :]
+        gathered(arrived[pl.ds((2 * block + c) * height + rb * ROWS - base, ROWS), :], number)
+        - u[own, c, at, :]
         for c in range(2)
     ]
     return flow(e[0], e[1], half)
@@ -341,7 +343,7 @@
         own, block, hops = pairs_of(after, sections)[j]
         stiff = wide_splat(splat, FAST + hops - 1, width)
         for rb in range(rows // ROWS):
-            f = side_flow(u, own, fast, 2 * block * rows, index, j, stiff, rb)
+            f = side_flow(u, own, fast, block, rows, 0, index, j, stiff, rb)
             for c in range(2):
                 total[own, c, rows_of(rb), :] += f[c]
 
@@ -399,23 +401,24 @@
     by_side(body)
 
 
-def slow_values(u, after, arrived, index, splat, total, j, rb):
+def slow_values(u, after, arrived, height, base, index, splat, total, j, rb):
     sections, _, rows, width = u.shape
     own = pairs_of(after, sections)[j][0]
     value = [total[own, c, rows_of(rb), :] for c in range(2)]
     for p, (section, block, hops) in enumerate(pairs_of(after, sections)):
         if section == own:
             stiff = wide_splat(splat, SLOW + hops - 1, width)
-            f = side_flow(u, own, arrived, 2 * block * rows, index, p, stiff, rb)
+            f = side_flow(u, own, arrived, block, height, base, index, p, stiff, rb)
             value = [value[c] + f[c] for c in range(2)]
     return value
 
 
 def step_kernel(
     u, total, arrived, half, shift, splat,
-    new_u, new_w, slow, fast, index, rim_a, rim_b,
+    new_u, new_w, slow_top, slow_rest, fast, index, rim_a, rim_b,
 ):
     sections, _, rows, width = u.shape
+    top = slow_top.shape[0] // 4
 
     def body(after):
         put_index(after, shift, arrived, 4 * rows, index)
@@ -424,9 +427,11 @@
         for s in range(sections):
             moving = wide_splat(splat, MOVING + s, width)
             for rb in range(rows // ROWS):
-                at = rows_of(rb)
+                at, row = rows_of(rb), rb * ROWS
                 if s in slow_edge:
-                    value = slow_values(u, after, arrived, index, splat, total, slow_edge.index(s), rb)
+                    value = slow_values(
+                        u, after, arrived, rows, 0, index, splat, total, slow_edge.index(s), rb
+                    )
                 else:
                     value = [total[s, c, at, :] for c in range(2)]
                 for c in range(2):
@@ -434,10 +439,14 @@
                     moved = u[s, c, at, :] + STEP * v
                     new_w[s, c, at, :] = v
                     new_u[s, c, at, :] = moved
-                    for edge, out in ((slow_edge, slow), (fast_edge, fast)):
-                        if s in edge:
-                            first = (2 * edge.index(s) + c) * rows
-                            out[pl.ds(first + rb * ROWS, ROWS), :] = moved
+                    if s in fast_edge:
+                        fast[pl.ds((2 * fast_edge.index(s) + c) * rows + row, ROWS), :] = moved
+                    if s in slow_edge:
+                        k = 2 * slow_edge.index(s) + c
+                        if row < top:
+                            slow_top[pl.ds(k * top + row, ROWS), :] = moved
+                        else:
+                            slow_rest[pl.ds(k * (rows - top) + row - top, ROWS), :] = moved
 
     by_side(body)
     last = slice(rows - 1, rows)
@@ -451,9 +460,12 @@
     )
 
 
-def last_kernel(u, total, arrived, index, splat, out_u_in, out_w_in, out_u, out_w, new_u, new_w, sem):
-    sections, _, rows, width = u.shape
-    rbs = rows // ROWS
+def last_kernel(
+    base, u, total, arrived, index, splat, out_u_in, out_w_in, out_u, out_w, new_u, new_w, sem
+):
+    sections, _, rows, width = u.shape
+    height = arrived.shape[0] // 4
+    rbs = height // ROWS
     part = rbs // 2 if rbs % 2 == 0 else rbs
 
     def body(after):
@@ -461,18 +473,19 @@
         for j in range(2):
             own = pairs_of(after, sections)[j][0]
             moving = wide_splat(splat, MOVING + own, width)
-            for rb in range(rbs):
-                at = rows_of(rb)
-                value = slow_values(u, after, arrived, index, splat, total, j, rb)
+            for k in range(rbs):
+                rb = base // ROWS + k
+                value = slow_values(u, after, arrived, height, base, index, splat, total, j, rb)
                 for c in range(2):
                     v = value[c] * moving
-                    new_w[j, c, at, :] = v
-                    new_u[j, c, at, :] = u[own, c, at, :] + STEP * v
-                if (rb + 1) % part == 0:
-                    block = pl.ds((rb + 1 - part) * ROWS, part * ROWS)
+                    new_w[j, c, rows_of(k), :] = v
+                    new_u[j, c, rows_of(k), :] = u[own, c, rows_of(rb), :] + STEP * v
+                if (k + 1) % part == 0:
+                    here = pl.ds((k + 1 - part) * ROWS, part * ROWS)
+                    there = pl.ds(base + (k + 1 - part) * ROWS, part * ROWS)
                     for source, target in ((new_u, out_u), (new_w, out_w)):
                         copy = pltpu.make_async_copy(
-                            source.at[j, :, block], target.at[own, :, block], sem.at[len(copies)]
+                            source.at[j, :, here], target.at[own, :, there], sem.at[len(copies)]
                         )
                         copy.start()
                         copies.append(copy)
@@ -530,12 +543,14 @@
         [u, w, total, half, fast, rim_a, rim_b, shift, splat],
         {2: 0},
     )
-    u, w, slow, fast, index, rim_a, rim_b = call(
+    top = max(rows // ROWS * 3 // 4, 1) * ROWS
+    u, w, slow_top, slow_rest, fast, index, rim_a, rim_b = call(
         step_kernel,
-        [full, full, two, two, index, rim, rim],
+        [full, full, array(4 * top, width), array(4 * (rows - top), width), two, index, rim, rim],
         [u, total, slow, half, shift, splat],
     )
-    slow = exchange(slow, "sec", "b")
+    slow_top = exchange(slow_top, "sec", "b")
+    slow_rest = exchange(slow_rest, "sec", "b")
     fast = exchange(fast, "sec", "a")
     rim_a = exchange(rim_a, "strip", "a")
     rim_b = exchange(rim_b, "strip", "b")
@@ -550,18 +565,19 @@
         + [pltpu.SemaphoreType.DMA((2 * done,))],
         out_specs=[VMEM, ANY, ANY],
     )
-    return tuple(
-        call(
-            last_kernel,
+    for base, arrived in ((0, slow_top), (top, slow_rest)):
+        height = arrived.shape[0] // 4
+        out_u, out_w = call(
+            functools.partial(last_kernel, base),
             [full, full],
-            [u, total, slow, index, splat, out_u, out_w],
+            [u, total, arrived, index, splat, out_u, out_w],
             {5: 0, 6: 1},
-            scratch=[pltpu.VMEM((2, 2, rows, width), jnp.float32)] * 2
+            scratch=[pltpu.VMEM((2, 2, height, width), jnp.float32)] * 2
             + [pltpu.SemaphoreType.DMA((8,))],
             in_specs=[VMEM] * 5 + [ANY] * 2,
             out_specs=[ANY] * 2,
         )
-    )
+    return out_u, out_w
 
 
 def solution(mesh):

time: 40.5 us -> 41 us (1.012)
  waiting for transfers between devices: 4.96 us -> 2.33 us
  starting transfers between devices: 16.1 us -> 18.4 us
  Pallas kernels: 15.8 us -> 16.6 us
    ppermute x8 -> x9, waiting for transfers between devices: 4.96 us -> 2.33 us  [exchange(): return lax.ppermute(value, axis, route)]
    ppermute x8 -> x9, starting transfers between devices: 16.1 us -> 18.4 us  [exchange(): return lax.ppermute(value, axis, route)]
    pallas_call x8 -> x9, Pallas kernels: 15.8 us -> 16.6 us  [call(): pl.pallas_call(kernel, out_shape=outs, in_specs=in_specs or [VMEM] * len(...]
  transfers between devices with their start and end apart: 8 -> 9, of which waited for: 2 -> 1; matrix products, arithmetic and copies ran while one was open for 0% -> 0% of each run, Pallas kernels for 31% -> 35%
where the time goes in v4:
time: 41 us; the launch traced here: 40.4 us
  starting transfers between devices  18.4 us (45%)
  Pallas kernels  16.6 us (40%)
  waiting for transfers between devices  2.33 us (6%)
  local copies, waits for them, and re-layouts  2.16 us (5%)
  between operations  0.87 us (2%)
    ppermute x9, starting transfers between devices, exchange(): return lax.ppermute(value, axis, route)  18.4 us
    pallas_call x9, Pallas kernels, call(): pl.pallas_call(kernel, out_shape=outs, in_specs=in_specs or [VMEM] * len(...  16.6 us
    ppermute x9, waiting for transfers between devices, exchange(): return lax.ppermute(value, axis, route)  2.33 us
    unnamed x14, local copies, waits for them, and re-layouts  2.16 us
  transfers between devices with their start and end apart: 9, of which 1 were waited for; matrix products, arithmetic and copies ran while one was open for 0% of the time, Pallas kernels for 35%

profile of v4, /device:TPU:3, one launch (start us, length us, event | category | flops | bytes accessed | tf_op | source)
XLA Modules:
  0.0 40.4 jit_solution(7842431593997787158)
XLA Ops:
  0.6 0.0 copy-start
  0.6 1.4 %copy-done = f32[3,2,64,1024]{3,2,1,0:T(8,128)S(1)} copy-done((f32[3,2,64,1024]{3,2,1,0:T(8,128)S(1)}, f32[3,2,64,1024]{3,2,1,0:T(8,128)}, u32[]{:S(2)}) %copy-start) | copy-done | bytes 1572888
  2.0 0.0 copy-start.3
  2.0 0.7 %copy-done.3 = s32[3,2,8,8]{3,2,1,0:T(8,128)S(1)} copy-done((s32[3,2,8,8]{3,2,1,0:T(8,128)S(1)}, s32[3,2,8,8]{3,2,1,0:T(8,128)}, u32[]{:S(2)}) %copy-start.3) | copy-done | bytes 1560
  2.8 0.0 copy-start.1
  2.8 0.0 copy-start.4
  2.8 0.0 copy-start.5
  2.8 0.0 copy-start.6
  2.8 0.3 shard_map.86
  3.0 0.7 %collective-permute-start = (f32[264,1024]{1,0:T(8,128)S(1)}, f32[264,1024]{1,0:T(8,128)S(1)}, u32[]{:S(2)}, u32[]{:S(2)}) collective-permute-start(f32[264,1024]{1,0:T(8,128)S(1)} %get-tuple-element.24), channel_id=1, source_target_pairs={{0,8},{8,0},{16,24},{24,16},{1,9},{9,1},{17,25},{25,17},{2,10},{10... | collective-permute-start | bytes 3244040 | tf_op jit(solution)/shard_map/ppermute | solution.py:28
  3.8 3.2 %collective-permute-start.3 = (f32[264,1024]{1,0:T(8,128)S(1)}, f32[264,1024]{1,0:T(8,128)S(1)}, u32[]{:S(2)}, u32[]{:S(2)}) collective-permute-start(f32[264,1024]{1,0:T(8,128)S(1)} %get-tuple-element.31), channel_id=1, source_target_pairs={{8,16},{16,8},{9,17},{17,9},{10,18},{18,10},{11,19},{19,11},{12,20... | collective-permute-start | bytes 3244040 | tf_op jit(solution)/shard_map/ppermute | solution.py:28
  7.0 0.0 collective-permute-done.arrived.fast
  7.0 0.0 copy-done.1
  7.0 0.0 copy-done.4
  7.0 0.0 copy-done.5
  7.0 0.0 copy-done.6
  7.0 0.7 %shard_map.87 = (f32[16,1024]{1,0:T(8,128)S(1)}, f32[16,1024]{1,0:T(8,128)S(1)}, f32[10,8,128]{2,1,0:T(8,128)S(1)}) custom-call(f32[3,2,64,1024]{3,2,1,0:T(8,128)S(1)} %copy-done, s32[3,2,64,1024]{3,2,1,0:T(8,128)S(1)} %copy-done.1, f32[264,1024]{1,0:T(8,128)S(1)} %collective-permute-done.arrived.fast, f32[8]{0:T(128)S(1)} %copy-done.4, f32[2]{0:T(128)S(1)} %copy-done.5, ...), custom_call_target="tpu_custom_call" | custom-call | tf_op jit(solution)/shard_map/pallas_call | solution.py:499
  7.7 0.3 collective-permute-start.1
  8.0 4.1 %collective-permute-start.2 = (f32[16,1024]{1,0:T(8,128)S(1)}, f32[16,1024]{1,0:T(8,128)S(1)}, u32[]{:S(2)}, u32[]{:S(2)}) collective-permute-start(f32[16,1024]{1,0:T(8,128)S(1)} %get-tuple-element.29), channel_id=1, source_target_pairs={{1,2},{2,1},{3,4},{4,3},{5,6},{6,5},{9,10},{10,9},{11,12},{12,11},... | collective-permute-start | bytes 196616 | tf_op jit(solution)/shard_map/ppermute | solution.py:28
  12.2 0.0 copy-start.2
  12.2 4.2 %shard_map.88 = (f32[3,2,64,1024]{3,2,1,0:T(8,128)S(1)}, f32[3,2,64,1024]{3,2,1,0:T(8,128)S(1)}) custom-call(f32[3,2,64,1024]{3,2,1,0:T(8,128)S(1)} %copy-done, s32[3,2,64,1024]{3,2,1,0:T(8,128)S(1)} %copy-done.1, s32[3,2,8,8]{3,2,1,0:T(8,128)S(1)} %copy-done.3, f32[10,8,128]{2,1,0:T(8,128)S(1)} %get-tuple-element.25.splat), custom_call_target="tpu_custom_call" | custom-call | tf_op jit(solution)/shard_map/pallas_call | solution.py:499
  16.4 0.0 collective-permute-done.1.rim_a
  16.4 0.0 collective-permute-done.2.rim_b
  16.4 0.0 copy-done.2
  16.4 1.5 %shard_map.89 = (f32[3,2,64,1024]{3,2,1,0:T(8,128)S(1)}, s32[3,8,1024]{2,1,0:T(8,128)S(1)}) custom-call(f32[3,2,64,1024]{3,2,1,0:T(8,128)S(1)} %copy-done, f32[3,2,64,1024]{3,2,1,0:T(8,128)S(1)} %copy-done.2, f32[3,2,64,1024]{3,2,1,0:T(8,128)S(1)} %get-tuple-element.26.total_in, ...), custom_call_target="tpu_custom_call", output_to_operand_aliasing={{0}: (2, {})} | custom-call | tf_op jit(solution)/shard_map/pallas_call | solution.py:499
  17.9 2.3 %collective-permute-done.3.arrived = f32[264,1024]{1,0:T(8,128)S(1)} collective-permute-done((f32[264,1024]{1,0:T(8,128)S(1)}, f32[264,1024]{1,0:T(8,128)S(1)}, u32[]{:S(2)}, u32[]{:S(2)}) %collective-permute-start.3) | collective-permute-done | bytes 1081376 | tf_op jit(solution)/shard_map/ppermute | solution.py:28
  20.2 1.3 %shard_map.90 = (f32[3,2,64,1024]{3,2,1,0:T(8,128)S(1)}, f32[3,2,64,1024]{3,2,1,0:T(8,128)S(1)}, f32[192,1024]{1,0:T(8,128)S(1)}, f32[64,1024]{1,0:T(8,128)S(1)}...) custom-call(f32[3,2,64,1024]{3,2,1,0:T(8,128)S(1)} %copy-done, ...), custom_call_target="tpu_custom_call" | custom-call | tf_op jit(solution)/shard_map/pallas_call | solution.py:499
  21.6 0.1 collective-permute-start.4
  21.7 3.2 %collective-permute-start.8 = (f32[192,1024]{1,0:T(8,128)S(1)}, f32[192,1024]{1,0:T(8,128)S(1)}, u32[]{:S(2)}, u32[]{:S(2)}) collective-permute-start(f32[192,1024]{1,0:T(8,128)S(1)} %get-tuple-element.41), channel_id=1, source_target_pairs={{8,16},{16,8},{9,17},{17,9},{10,18},{18,10},{11,19},{19,11},{12,20... | collective-permute-start | bytes 2359304 | tf_op jit(solution)/shard_map/ppermute | solution.py:28
  24.9 2.4 %collective-permute-start.7 = (f32[64,1024]{1,0:T(8,128)S(1)}, f32[64,1024]{1,0:T(8,128)S(1)}, u32[]{:S(2)}, u32[]{:S(2)}) collective-permute-start(f32[64,1024]{1,0:T(8,128)S(1)} %get-tuple-element.39), channel_id=1, source_target_pairs={{8,16},{16,8},{9,17},{17,9},{10,18},{18,10},{11,19},{19,11},{12,20... | collective-permute-start | bytes 786440 | tf_op jit(solution)/shard_map/ppermute | solution.py:28
  27.3 0.1 collective-permute-start.5
  27.3 4.4 %collective-permute-start.6 = (f32[16,1024]{1,0:T(8,128)S(1)}, f32[16,1024]{1,0:T(8,128)S(1)}, u32[]{:S(2)}, u32[]{:S(2)}) collective-permute-start(f32[16,1024]{1,0:T(8,128)S(1)} %get-tuple-element.36), channel_id=1, source_target_pairs={{1,2},{2,1},{3,4},{4,3},{5,6},{6,5},{9,10},{10,9},{11,12},{12,11},... | collective-permute-start | bytes 196616 | tf_op jit(solution)/shard_map/ppermute | solution.py:28
  31.7 3.9 %shard_map.91.total_in = f32[3,2,64,1024]{3,2,1,0:T(8,128)S(1)} custom-call(f32[3,2,64,1024]{3,2,1,0:T(8,128)S(1)} %get-tuple-element.32.u, f32[3,2,64,1024]{3,2,1,0:T(8,128)S(1)} %get-tuple-element.33.w, f32[3,2,64,1024]{3,2,1,0:T(8,128)S(1)} %get-tuple-element.27.half, s32[3,2,8,8]{3,2,1,0:T(8,128)S(1)} %copy-done.3, f32[10,8,128]{2,1,0:T(8,128)S(1)} %get-tuple-element.25.splat), custom_call_target="tpu_custom_call" | custom-call | tf_op jit(solution)/shard_map/pallas_call | solution.py:499
  35.6 0.0 collective-permute-done.5.rim_a
  35.7 0.0 collective-permute-done.6.rim_b
  35.7 0.0 collective-permute-done.4.fast
  35.7 1.9 %shard_map.92 = (f32[3,2,64,1024]{3,2,1,0:T(8,128)S(1)}, f32[3,2,64,1024]{3,2,1,0:T(8,128)}, f32[3,2,64,1024]{3,2,1,0:T(8,128)}) custom-call(f32[3,2,64,1024]{3,2,1,0:T(8,128)S(1)} %get-tuple-element.32.u, f32[3,2,64,1024]{3,2,1,0:T(8,128)S(1)} %shard_map.91.total_in, ...), custom_call_target="tpu_custom_call", output_to_operand_aliasing={{0}: (1, {})} | custom-call | tf_op jit(solution)/shard_map/pallas_call | solution.py:499
  37.5 0.0 collective-permute-done.8.arrived
  37.6 1.7 %shard_map.93 = (f32[3,2,64,1024]{3,2,1,0:T(8,128)}, f32[3,2,64,1024]{3,2,1,0:T(8,128)}) custom-call(f32[3,2,64,1024]{3,2,1,0:T(8,128)S(1)} %get-tuple-element.32.u, f32[3,2,64,1024]{3,2,1,0:T(8,128)S(1)} %get-tuple-element.38.total, f32[192,1024]{1,0:T(8,128)S(1)} %collective-permute-done.8.arrived, ...), custom_call_target="tpu_custom_call", output_to_operand_aliasing={{0}: (5, {}), {1}: (6, {})} | custom-call | tf_op jit(solution)/shard_map/pallas_call | solution.py:499
  39.3 0.0 collective-permute-done.7.arrived
  39.3 1.1 %shard_map.94 = (f32[3,2,64,1024]{3,2,1,0:T(8,128)}, f32[3,2,64,1024]{3,2,1,0:T(8,128)}) custom-call(f32[3,2,64,1024]{3,2,1,0:T(8,128)S(1)} %get-tuple-element.32.u, f32[3,2,64,1024]{3,2,1,0:T(8,128)S(1)} %get-tuple-element.38.total, f32[64,1024]{1,0:T(8,128)S(1)} %collective-permute-done.7.arrived, ...), custom_call_target="tpu_custom_call", output_to_operand_aliasing={{0}: (5, {}), {1}: (6, {})} | custom-call | tf_op jit(solution)/shard_map/pallas_call | solution.py:499
Async XLA Ops:
  0.6 1.4 %copy-start = (f32[3,2,64,1024]{3,2,1,0:T(8,128)S(1)}, f32[3,2,64,1024]{3,2,1,0:T(8,128)}, u32[]{:S(2)}) copy-start(f32[3,2,64,1024]{3,2,1,0:T(8,128)} %u.9) | copy-start | bytes 4718596
  2.0 0.7 %copy-start.3 = (s32[3,2,8,8]{3,2,1,0:T(8,128)S(1)}, s32[3,2,8,8]{3,2,1,0:T(8,128)}, u32[]{:S(2)}) copy-start(s32[3,2,8,8]{3,2,1,0:T(8,128)} %shift.9) | copy-start | bytes 4612
  2.8 4.2 %copy-start.1 = (s32[3,2,64,1024]{3,2,1,0:T(8,128)S(1)}, s32[3,2,64,1024]{3,2,1,0:T(8,128)}, u32[]{:S(2)}) copy-start(s32[3,2,64,1024]{3,2,1,0:T(8,128)} %cls.3) | copy-start | bytes 4718596
  2.8 4.2 %copy-start.4 = (f32[8]{0:T(128)S(1)}, f32[8]{0:T(128)}, u32[]{:S(2)}) copy-start(f32[8]{0:T(128)} %stiff.1) | copy-start | bytes 100
  2.8 4.2 %copy-start.5 = (f32[2]{0:T(128)S(1)}, f32[2]{0:T(128)}, u32[]{:S(2)}) copy-start(f32[2]{0:T(128)} %cross.1) | copy-start | bytes 28
  2.8 4.2 %copy-start.6 = (s32[3]{0:T(128)S(1)}, s32[3]{0:T(128)}, u32[]{:S(2)}) copy-start(s32[3]{0:T(128)} %fixed.1) | copy-start | bytes 40
  3.0 3.9 %collective-permute-start = (f32[264,1024]{1,0:T(8,128)S(1)}, f32[264,1024]{1,0:T(8,128)S(1)}, u32[]{:S(2)}, u32[]{:S(2)}) collective-permute-start(f32[264,1024]{1,0:T(8,128)S(1)} %get-tuple-element.24), channel_id=1, source_target_pairs={{0,8},{8,0},{16,24},{24,16},{1,9},{9,1},{17,25},{25,17},{2,10},{10... | collective-permute-start | bytes 3244040 | tf_op jit(solution)/shard_map/ppermute | solution.py:28
  3.8 16.5 %collective-permute-start.3 = (f32[264,1024]{1,0:T(8,128)S(1)}, f32[264,1024]{1,0:T(8,128)S(1)}, u32[]{:S(2)}, u32[]{:S(2)}) collective-permute-start(f32[264,1024]{1,0:T(8,128)S(1)} %get-tuple-element.31), channel_id=1, source_target_pairs={{8,16},{16,8},{9,17},{17,9},{10,18},{18,10},{11,19},{19,11},{12,20... | collective-permute-start | bytes 3244040 | tf_op jit(solution)/shard_map/ppermute | solution.py:28
  7.7 8.6 %collective-permute-start.1 = (f32[16,1024]{1,0:T(8,128)S(1)}, f32[16,1024]{1,0:T(8,128)S(1)}, u32[]{:S(2)}, u32[]{:S(2)}) collective-permute-start(f32[16,1024]{1,0:T(8,128)S(1)} %get-tuple-element.28), channel_id=1, source_target_pairs={{0,1},{1,0},{2,3},{3,2},{4,5},{5,4},{6,7},{7,6},{8,9},{9,8},{10,11... | collective-permute-start | bytes 196616 | tf_op jit(solution)/shard_map/ppermute | solution.py:28
  8.0 8.3 %collective-permute-start.2 = (f32[16,1024]{1,0:T(8,128)S(1)}, f32[16,1024]{1,0:T(8,128)S(1)}, u32[]{:S(2)}, u32[]{:S(2)}) collective-permute-start(f32[16,1024]{1,0:T(8,128)S(1)} %get-tuple-element.29), channel_id=1, source_target_pairs={{1,2},{2,1},{3,4},{4,3},{5,6},{6,5},{9,10},{10,9},{11,12},{12,11},... | collective-permute-start | bytes 196616 | tf_op jit(solution)/shard_map/ppermute | solution.py:28
  12.2 4.2 %copy-start.2 = (f32[3,2,64,1024]{3,2,1,0:T(8,128)S(1)}, f32[3,2,64,1024]{3,2,1,0:T(8,128)}, u32[]{:S(2)}) copy-start(f32[3,2,64,1024]{3,2,1,0:T(8,128)} %w.1) | copy-start | bytes 4718596
  21.6 14.1 %collective-permute-start.4 = (f32[256,1024]{1,0:T(8,128)S(1)}, f32[256,1024]{1,0:T(8,128)S(1)}, u32[]{:S(2)}, u32[]{:S(2)}) collective-permute-start(f32[256,1024]{1,0:T(8,128)S(1)} %get-tuple-element.34), channel_id=1, source_target_pairs={{0,8},{8,0},{16,24},{24,16},{1,9},{9,1},{17,25},{25,17},{2,10},{10... | collective-permute-start | bytes 3145736 | tf_op jit(solution)/shard_map/ppermute | solution.py:28
  21.7 15.9 %collective-permute-start.8 = (f32[192,1024]{1,0:T(8,128)S(1)}, f32[192,1024]{1,0:T(8,128)S(1)}, u32[]{:S(2)}, u32[]{:S(2)}) collective-permute-start(f32[192,1024]{1,0:T(8,128)S(1)} %get-tuple-element.41), channel_id=1, source_target_pairs={{8,16},{16,8},{9,17},{17,9},{10,18},{18,10},{11,19},{19,11},{12,20... | collective-permute-start | bytes 2359304 | tf_op jit(solution)/shard_map/ppermute | solution.py:28
  24.9 14.4 %collective-permute-start.7 = (f32[64,1024]{1,0:T(8,128)S(1)}, f32[64,1024]{1,0:T(8,128)S(1)}, u32[]{:S(2)}, u32[]{:S(2)}) collective-permute-start(f32[64,1024]{1,0:T(8,128)S(1)} %get-tuple-element.39), channel_id=1, source_target_pairs={{8,16},{16,8},{9,17},{17,9},{10,18},{18,10},{11,19},{19,11},{12,20... | collective-permute-start | bytes 786440 | tf_op jit(solution)/shard_map/ppermute | solution.py:28
  27.3 8.4 %collective-permute-start.5 = (f32[16,1024]{1,0:T(8,128)S(1)}, f32[16,1024]{1,0:T(8,128)S(1)}, u32[]{:S(2)}, u32[]{:S(2)}) collective-permute-start(f32[16,1024]{1,0:T(8,128)S(1)} %get-tuple-element.35), channel_id=1, source_target_pairs={{0,1},{1,0},{2,3},{3,2},{4,5},{5,4},{6,7},{7,6},{8,9},{9,8},{10,11... | collective-permute-start | bytes 196616 | tf_op jit(solution)/shard_map/ppermute | solution.py:28
  27.3 8.3 %collective-permute-start.6 = (f32[16,1024]{1,0:T(8,128)S(1)}, f32[16,1024]{1,0:T(8,128)S(1)}, u32[]{:S(2)}, u32[]{:S(2)}) collective-permute-start(f32[16,1024]{1,0:T(8,128)S(1)} %get-tuple-element.36), channel_id=1, source_target_pairs={{1,2},{2,1},{3,4},{4,3},{5,6},{6,5},{9,10},{10,9},{11,12},{12,11},... | collective-permute-start | bytes 196616 | tf_op jit(solution)/shard_map/ppermute | solution.py:28

commit v5 on v4

--- a/solution.py
+++ b/solution.py
@@ -176,19 +176,23 @@
         splat[MOVING + s] = jnp.full(tile, jnp.where(fixed[s] == 0, 1.0, 0.0))
 
 
-def lead_kernel(u, shift, slow, fast):
+def lead_kernel(u, shift, slow_top, slow_rest, fast):
     sections, _, rows, width = u.shape
+    rest = slow_rest.shape[0] // 4
+    top = rows - rest
 
     def body(after):
-        for out, side in ((slow, after), (fast, not after)):
-            for k, own in enumerate((near_of(side, sections), second_of(side, sections))):
-                for c in range(2):
-                    out[(2 * k + c) * rows : (2 * k + c + 1) * rows, :] = u[own, c]
+        for j in range(2):
+            for c in range(2):
+                k = 2 * j + c
+                block = u[(near_of, second_of)[j](after, sections), c]
+                slow_top[k * top : (k + 1) * top, :] = block[:top]
+                slow_rest[k * rest : (k + 1) * rest, :] = block[top:]
+                fast[k * rows : (k + 1) * rows, :] = u[(near_of, second_of)[j](not after, sections), c]
 
     by_side(body)
-    put_tail(shift, slow, 4 * rows, width)
-    after_blocks = slice(4 * rows, slow.shape[0])
-    fast[after_blocks, :] = slow[after_blocks, :]
+    put_tail(shift, slow_top, 4 * top, width)
+    fast[4 * rows : fast.shape[0], :] = slow_top[4 * top : slow_top.shape[0], :]
 
 
 def prepare_kernel(u, cls, arrived, stiff, cross, fixed, rim_a, rim_b, splat):
@@ -218,7 +222,7 @@
     return values[0]
 
 
-def inside(u, w, total, half_across, half_below, shift, splat, scalars, sem):
+def inside(u, w, total, half_across, half_below, shift, splat, scalars, sem, forces):
     sections, _, rows, width = u.shape
     rbs, cbs = rows // ROWS, width // COLS
     load = pltpu.make_async_copy(shift, scalars, sem)
@@ -241,36 +245,49 @@
     lax.fori_loop(0, cbs, below, 0)
     load.wait()
     last = lax.broadcasted_iota(jnp.int32, (ROWS, width), 1) == width - 1
-
-    def row(rb, carry):
-        at = rows_of(rb)
-        add = [[total[s, c, at, :] for c in range(2)] for s in range(sections)]
-        for s in range(sections):
-            x, y = u[s, 0, at, :], u[s, 1, at, :]
-            half = jnp.where(last, 0.0, half_across(s, at))
-            f = flow(pltpu.roll(x, width - 1, 1) - x, pltpu.roll(y, width - 1, 1) - y, half)
-            for c in range(2):
-                add[s][c] = add[s][c] + (f[c] - pltpu.roll(f[c], 1, 1))
-        for hops in (1, 2):
-            half = wide_splat(splat, INSIDE + hops - 1, width)
-            for s in range(sections - hops):
-                offsets = [scalars[s, hops - 1, rb, cb] for cb in range(cbs)]
-                there = [(-o) & (COLS - 1) for o in offsets]
-                back = [o & (COLS - 1) for o in offsets]
-                e = [turned(u[s + hops, c, at, :], there) - u[s, c, at, :] for c in range(2)]
-                f = flow(e[0], e[1], half)
-                for c in range(2):
-                    add[s][c] = add[s][c] + f[c]
-                    add[s + hops][c] = add[s + hops][c] - turned(f[c], back)
-        for s in range(sections):
-            for c in range(2):
-                total[s, c, at, :] = add[s][c]
-        return carry
-
-    lax.fori_loop(0, rbs, row, 0)
-
-
-def first_inside_kernel(u, cls, shift, splat, total, half, scalars, sem):
+    pairs = [(s, hops) for hops in (1, 2) for s in range(sections - hops)]
+
+    def over_rows(body):
+        lax.fori_loop(0, rbs, lambda rb, carry: body(rb, rows_of(rb)) or carry, 0, unroll=True)
+
+    def put(k, s, at, f):
+        for c in range(2):
+            total[s, c, at, :] += f[c]
+            forces[k, c, at, :] = f[c]
+
+    def across(s, rb, at):
+        x, y = u[s, 0, at, :], u[s, 1, at, :]
+        half = jnp.where(last, 0.0, half_across(s, at))
+        f = flow(pltpu.roll(x, width - 1, 1) - x, pltpu.roll(y, width - 1, 1) - y, half)
+        put(len(pairs) + s, s, at, f)
+
+    def across_back(s, rb, at):
+        for c in range(2):
+            total[s, c, at, :] -= pltpu.roll(forces[len(pairs) + s, c, at, :], 1, 1)
+
+    def between(k, rb, at):
+        s, hops = pairs[k]
+        there = [(-scalars[s, hops - 1, rb, cb]) & (COLS - 1) for cb in range(cbs)]
+        e = [turned(u[s + hops, c, at, :], there) - u[s, c, at, :] for c in range(2)]
+        put(k, s, at, flow(e[0], e[1], wide_splat(splat, INSIDE + hops - 1, width)))
+
+    def between_back(k, rb, at):
+        s, hops = pairs[k]
+        back = [scalars[s, hops - 1, rb, cb] & (COLS - 1) for cb in range(cbs)]
+        for c in range(2):
+            total[s + hops, c, at, :] -= turned(forces[k, c, at, :], back)
+
+    for body, count in (
+        (across, sections),
+        (between, len(pairs)),
+        (across_back, sections),
+        (between_back, len(pairs)),
+    ):
+        for k in range(count):
+            over_rows(functools.partial(body, k))
+
+
+def first_inside_kernel(u, cls, shift, splat, total, half, scalars, sem, forces):
     table = splat[TABLE]
     values = [jnp.broadcast_to(table[:, k : k + 1], (ROWS, COLS)) for k in range(CLASSES)]
     rows = u.shape[2]
@@ -289,17 +306,17 @@
         half[s, 1, :, at] = k
         return k
 
-    inside(u, None, total, half_across, half_below, shift, splat, scalars, sem)
-
-
-def later_inside_kernel(u, w, half, shift, splat, total, scalars, sem):
+    inside(u, None, total, half_across, half_below, shift, splat, scalars, sem, forces)
+
+
+def later_inside_kernel(u, w, half, shift, splat, total, scalars, sem, forces):
     def half_across(s, at):
         return half[s, 0, at, :]
 
     def half_below(s, at):
         return half[s, 1, :, at]
 
-    inside(u, w, total, half_across, half_below, shift, splat, scalars, sem)
+    inside(u, w, total, half_across, half_below, shift, splat, scalars, sem, forces)
 
 
 def side_flow(u, own, arrived, block, height, base, index, j, half, rb):
@@ -343,7 +360,10 @@
         own, block, hops = pairs_of(after, sections)[j]
         stiff = wide_splat(splat, FAST + hops - 1, width)
         for rb in range(rows // ROWS):
-            f = side_flow(u, own, fast, block, rows, 0, index, j, stiff, rb)
+            if isinstance(fast, tuple):
+                f = side_flow(u, own, fast[block], 0, rows, 0, index, j, stiff, rb)
+            else:
+                f = side_flow(u, own, fast, block, rows, 0, index, j, stiff, rb)
             for c in range(2):
                 total[own, c, rows_of(rb), :] += f[c]
 
@@ -369,9 +389,11 @@
 
 
 def later_rims_kernel(
-    u, total_in, half, fast, rim_a, rim_b, index, splat, total, out_u, out_w, new_u, new_w, sem
+    u, total_in, half, fast_near, fast_far, rim_a, rim_b, index, splat,
+    total, out_u, out_w, new_u, new_w, sem,
 ):
     sections, _, rows, width = u.shape
+    fast = (fast_near, fast_far)
 
     def body(after):
         near = (near_of(after, sections), second_of(after, sections))
@@ -413,46 +435,65 @@
     return value
 
 
-def step_kernel(
-    u, total, arrived, half, shift, splat,
-    new_u, new_w, slow_top, slow_rest, fast, index, rim_a, rim_b,
+def step_rows(u, after, arrived, height, base, index, splat, total, new_u, new_w, sections, sent):
+    count, _, _, width = u.shape
+    slow_edge = (near_of(after, count), second_of(after, count))
+    for s in sections:
+        moving = wide_splat(splat, MOVING + s, width)
+        for row in range(base, base + height, ROWS):
+            at, rb = pl.ds(row, ROWS), row // ROWS
+            if s in slow_edge:
+                j = slow_edge.index(s)
+                value = slow_values(u, after, arrived, height, base, index, splat, total, j, rb)
+            else:
+                value = [total[s, c, at, :] for c in range(2)]
+            for c in range(2):
+                v = value[c] * moving
+                moved = u[s, c, at, :] + STEP * v
+                new_w[s, c, at, :] = v
+                new_u[s, c, at, :] = moved
+                if s in slow_edge:
+                    sent[pl.ds((2 * j + c) * height + row - base, ROWS), :] = moved
+
+
+def top_kernel(u, total, arrived, shift, splat, new_u, new_w, slow, index):
+    sections = u.shape[0]
+    height = slow.shape[0] // 4
+
+    def body(after):
+        put_index(after, shift, arrived, 4 * height, index)
+        edge = (near_of(after, sections), second_of(after, sections))
+        step_rows(u, after, arrived, height, 0, index, splat, total, new_u, new_w, edge, slow)
+
+    by_side(body)
+
+
+def rest_kernel(
+    u, total, new_u_in, new_w_in, arrived, index, splat,
+    new_u, new_w, slow, fast_near, fast_far,
 ):
-    sections, _, rows, width = u.shape
-    top = slow_top.shape[0] // 4
+    sections, _, rows, _ = u.shape
+    height = slow.shape[0] // 4
 
     def body(after):
-        put_index(after, shift, arrived, 4 * rows, index)
-        slow_edge = (near_of(after, sections), second_of(after, sections))
-        fast_edge = (near_of(not after, sections), second_of(not after, sections))
-        for s in range(sections):
-            moving = wide_splat(splat, MOVING + s, width)
-            for rb in range(rows // ROWS):
-                at, row = rows_of(rb), rb * ROWS
-                if s in slow_edge:
-                    value = slow_values(
-                        u, after, arrived, rows, 0, index, splat, total, slow_edge.index(s), rb
-                    )
-                else:
-                    value = [total[s, c, at, :] for c in range(2)]
-                for c in range(2):
-                    v = value[c] * moving
-                    moved = u[s, c, at, :] + STEP * v
-                    new_w[s, c, at, :] = v
-                    new_u[s, c, at, :] = moved
-                    if s in fast_edge:
-                        fast[pl.ds((2 * fast_edge.index(s) + c) * rows + row, ROWS), :] = moved
-                    if s in slow_edge:
-                        k = 2 * slow_edge.index(s) + c
-                        if row < top:
-                            slow_top[pl.ds(k * top + row, ROWS), :] = moved
-                        else:
-                            slow_rest[pl.ds(k * (rows - top) + row - top, ROWS), :] = moved
+        edge = (near_of(after, sections), second_of(after, sections))
+        others = [s for s in range(sections) if s not in edge]
+        base = rows - height
+        step_rows(u, after, arrived, height, base, index, splat, total, new_u, new_w, edge, slow)
+        step_rows(u, after, None, rows, 0, index, splat, total, new_u, new_w, others, None)
+        for j, s in enumerate((near_of(not after, sections), second_of(not after, sections))):
+            for c in range(2):
+                (fast_near, fast_far)[j][c * rows : (c + 1) * rows, :] = new_u[s, c]
 
     by_side(body)
+
+
+def rims_kernel(u, half, arrived, rim_a, rim_b):
+    sections, _, rows, _ = u.shape
     last = slice(rows - 1, rows)
     put_rims(
-        lambda s, c: new_u[s, c, 0:1, :],
-        lambda s, c: new_u[s, c, last, :],
+        lambda s, c: u[s, c, 0:1, :],
+        lambda s, c: u[s, c, last, :],
         lambda s: half[s, 1, last, :],
         rim_a,
         rim_b,
@@ -515,16 +556,26 @@
         return jax.ShapeDtypeStruct(shape, dtype)
 
     full = array(*u.shape)
-    two = array(4 * rows, width)
+    one = array(2 * rows, width)
     rim = array(-(-3 * sections // ROWS) * ROWS, width)
     splat = array(MOVING + sections, ROWS, COLS)
     index = array(3, tail_rows(rows), width, dtype=jnp.int32)
-    scalars = [pltpu.SMEM(shift.shape, jnp.int32), pltpu.SemaphoreType.DMA]
+    scalars = [
+        pltpu.SMEM(shift.shape, jnp.int32),
+        pltpu.SemaphoreType.DMA,
+        pltpu.VMEM((3 * sections - 3,) + u.shape[1:], jnp.float32),
+    ]
     smem = pl.BlockSpec(memory_space=pltpu.SMEM)
 
-    two_tail = array(4 * rows + index.shape[1], width)
-    slow, fast = call(lead_kernel, [two_tail, two_tail], [u, shift])
-    slow = exchange(slow, "sec", "b")
+    top = max(rows // ROWS * 3 // 4, 1) * ROWS
+    tail = index.shape[1]
+    slow_top, slow_rest, fast = call(
+        lead_kernel,
+        [array(4 * top + tail, width), array(4 * (rows - top), width), array(4 * rows + tail, width)],
+        [u, shift],
+    )
+    slow_top = exchange(slow_top, "sec", "b")
+    slow_rest = exchange(slow_rest, "sec", "b")
     fast = exchange(fast, "sec", "a")
     rim_a, rim_b, splat = call(
         prepare_kernel,
@@ -543,15 +594,24 @@
         [u, w, total, half, fast, rim_a, rim_b, shift, splat],
         {2: 0},
     )
-    top = max(rows // ROWS * 3 // 4, 1) * ROWS
-    u, w, slow_top, slow_rest, fast, index, rim_a, rim_b = call(
-        step_kernel,
-        [full, full, array(4 * top, width), array(4 * (rows - top), width), two, index, rim, rim],
-        [u, total, slow, half, shift, splat],
+    new_u, new_w, slow_top, index = call(
+        top_kernel,
+        [full, full, array(4 * top, width), index],
+        [u, total, slow_top, shift, splat],
     )
     slow_top = exchange(slow_top, "sec", "b")
+    u, w, slow_rest, fast_near, fast_far = call(
+        rest_kernel,
+        [full, full, array(4 * (rows - top), width), one, one],
+        [u, total, new_u, new_w, slow_rest, index, splat],
+        {2: 0, 3: 1},
+    )
     slow_rest = exchange(slow_rest, "sec", "b")
-    fast = exchange(fast, "sec", "a")
+    fast_near = exchange(fast_near, "sec", "a")
+    fast_far = exchange(fast_far, "sec", "a")
+    rim_a, rim_b = call(
+        rims_kernel, [rim, rim], [u, half, fast_near], in_specs=[VMEM] * 2 + [ANY]
+    )
     rim_a = exchange(rim_a, "strip", "a")
     rim_b = exchange(rim_b, "strip", "b")
     (total,) = call(later_inside_kernel, [full], [u, w, half, shift, splat], scratch=scalars)
@@ -559,8 +619,9 @@
     total, out_u, out_w = call(
         later_rims_kernel,
         [full, full, full],
-        [u, total, half, fast, rim_a, rim_b, fast_index, splat],
+        [u, total, half, fast_near, fast_far, rim_a, rim_b, fast_index, splat],
         {1: 0},
+        in_specs=[VMEM] * 9,
         scratch=[pltpu.VMEM((done, 2, rows, width), jnp.float32)] * 2
         + [pltpu.SemaphoreType.DMA((2 * done,))],
         out_specs=[VMEM, ANY, ANY],

time: 41 us -> 41.3 us (level)
  the two profiles are of different devices: /device:TPU:3 before, /device:TPU:12 now
where the time goes in v5:
time: 41.3 us; the launch traced here: 40.9 us
  starting transfers between devices  18.9 us (46%)
  Pallas kernels  15.1 us (37%)
  waiting for transfers between devices  3.69 us (9%)
  local copies, waits for them, and re-layouts  2.16 us (5%)
  between operations  1.05 us (3%)
    ppermute x11, starting transfers between devices, exchange(): return lax.ppermute(value, axis, route)  18.9 us
    pallas_call x11, Pallas kernels, call(): pl.pallas_call(kernel, out_shape=outs, in_specs=in_specs or [VMEM] * len(...  15.1 us
    ppermute x11, waiting for transfers between devices, exchange(): return lax.ppermute(value, axis, route)  3.69 us
    unnamed x14, local copies, waits for them, and re-layouts  2.16 us
  transfers between devices with their start and end apart: 11, of which 2 were waited for; matrix products, arithmetic and copies ran while one was open for 0% of the time, Pallas kernels for 34%

profile of v5, /device:TPU:12, one launch (start us, length us, event | category | flops | bytes accessed | tf_op | source)
XLA Modules:
  0.0 40.9 jit_solution(6283129699858518151)
XLA Ops:
  0.6 0.0 copy-start
  0.6 1.4 %copy-done = f32[3,2,64,1024]{3,2,1,0:T(8,128)S(1)} copy-done((f32[3,2,64,1024]{3,2,1,0:T(8,128)S(1)}, f32[3,2,64,1024]{3,2,1,0:T(8,128)}, u32[]{:S(2)}) %copy-start) | copy-done | bytes 1572888
  2.0 0.0 copy-start.3
  2.0 0.7 %copy-done.3 = s32[3,2,8,8]{3,2,1,0:T(8,128)S(1)} copy-done((s32[3,2,8,8]{3,2,1,0:T(8,128)S(1)}, s32[3,2,8,8]{3,2,1,0:T(8,128)}, u32[]{:S(2)}) %copy-start.3) | copy-done | bytes 1560
  2.8 0.0 copy-start.1
  2.8 0.0 copy-start.4
  2.8 0.0 copy-start.5
  2.8 0.0 copy-start.6
  2.8 0.3 shard_map.86
  3.0 0.1 collective-permute-start
  3.1 2.5 %collective-permute-start.3 = (f32[200,1024]{1,0:T(8,128)S(1)}, f32[200,1024]{1,0:T(8,128)S(1)}, u32[]{:S(2)}, u32[]{:S(2)}) collective-permute-start(f32[200,1024]{1,0:T(8,128)S(1)} %get-tuple-element.35), channel_id=1, source_target_pairs={{8,16},{16,8},{9,17},{17,9},{10,18},{18,10},{11,19},{19,11},{12,20... | collective-permute-start | bytes 2457608 | tf_op jit(solution)/shard_map/ppermute | solution.py:28
  5.6 3.2 %collective-permute-start.4 = (f32[64,1024]{1,0:T(8,128)S(1)}, f32[64,1024]{1,0:T(8,128)S(1)}, u32[]{:S(2)}, u32[]{:S(2)}) collective-permute-start(f32[64,1024]{1,0:T(8,128)S(1)} %get-tuple-element.38), channel_id=1, source_target_pairs={{8,16},{16,8},{9,17},{17,9},{10,18},{18,10},{11,19},{19,11},{12,20... | collective-permute-start | bytes 786440 | tf_op jit(solution)/shard_map/ppermute | solution.py:28
  8.8 0.0 collective-permute-done.arrived.fast
  8.8 0.0 copy-done.1
  8.9 0.0 copy-done.4
  8.9 0.0 copy-done.5
  8.9 0.0 copy-done.6
  8.9 0.7 %shard_map.87 = (f32[16,1024]{1,0:T(8,128)S(1)}, f32[16,1024]{1,0:T(8,128)S(1)}, f32[10,8,128]{2,1,0:T(8,128)S(1)}) custom-call(f32[3,2,64,1024]{3,2,1,0:T(8,128)S(1)} %copy-done, s32[3,2,64,1024]{3,2,1,0:T(8,128)S(1)} %copy-done.1, f32[264,1024]{1,0:T(8,128)S(1)} %collective-permute-done.arrived.fast, f32[8]{0:T(128)S(1)} %copy-done.4, f32[2]{0:T(128)S(1)} %copy-done.5, ...), custom_call_target="tpu_custom_call" | custom-call | tf_op jit(solution)/shard_map/pallas_call | solution.py:540
  9.6 1.6 %collective-permute-start.1 = (f32[16,1024]{1,0:T(8,128)S(1)}, f32[16,1024]{1,0:T(8,128)S(1)}, u32[]{:S(2)}, u32[]{:S(2)}) collective-permute-start(f32[16,1024]{1,0:T(8,128)S(1)} %get-tuple-element.32), channel_id=1, source_target_pairs={{0,1},{1,0},{2,3},{3,2},{4,5},{5,4},{6,7},{7,6},{8,9},{9,8},{10,11... | collective-permute-start | bytes 196616 | tf_op jit(solution)/shard_map/ppermute | solution.py:28
  11.1 2.3 %collective-permute-start.2 = (f32[16,1024]{1,0:T(8,128)S(1)}, f32[16,1024]{1,0:T(8,128)S(1)}, u32[]{:S(2)}, u32[]{:S(2)}) collective-permute-start(f32[16,1024]{1,0:T(8,128)S(1)} %get-tuple-element.33), channel_id=1, source_target_pairs={{1,2},{2,1},{3,4},{4,3},{5,6},{6,5},{9,10},{10,9},{11,12},{12,11},... | collective-permute-start | bytes 196616 | tf_op jit(solution)/shard_map/ppermute | solution.py:28
  13.5 0.0 copy-start.2
  13.5 3.3 %shard_map.88 = (f32[3,2,64,1024]{3,2,1,0:T(8,128)S(1)}, f32[3,2,64,1024]{3,2,1,0:T(8,128)S(1)}) custom-call(f32[3,2,64,1024]{3,2,1,0:T(8,128)S(1)} %copy-done, s32[3,2,64,1024]{3,2,1,0:T(8,128)S(1)} %copy-done.1, s32[3,2,8,8]{3,2,1,0:T(8,128)S(1)} %copy-done.3, f32[10,8,128]{2,1,0:T(8,128)S(1)} %get-tuple-element.29.splat), custom_call_target="tpu_custom_call" | custom-call | tf_op jit(solution)/shard_map/pallas_call | solution.py:540
  16.7 0.0 collective-permute-done.1.rim_a
  16.7 1.4 %collective-permute-done.2.rim_b = f32[16,1024]{1,0:T(8,128)S(1)} collective-permute-done((f32[16,1024]{1,0:T(8,128)S(1)}, f32[16,1024]{1,0:T(8,128)S(1)}, u32[]{:S(2)}, u32[]{:S(2)}) %collective-permute-start.2) | collective-permute-done | bytes 65568 | tf_op jit(solution)/shard_map/ppermute | solution.py:28
  18.2 0.0 copy-done.2
  18.2 1.6 %shard_map.89 = (f32[3,2,64,1024]{3,2,1,0:T(8,128)S(1)}, s32[3,8,1024]{2,1,0:T(8,128)S(1)}) custom-call(f32[3,2,64,1024]{3,2,1,0:T(8,128)S(1)} %copy-done, f32[3,2,64,1024]{3,2,1,0:T(8,128)S(1)} %copy-done.2, f32[3,2,64,1024]{3,2,1,0:T(8,128)S(1)} %get-tuple-element.30.total_in, ...), custom_call_target="tpu_custom_call", output_to_operand_aliasing={{0}: (2, {})} | custom-call | tf_op jit(solution)/shard_map/pallas_call | solution.py:540
  19.8 0.0 collective-permute-done.3.arrived
  19.8 1.0 %shard_map.90 = (f32[3,2,64,1024]{3,2,1,0:T(8,128)S(1)}, f32[3,2,64,1024]{3,2,1,0:T(8,128)S(1)}, f32[192,1024]{1,0:T(8,128)S(1)}, s32[3,8,1024]{2,1,0:T(8,128)S(1)}) custom-call(f32[3,2,64,1024]{3,2,1,0:T(8,128)S(1)} %copy-done, f32[3,2,64,1024]{3,2,1,0:T(8,128)S(1)} %get-tuple-element.34.total, f32[200,1024]{1,0:T(8,128)S(1)} %collective-permute-done.3.arrived, ...), custom_call_target="tpu_custom_call" | custom-call | tf_op jit(solution)/shard_map/pallas_call | solution.py:540
  20.8 1.9 %collective-permute-start.10 = (f32[192,1024]{1,0:T(8,128)S(1)}, f32[192,1024]{1,0:T(8,128)S(1)}, u32[]{:S(2)}, u32[]{:S(2)}) collective-permute-start(f32[192,1024]{1,0:T(8,128)S(1)} %get-tuple-element.49), channel_id=1, source_target_pairs={{8,16},{16,8},{9,17},{17,9},{10,18},{18,10},{11,19},{19,11},{12,20... | collective-permute-start | bytes 2359304 | tf_op jit(solution)/shard_map/ppermute | solution.py:28
  22.7 0.0 collective-permute-done.4.arrived
  22.7 0.5 %shard_map.91 = (f32[3,2,64,1024]{3,2,1,0:T(8,128)S(1)}, f32[3,2,64,1024]{3,2,1,0:T(8,128)S(1)}, f32[64,1024]{1,0:T(8,128)S(1)}, f32[128,1024]{1,0:T(8,128)S(1)}, f32[128,1024]{1,0:T(8,128)S(1)}) custom-call(f32[3,2,64,1024]{3,2,1,0:T(8,128)S(1)} %copy-done, ...), custom_call_target="tpu_custom_call", output_to_operand_aliasing={{0}: (2, {}), {1}: (3, {})} | custom-call | tf_op jit(solution)/shard_map/pallas_call | solution.py:540
  23.2 0.1 collective-permute-start.5
  23.3 0.5 %collective-permute-start.6 = (f32[128,1024]{1,0:T(8,128)S(1)}, f32[128,1024]{1,0:T(8,128)S(1)}, u32[]{:S(2)}, u32[]{:S(2)}) collective-permute-start(f32[128,1024]{1,0:T(8,128)S(1)} %get-tuple-element.43), channel_id=1, source_target_pairs={{0,8},{8,0},{16,24},{24,16},{1,9},{9,1},{17,25},{25,17},{2,10},{10... | collective-permute-start | bytes 1572872 | tf_op jit(solution)/shard_map/ppermute | solution.py:28
  23.8 3.6 %collective-permute-start.9 = (f32[64,1024]{1,0:T(8,128)S(1)}, f32[64,1024]{1,0:T(8,128)S(1)}, u32[]{:S(2)}, u32[]{:S(2)}) collective-permute-start(f32[64,1024]{1,0:T(8,128)S(1)} %get-tuple-element.48), channel_id=1, source_target_pairs={{8,16},{16,8},{9,17},{17,9},{10,18},{18,10},{11,19},{19,11},{12,20... | collective-permute-start | bytes 786440 | tf_op jit(solution)/shard_map/ppermute | solution.py:28
  27.4 0.0 collective-permute-done.5.arrived.fast_near
  27.5 1.3 %collective-permute-start.7 = (f32[16,1024]{1,0:T(8,128)S(1)}, f32[16,1024]{1,0:T(8,128)S(1)}, u32[]{:S(2)}, u32[]{:S(2)}) collective-permute-start(f32[16,1024]{1,0:T(8,128)S(1)} %get-tuple-element.44), channel_id=1, source_target_pairs={{0,1},{1,0},{2,3},{3,2},{4,5},{5,4},{6,7},{7,6},{8,9},{9,8},{10,11... | collective-permute-start | bytes 196616 | tf_op jit(solution)/shard_map/ppermute | solution.py:28
  28.7 1.9 %collective-permute-start.8 = (f32[16,1024]{1,0:T(8,128)S(1)}, f32[16,1024]{1,0:T(8,128)S(1)}, u32[]{:S(2)}, u32[]{:S(2)}) collective-permute-start(f32[16,1024]{1,0:T(8,128)S(1)} %get-tuple-element.45), channel_id=1, source_target_pairs={{1,2},{2,1},{3,4},{4,3},{5,6},{6,5},{9,10},{10,9},{11,12},{12,11},... | collective-permute-start | bytes 196616 | tf_op jit(solution)/shard_map/ppermute | solution.py:28
  30.7 2.9 %shard_map.92.total_in = f32[3,2,64,1024]{3,2,1,0:T(8,128)S(1)} custom-call(f32[3,2,64,1024]{3,2,1,0:T(8,128)S(1)} %get-tuple-element.40.u, f32[3,2,64,1024]{3,2,1,0:T(8,128)S(1)} %get-tuple-element.41.w, f32[3,2,64,1024]{3,2,1,0:T(8,128)S(1)} %get-tuple-element.31.half, s32[3,2,8,8]{3,2,1,0:T(8,128)S(1)} %copy-done.3, f32[10,8,128]{2,1,0:T(8,128)S(1)} %get-tuple-element.29.splat), custom_call_target="tpu_custom_call" | custom-call | tf_op jit(solution)/shard_map/pallas_call | solution.py:540
  33.5 0.0 collective-permute-done.6.fast_far
  33.5 0.0 collective-permute-done.7.rim_a
  33.6 2.2 %collective-permute-done.8.rim_b = f32[16,1024]{1,0:T(8,128)S(1)} collective-permute-done((f32[16,1024]{1,0:T(8,128)S(1)}, f32[16,1024]{1,0:T(8,128)S(1)}, u32[]{:S(2)}, u32[]{:S(2)}) %collective-permute-start.8) | collective-permute-done | bytes 65568 | tf_op jit(solution)/shard_map/ppermute | solution.py:28
  35.8 2.1 %shard_map.94 = (f32[3,2,64,1024]{3,2,1,0:T(8,128)S(1)}, f32[3,2,64,1024]{3,2,1,0:T(8,128)}, f32[3,2,64,1024]{3,2,1,0:T(8,128)}) custom-call(f32[3,2,64,1024]{3,2,1,0:T(8,128)S(1)} %get-tuple-element.40.u, f32[3,2,64,1024]{3,2,1,0:T(8,128)S(1)} %shard_map.92.total_in, ...), custom_call_target="tpu_custom_call", output_to_operand_aliasing={{0}: (1, {})} | custom-call | tf_op jit(solution)/shard_map/pallas_call | solution.py:540
  37.9 0.0 collective-permute-done.10.arrived
  37.9 1.7 %shard_map.95 = (f32[3,2,64,1024]{3,2,1,0:T(8,128)}, f32[3,2,64,1024]{3,2,1,0:T(8,128)}) custom-call(f32[3,2,64,1024]{3,2,1,0:T(8,128)S(1)} %get-tuple-element.40.u, f32[3,2,64,1024]{3,2,1,0:T(8,128)S(1)} %get-tuple-element.47.total, f32[192,1024]{1,0:T(8,128)S(1)} %collective-permute-done.10.arrived, ...), custom_call_target="tpu_custom_call", output_to_operand_aliasing={{0}: (5, {}), {1}: (6, {})} | custom-call | tf_op jit(solution)/shard_map/pallas_call | solution.py:540
  39.7 0.0 collective-permute-done.9.arrived
  39.7 1.1 %shard_map.96 = (f32[3,2,64,1024]{3,2,1,0:T(8,128)}, f32[3,2,64,1024]{3,2,1,0:T(8,128)}) custom-call(f32[3,2,64,1024]{3,2,1,0:T(8,128)S(1)} %get-tuple-element.40.u, f32[3,2,64,1024]{3,2,1,0:T(8,128)S(1)} %get-tuple-element.47.total, f32[64,1024]{1,0:T(8,128)S(1)} %collective-permute-done.9.arrived, ...), custom_call_target="tpu_custom_call", output_to_operand_aliasing={{0}: (5, {}), {1}: (6, {})} | custom-call | tf_op jit(solution)/shard_map/pallas_call | solution.py:540
  (1 shorter events, 0.0 us)
Async XLA Ops:
  0.6 1.4 %copy-start = (f32[3,2,64,1024]{3,2,1,0:T(8,128)S(1)}, f32[3,2,64,1024]{3,2,1,0:T(8,128)}, u32[]{:S(2)}) copy-start(f32[3,2,64,1024]{3,2,1,0:T(8,128)} %u.11) | copy-start | bytes 4718596
  2.0 0.7 %copy-start.3 = (s32[3,2,8,8]{3,2,1,0:T(8,128)S(1)}, s32[3,2,8,8]{3,2,1,0:T(8,128)}, u32[]{:S(2)}) copy-start(s32[3,2,8,8]{3,2,1,0:T(8,128)} %shift.9) | copy-start | bytes 4612
  2.8 6.1 %copy-start.1 = (s32[3,2,64,1024]{3,2,1,0:T(8,128)S(1)}, s32[3,2,64,1024]{3,2,1,0:T(8,128)}, u32[]{:S(2)}) copy-start(s32[3,2,64,1024]{3,2,1,0:T(8,128)} %cls.3) | copy-start | bytes 4718596
  2.8 6.1 %copy-start.4 = (f32[8]{0:T(128)S(1)}, f32[8]{0:T(128)}, u32[]{:S(2)}) copy-start(f32[8]{0:T(128)} %stiff.1) | copy-start | bytes 100
  2.8 6.1 %copy-start.5 = (f32[2]{0:T(128)S(1)}, f32[2]{0:T(128)}, u32[]{:S(2)}) copy-start(f32[2]{0:T(128)} %cross.1) | copy-start | bytes 28
  2.8 6.1 %copy-start.6 = (s32[3]{0:T(128)S(1)}, s32[3]{0:T(128)}, u32[]{:S(2)}) copy-start(s32[3]{0:T(128)} %fixed.1) | copy-start | bytes 40
  3.0 5.8 %collective-permute-start = (f32[264,1024]{1,0:T(8,128)S(1)}, f32[264,1024]{1,0:T(8,128)S(1)}, u32[]{:S(2)}, u32[]{:S(2)}) collective-permute-start(f32[264,1024]{1,0:T(8,128)S(1)} %get-tuple-element.28), channel_id=1, source_target_pairs={{0,8},{8,0},{16,24},{24,16},{1,9},{9,1},{17,25},{25,17},{2,10},{10... | collective-permute-start | bytes 3244040 | tf_op jit(solution)/shard_map/ppermute | solution.py:28
  3.1 16.6 %collective-permute-start.3 = (f32[200,1024]{1,0:T(8,128)S(1)}, f32[200,1024]{1,0:T(8,128)S(1)}, u32[]{:S(2)}, u32[]{:S(2)}) collective-permute-start(f32[200,1024]{1,0:T(8,128)S(1)} %get-tuple-element.35), channel_id=1, source_target_pairs={{8,16},{16,8},{9,17},{17,9},{10,18},{18,10},{11,19},{19,11},{12,20... | collective-permute-start | bytes 2457608 | tf_op jit(solution)/shard_map/ppermute | solution.py:28
  5.6 17.1 %collective-permute-start.4 = (f32[64,1024]{1,0:T(8,128)S(1)}, f32[64,1024]{1,0:T(8,128)S(1)}, u32[]{:S(2)}, u32[]{:S(2)}) collective-permute-start(f32[64,1024]{1,0:T(8,128)S(1)} %get-tuple-element.38), channel_id=1, source_target_pairs={{8,16},{16,8},{9,17},{17,9},{10,18},{18,10},{11,19},{19,11},{12,20... | collective-permute-start | bytes 786440 | tf_op jit(solution)/shard_map/ppermute | solution.py:28
  9.6 7.2 %collective-permute-start.1 = (f32[16,1024]{1,0:T(8,128)S(1)}, f32[16,1024]{1,0:T(8,128)S(1)}, u32[]{:S(2)}, u32[]{:S(2)}) collective-permute-start(f32[16,1024]{1,0:T(8,128)S(1)} %get-tuple-element.32), channel_id=1, source_target_pairs={{0,1},{1,0},{2,3},{3,2},{4,5},{5,4},{6,7},{7,6},{8,9},{9,8},{10,11... | collective-permute-start | bytes 196616 | tf_op jit(solution)/shard_map/ppermute | solution.py:28
  11.1 7.0 %collective-permute-start.2 = (f32[16,1024]{1,0:T(8,128)S(1)}, f32[16,1024]{1,0:T(8,128)S(1)}, u32[]{:S(2)}, u32[]{:S(2)}) collective-permute-start(f32[16,1024]{1,0:T(8,128)S(1)} %get-tuple-element.33), channel_id=1, source_target_pairs={{1,2},{2,1},{3,4},{4,3},{5,6},{6,5},{9,10},{10,9},{11,12},{12,11},... | collective-permute-start | bytes 196616 | tf_op jit(solution)/shard_map/ppermute | solution.py:28
  13.5 4.7 %copy-start.2 = (f32[3,2,64,1024]{3,2,1,0:T(8,128)S(1)}, f32[3,2,64,1024]{3,2,1,0:T(8,128)}, u32[]{:S(2)}) copy-start(f32[3,2,64,1024]{3,2,1,0:T(8,128)} %w.1) | copy-start | bytes 4718596
  20.8 17.1 %collective-permute-start.10 = (f32[192,1024]{1,0:T(8,128)S(1)}, f32[192,1024]{1,0:T(8,128)S(1)}, u32[]{:S(2)}, u32[]{:S(2)}) collective-permute-start(f32[192,1024]{1,0:T(8,128)S(1)} %get-tuple-element.49), channel_id=1, source_target_pairs={{8,16},{16,8},{9,17},{17,9},{10,18},{18,10},{11,19},{19,11},{12,20... | collective-permute-start | bytes 2359304 | tf_op jit(solution)/shard_map/ppermute | solution.py:28
  23.2 4.2 %collective-permute-start.5 = (f32[128,1024]{1,0:T(8,128)S(1)}, f32[128,1024]{1,0:T(8,128)S(1)}, u32[]{:S(2)}, u32[]{:S(2)}) collective-permute-start(f32[128,1024]{1,0:T(8,128)S(1)} %get-tuple-element.42), channel_id=1, source_target_pairs={{0,8},{8,0},{16,24},{24,16},{1,9},{9,1},{17,25},{25,17},{2,10},{10... | collective-permute-start | bytes 1572872 | tf_op jit(solution)/shard_map/ppermute | solution.py:28
  23.3 10.2 %collective-permute-start.6 = (f32[128,1024]{1,0:T(8,128)S(1)}, f32[128,1024]{1,0:T(8,128)S(1)}, u32[]{:S(2)}, u32[]{:S(2)}) collective-permute-start(f32[128,1024]{1,0:T(8,128)S(1)} %get-tuple-element.43), channel_id=1, source_target_pairs={{0,8},{8,0},{16,24},{24,16},{1,9},{9,1},{17,25},{25,17},{2,10},{10... | collective-permute-start | bytes 1572872 | tf_op jit(solution)/shard_map/ppermute | solution.py:28
  23.8 15.9 %collective-permute-start.9 = (f32[64,1024]{1,0:T(8,128)S(1)}, f32[64,1024]{1,0:T(8,128)S(1)}, u32[]{:S(2)}, u32[]{:S(2)}) collective-permute-start(f32[64,1024]{1,0:T(8,128)S(1)} %get-tuple-element.48), channel_id=1, source_target_pairs={{8,16},{16,8},{9,17},{17,9},{10,18},{18,10},{11,19},{19,11},{12,20... | collective-permute-start | bytes 786440 | tf_op jit(solution)/shard_map/ppermute | solution.py:28
  27.5 6.1 %collective-permute-start.7 = (f32[16,1024]{1,0:T(8,128)S(1)}, f32[16,1024]{1,0:T(8,128)S(1)}, u32[]{:S(2)}, u32[]{:S(2)}) collective-permute-start(f32[16,1024]{1,0:T(8,128)S(1)} %get-tuple-element.44), channel_id=1, source_target_pairs={{0,1},{1,0},{2,3},{3,2},{4,5},{5,4},{6,7},{7,6},{8,9},{9,8},{10,11... | collective-permute-start | bytes 196616 | tf_op jit(solution)/shard_map/ppermute | solution.py:28
  28.7 7.0 %collective-permute-start.8 = (f32[16,1024]{1,0:T(8,128)S(1)}, f32[16,1024]{1,0:T(8,128)S(1)}, u32[]{:S(2)}, u32[]{:S(2)}) collective-permute-start(f32[16,1024]{1,0:T(8,128)S(1)} %get-tuple-element.45), channel_id=1, source_target_pairs={{1,2},{2,1},{3,4},{4,3},{5,6},{6,5},{9,10},{10,9},{11,12},{12,11},... | collective-permute-start | bytes 196616 | tf_op jit(solution)/shard_map/ppermute | solution.py:28

commit v6 on v2

--- a/solution.py
+++ b/solution.py
@@ -1,3 +1,5 @@
+import functools
+
 import jax
 import jax.numpy as jnp
 from jax import lax
@@ -169,9 +171,10 @@
     by_side(body)
 
 
-def prepare_kernel(u, cls, before, stiff, cross, fixed, rim_a, rim_b, splat):
+def prepare_kernel(u, cls, shift, arrived, stiff, cross, fixed, rim_a, rim_b, splat, offsets):
     sections, _, rows, _ = u.shape
     last = slice(rows - 1, rows)
+    offsets[...] = shift[...]
     put_splat(stiff, cross, fixed, splat)
     table = splat[TABLE]
     put_rims(
@@ -196,7 +199,7 @@
     return values[0]
 
 
-def inside(u, w, total, half_across, half_below, shift, splat, scalars, sem):
+def inside(u, w, total, half_across, half_below, shift, splat, scalars, sem, forces):
     sections, _, rows, width = u.shape
     rbs, cbs = rows // ROWS, width // COLS
     load = pltpu.make_async_copy(shift, scalars, sem)
@@ -219,36 +222,49 @@
     lax.fori_loop(0, cbs, below, 0)
     load.wait()
     last = lax.broadcasted_iota(jnp.int32, (ROWS, width), 1) == width - 1
-
-    def row(rb, carry):
-        at = rows_of(rb)
-        add = [[total[s, c, at, :] for c in range(2)] for s in range(sections)]
-        for s in range(sections):
-            x, y = u[s, 0, at, :], u[s, 1, at, :]
-            half = jnp.where(last, 0.0, half_across(s, at))
-            f = flow(pltpu.roll(x, width - 1, 1) - x, pltpu.roll(y, width - 1, 1) - y, half)
-            for c in range(2):
-                add[s][c] = add[s][c] + (f[c] - pltpu.roll(f[c], 1, 1))
-        for hops in (1, 2):
-            half = wide_splat(splat, INSIDE + hops - 1, width)
-            for s in range(sections - hops):
-                offsets = [scalars[s, hops - 1, rb, cb] for cb in range(cbs)]
-                there = [(-o) & (COLS - 1) for o in offsets]
-                back = [o & (COLS - 1) for o in offsets]
-                e = [turned(u[s + hops, c, at, :], there) - u[s, c, at, :] for c in range(2)]
-                f = flow(e[0], e[1], half)
-                for c in range(2):
-                    add[s][c] = add[s][c] + f[c]
-                    add[s + hops][c] = add[s + hops][c] - turned(f[c], back)
-        for s in range(sections):
-            for c in range(2):
-                total[s, c, at, :] = add[s][c]
-        return carry
-
-    lax.fori_loop(0, rbs, row, 0)
-
-
-def first_inside_kernel(u, cls, shift, splat, total, half, scalars, sem):
+    pairs = [(s, hops) for hops in (1, 2) for s in range(sections - hops)]
+
+    def over_rows(body):
+        lax.fori_loop(0, rbs, lambda rb, carry: body(rb, rows_of(rb)) or carry, 0, unroll=True)
+
+    def put(k, s, at, f):
+        for c in range(2):
+            total[s, c, at, :] += f[c]
+            forces[k, c, at, :] = f[c]
+
+    def across(s, rb, at):
+        x, y = u[s, 0, at, :], u[s, 1, at, :]
+        half = jnp.where(last, 0.0, half_across(s, at))
+        f = flow(pltpu.roll(x, width - 1, 1) - x, pltpu.roll(y, width - 1, 1) - y, half)
+        put(len(pairs) + s, s, at, f)
+
+    def across_back(s, rb, at):
+        for c in range(2):
+            total[s, c, at, :] -= pltpu.roll(forces[len(pairs) + s, c, at, :], 1, 1)
+
+    def between(k, rb, at):
+        s, hops = pairs[k]
+        there = [(-scalars[s, hops - 1, rb, cb]) & (COLS - 1) for cb in range(cbs)]
+        e = [turned(u[s + hops, c, at, :], there) - u[s, c, at, :] for c in range(2)]
+        put(k, s, at, flow(e[0], e[1], wide_splat(splat, INSIDE + hops - 1, width)))
+
+    def between_back(k, rb, at):
+        s, hops = pairs[k]
+        back = [scalars[s, hops - 1, rb, cb] & (COLS - 1) for cb in range(cbs)]
+        for c in range(2):
+            total[s + hops, c, at, :] -= turned(forces[k, c, at, :], back)
+
+    for body, count in (
+        (across, sections),
+        (between, len(pairs)),
+        (across_back, sections),
+        (between_back, len(pairs)),
+    ):
+        for k in range(count):
+            over_rows(functools.partial(body, k))
+
+
+def first_inside_kernel(u, cls, shift, splat, total, half, scalars, sem, forces):
     table = splat[TABLE]
     values = [jnp.broadcast_to(table[:, k : k + 1], (ROWS, COLS)) for k in range(CLASSES)]
     rows = u.shape[2]
@@ -267,25 +283,25 @@
         half[s, 1, :, at] = k
         return k
 
-    inside(u, None, total, half_across, half_below, shift, splat, scalars, sem)
-
-
-def later_inside_kernel(u, w, half, shift, splat, total, scalars, sem):
+    inside(u, None, total, half_across, half_below, shift, splat, scalars, sem, forces)
+
+
+def later_inside_kernel(u, w, half, shift, splat, total, scalars, sem, forces):
     def half_across(s, at):
         return half[s, 0, at, :]
 
     def half_below(s, at):
         return half[s, 1, :, at]
 
-    inside(u, w, total, half_across, half_below, shift, splat, scalars, sem)
-
-
-def side_flow(u, own, arrived, first, index, j, half, rb):
-    rows = u.shape[2]
+    inside(u, w, total, half_across, half_below, shift, splat, scalars, sem, forces)
+
+
+def side_flow(u, own, arrived, block, height, base, index, j, half, rb):
     at = rows_of(rb)
     number = index[j, rb : rb + 1, :]
     e = [
-        gathered(arrived[pl.ds(first + c * rows + rb * ROWS, ROWS), :], number) - u[own, c, at, :]
+        gathered(arrived[pl.ds((2 * block + c) * height + rb * ROWS - base, ROWS), :], number)
+        - u[own, c, at, :]
         for c in range(2)
     ]
     return flow(e[0], e[1], half)
@@ -321,12 +337,14 @@
         own, block, hops = pairs_of(after, sections)[j]
         stiff = wide_splat(splat, FAST + hops - 1, width)
         for rb in range(rows // ROWS):
-            f = side_flow(u, own, fast, 2 * block * rows, index, j, stiff, rb)
+            f = side_flow(u, own, fast, block, rows, 0, index, j, stiff, rb)
             for c in range(2):
                 total[own, c, rows_of(rb), :] += f[c]
 
 
-def first_rims_kernel(u, w, total_in, half, fast, rim_a, rim_b, shift, before, splat, total, index):
+def first_rims_kernel(
+    u, w, total_in, half, fast, rim_a, rim_b, shift, before, splat, total, index
+):
     sections, _, rows, _ = u.shape
 
     def damp(rb, carry):
@@ -347,7 +365,8 @@
 
 
 def later_rims_kernel(
-    u, total_in, half, fast, rim_a, rim_b, index, splat, total, out_u, out_w, new_u, new_w, sem
+    u, total_in, half, fast, rim_a, rim_b, index, splat,
+    total, out_u, out_w, new_u, new_w, sem,
 ):
     sections, _, rows, width = u.shape
 
@@ -379,14 +398,14 @@
     by_side(body)
 
 
-def slow_values(u, after, arrived, index, splat, total, j, rb):
+def slow_values(u, after, arrived, height, base, index, splat, total, j, rb):
     sections, _, rows, width = u.shape
     own = pairs_of(after, sections)[j][0]
     value = [total[own, c, rows_of(rb), :] for c in range(2)]
     for p, (section, block, hops) in enumerate(pairs_of(after, sections)):
         if section == own:
             stiff = wide_splat(splat, SLOW + hops - 1, width)
-            f = side_flow(u, own, arrived, 2 * block * rows, index, p, stiff, rb)
+            f = side_flow(u, own, arrived, block, height, base, index, p, stiff, rb)
             value = [value[c] + f[c] for c in range(2)]
     return value
 
@@ -404,9 +423,11 @@
         for s in range(sections):
             moving = wide_splat(splat, MOVING + s, width)
             for rb in range(rows // ROWS):
-                at = rows_of(rb)
+                at, row = rows_of(rb), rb * ROWS
                 if s in slow_edge:
-                    value = slow_values(u, after, arrived, index, splat, total, slow_edge.index(s), rb)
+                    value = slow_values(
+                        u, after, arrived, rows, 0, index, splat, total, slow_edge.index(s), rb
+                    )
                 else:
                     value = [total[s, c, at, :] for c in range(2)]
                 for c in range(2):
@@ -416,8 +437,7 @@
                     new_u[s, c, at, :] = moved
                     for edge, out in ((slow_edge, slow), (fast_edge, fast)):
                         if s in edge:
-                            first = (2 * edge.index(s) + c) * rows
-                            out[pl.ds(first + rb * ROWS, ROWS), :] = moved
+                            out[pl.ds((2 * edge.index(s) + c) * rows + row, ROWS), :] = moved
 
     by_side(body)
     last = slice(rows - 1, rows)
@@ -431,9 +451,12 @@
     )
 
 
-def last_kernel(u, total, arrived, index, splat, out_u_in, out_w_in, out_u, out_w, new_u, new_w, sem):
-    sections, _, rows, width = u.shape
-    rbs = rows // ROWS
+def last_kernel(
+    base, u, total, arrived, index, splat, out_u_in, out_w_in, out_u, out_w, new_u, new_w, sem
+):
+    sections, _, rows, width = u.shape
+    height = arrived.shape[0] // 4
+    rbs = height // ROWS
     part = rbs // 2 if rbs % 2 == 0 else rbs
 
     def body(after):
@@ -441,18 +464,19 @@
         for j in range(2):
             own = pairs_of(after, sections)[j][0]
             moving = wide_splat(splat, MOVING + own, width)
-            for rb in range(rbs):
-                at = rows_of(rb)
-                value = slow_values(u, after, arrived, index, splat, total, j, rb)
+            for k in range(rbs):
+                rb = base // ROWS + k
+                value = slow_values(u, after, arrived, height, base, index, splat, total, j, rb)
                 for c in range(2):
                     v = value[c] * moving
-                    new_w[j, c, at, :] = v
-                    new_u[j, c, at, :] = u[own, c, at, :] + STEP * v
-                if (rb + 1) % part == 0:
-                    block = pl.ds((rb + 1 - part) * ROWS, part * ROWS)
+                    new_w[j, c, rows_of(k), :] = v
+                    new_u[j, c, rows_of(k), :] = u[own, c, rows_of(rb), :] + STEP * v
+                if (k + 1) % part == 0:
+                    here = pl.ds((k + 1 - part) * ROWS, part * ROWS)
+                    there = pl.ds(base + (k + 1 - part) * ROWS, part * ROWS)
                     for source, target in ((new_u, out_u), (new_w, out_w)):
                         copy = pltpu.make_async_copy(
-                            source.at[j, :, block], target.at[own, :, block], sem.at[len(copies)]
+                            source.at[j, :, here], target.at[own, :, there], sem.at[len(copies)]
                         )
                         copy.start()
                         copies.append(copy)
@@ -486,20 +510,24 @@
     rim = array(-(-3 * sections // ROWS) * ROWS, width)
     splat = array(MOVING + sections, ROWS, COLS)
     index = array(3, tail_rows(rows), width, dtype=jnp.int32)
-    scalars = [pltpu.SMEM(shift.shape, jnp.int32), pltpu.SemaphoreType.DMA]
+    scalars = [
+        pltpu.SMEM(shift.shape, jnp.int32),
+        pltpu.SemaphoreType.DMA,
+        pltpu.VMEM((3 * sections - 3,) + u.shape[1:], jnp.float32),
+    ]
     smem = pl.BlockSpec(memory_space=pltpu.SMEM)
 
-    n = lax.axis_size("sec")
-    before = lax.ppermute(shift, "sec", [(i, i + 1) for i in range(n - 1)])
     slow, fast = call(lead_kernel, [two, two], [u])
     slow = exchange(slow, "sec", "b")
     fast = exchange(fast, "sec", "a")
-    rim_a, rim_b, splat = call(
+    rim_a, rim_b, splat, offsets = call(
         prepare_kernel,
-        [rim, rim, splat],
-        [u, cls, before, stiff, cross, fixed],
-        in_specs=[VMEM] * 3 + [smem] * 3,
-    )
+        [rim, rim, splat, array(*shift.shape, dtype=jnp.int32)],
+        [u, cls, shift, fast, stiff, cross, fixed],
+        in_specs=[VMEM] * 3 + [ANY] + [smem] * 3,
+    )
+    before_fast = exchange(offsets, "sec", "a")
+    before_slow = exchange(offsets, "sec", "b")
     rim_a = exchange(rim_a, "strip", "a")
     rim_b = exchange(rim_b, "strip", "b")
     total, half = call(
@@ -508,13 +536,13 @@
     total, fast_index = call(
         first_rims_kernel,
         [full, index],
-        [u, w, total, half, fast, rim_a, rim_b, shift, before, splat],
+        [u, w, total, half, fast, rim_a, rim_b, shift, before_fast, splat],
         {2: 0},
     )
     u, w, slow, fast, index, rim_a, rim_b = call(
         step_kernel,
         [full, full, two, two, index, rim, rim],
-        [u, total, slow, half, shift, before, splat],
+        [u, total, slow, half, shift, before_slow, splat],
     )
     slow = exchange(slow, "sec", "b")
     fast = exchange(fast, "sec", "a")
@@ -527,13 +555,14 @@
         [full, full, full],
         [u, total, half, fast, rim_a, rim_b, fast_index, splat],
         {1: 0},
+        in_specs=[VMEM] * 8,
         scratch=[pltpu.VMEM((done, 2, rows, width), jnp.float32)] * 2
         + [pltpu.SemaphoreType.DMA((2 * done,))],
         out_specs=[VMEM, ANY, ANY],
     )
     return tuple(
         call(
-            last_kernel,
+            functools.partial(last_kernel, 0),
             [full, full],
             [u, total, slow, index, splat, out_u, out_w],
             {5: 0, 6: 1},

time: 50.4 us -> 40.2 us (0.80)
  waiting for transfers between devices: 11.7 us -> 4.42 us
  Pallas kernels: 15.8 us -> 13.8 us
  starting transfers between devices: 20.3 us -> 18.5 us
  local copies, waits for them, and re-layouts: 1.43 us -> 2.16 us
    ppermute x1 -> x0, waiting for transfers between devices: 9.48 us -> none  [per_device(): before = lax.ppermute(shift, 'sec', [(i, i + 1) for i in range(n - 1)])]
    ppermute x1 -> x0, starting transfers between devices: 2.5 us -> none  [per_device(): before = lax.ppermute(shift, 'sec', [(i, i + 1) for i in range(n - 1)])]
    ppermute x8 -> x10, waiting for transfers between devices: 2.22 us -> 4.42 us  [exchange(): return lax.ppermute(value, axis, route)]
    pallas_call x8, Pallas kernels: 15.8 us -> 13.8 us  [call(): pl.pallas_call(kernel, out_shape=outs, in_specs=in_specs or [VMEM] * len(...]
    unnamed x14 -> x16, local copies, waits for them, and re-layouts: 1.43 us -> 2.16 us
    ppermute x8 -> x10, starting transfers between devices: 17.8 us -> 18.5 us  [exchange(): return lax.ppermute(value, axis, route)]
  transfers between devices with their start and end apart: 9 -> 10, of which waited for: 2 -> 1; matrix products, arithmetic and copies ran while one was open for 0% -> 0% of each run, Pallas kernels for 24% -> 26%
where the time goes in v6:
time: 40.2 us; the launch traced here: 39.9 us
  starting transfers between devices  18.5 us (46%)
  Pallas kernels  13.8 us (34%)
  waiting for transfers between devices  4.42 us (11%)
  local copies, waits for them, and re-layouts  2.16 us (5%)
  between operations  1.05 us (3%)
    ppermute x10, starting transfers between devices, exchange(): return lax.ppermute(value, axis, route)  18.5 us
    pallas_call x8, Pallas kernels, call(): pl.pallas_call(kernel, out_shape=outs, in_specs=in_specs or [VMEM] * len(...  13.8 us
    ppermute x10, waiting for transfers between devices, exchange(): return lax.ppermute(value, axis, route)  4.42 us
    unnamed x16, local copies, waits for them, and re-layouts  2.16 us
  transfers between devices with their start and end apart: 10, of which 1 were waited for; matrix products, arithmetic and copies ran while one was open for 0% of the time, Pallas kernels for 26%

profile of v6, /device:TPU:3, one launch (start us, length us, event | category | flops | bytes accessed | tf_op | source)
XLA Modules:
  0.0 39.9 jit_solution(9227778332300538434)
XLA Ops:
  0.6 0.0 copy-start
  0.6 1.4 %copy-done = f32[3,2,64,1024]{3,2,1,0:T(8,128)S(1)} copy-done((f32[3,2,64,1024]{3,2,1,0:T(8,128)S(1)}, f32[3,2,64,1024]{3,2,1,0:T(8,128)}, u32[]{:S(2)}) %copy-start) | copy-done | bytes 1572888
  2.0 0.0 copy-start.1
  2.0 0.0 copy-start.5
  2.0 0.0 copy-start.6
  2.0 0.0 copy-start.7
  2.1 0.2 shard_map.86
  2.2 0.7 %collective-permute-start = (f32[256,1024]{1,0:T(8,128)S(1)}, f32[256,1024]{1,0:T(8,128)S(1)}, u32[]{:S(2)}, u32[]{:S(2)}) collective-permute-start(f32[256,1024]{1,0:T(8,128)S(1)} %get-tuple-element.22), channel_id=1, source_target_pairs={{0,8},{8,0},{16,24},{24,16},{1,9},{9,1},{17,25},{25,17},{2,10},{10... | collective-permute-start | bytes 3145736 | tf_op jit(solution)/shard_map/ppermute | solution.py:28
  3.0 3.2 %collective-permute-start.4 = (f32[256,1024]{1,0:T(8,128)S(1)}, f32[256,1024]{1,0:T(8,128)S(1)}, u32[]{:S(2)}, u32[]{:S(2)}) collective-permute-start(f32[256,1024]{1,0:T(8,128)S(1)} %get-tuple-element.30), channel_id=1, source_target_pairs={{8,16},{16,8},{9,17},{17,9},{10,18},{18,10},{11,19},{19,11},{12,20... | collective-permute-start | bytes 3145736 | tf_op jit(solution)/shard_map/ppermute | solution.py:28
  6.1 0.0 collective-permute-done.arrived.fast
  6.2 0.0 copy-done.1
  6.2 0.0 copy-done.5
  6.2 0.0 copy-done.6
  6.2 0.0 copy-done.7
  6.2 0.0 copy-start.3
  6.2 0.7 %copy-done.3 = s32[3,2,8,8]{3,2,1,0:T(8,128)S(1)} copy-done((s32[3,2,8,8]{3,2,1,0:T(8,128)S(1)}, s32[3,2,8,8]{3,2,1,0:T(8,128)}, u32[]{:S(2)}) %copy-start.3) | copy-done | bytes 1560
  6.9 0.0 copy-start.4
  6.9 0.7 %shard_map.87 = (f32[16,1024]{1,0:T(8,128)S(1)}, f32[16,1024]{1,0:T(8,128)S(1)}, f32[10,8,128]{2,1,0:T(8,128)S(1)}, s32[3,2,8,8]{3,2,1,0:T(8,128)S(1)}) custom-call(f32[3,2,64,1024]{3,2,1,0:T(8,128)S(1)} %copy-done, s32[3,2,64,1024]{3,2,1,0:T(8,128)S(1)} %copy-done.1, s32[3,2,8,8]{3,2,1,0:T(8,128)S(1)} %copy-done.3, ...), custom_call_target="tpu_custom_call" | custom-call | tf_op jit(solution)/shard_map/pallas_call | solution.py:490
  7.6 0.3 collective-permute-start.1
  7.9 4.1 %collective-permute-start.2 = (f32[16,1024]{1,0:T(8,128)S(1)}, f32[16,1024]{1,0:T(8,128)S(1)}, u32[]{:S(2)}, u32[]{:S(2)}) collective-permute-start(f32[16,1024]{1,0:T(8,128)S(1)} %get-tuple-element.27), channel_id=1, source_target_pairs={{1,2},{2,1},{3,4},{4,3},{5,6},{6,5},{9,10},{10,9},{11,12},{12,11},... | collective-permute-start | bytes 196616 | tf_op jit(solution)/shard_map/ppermute | solution.py:28
  12.1 0.1 collective-permute-start.3
  12.1 3.0 %collective-permute-start.5 = (s32[3,2,8,8]{3,2,1,0:T(8,128)S(1)}, s32[3,2,8,8]{3,2,1,0:T(8,128)S(1)}, u32[]{:S(2)}, u32[]{:S(2)}) collective-permute-start(s32[3,2,8,8]{3,2,1,0:T(8,128)S(1)} %get-tuple-element.28), channel_id=1, source_target_pairs={{8,16},{16,8},{9,17},{17,9},{10,18},{18,10},{11,19},{19,11},{12,20... | collective-permute-start | bytes 4616 | tf_op jit(solution)/shard_map/ppermute | solution.py:28
  15.2 0.0 copy-done.4
  15.2 0.0 copy-start.2
  15.2 3.2 %shard_map.88 = (f32[3,2,64,1024]{3,2,1,0:T(8,128)S(1)}, f32[3,2,64,1024]{3,2,1,0:T(8,128)S(1)}) custom-call(f32[3,2,64,1024]{3,2,1,0:T(8,128)S(1)} %copy-done, s32[3,2,64,1024]{3,2,1,0:T(8,128)S(1)} %copy-done.1, s32[3,2,8,8]{3,2,1,0:T(8,128)S(1)} %copy-done.4, f32[10,8,128]{2,1,0:T(8,128)S(1)} %get-tuple-element.23.splat), custom_call_target="tpu_custom_call" | custom-call | tf_op jit(solution)/shard_map/pallas_call | solution.py:490
  18.5 0.0 collective-permute-done.3.before
  18.5 0.0 collective-permute-done.1.rim_a
  18.5 0.0 collective-permute-done.2.rim_b
  18.5 0.0 copy-done.2
  18.5 1.6 %shard_map.89 = (f32[3,2,64,1024]{3,2,1,0:T(8,128)S(1)}, s32[3,8,1024]{2,1,0:T(8,128)S(1)}) custom-call(f32[3,2,64,1024]{3,2,1,0:T(8,128)S(1)} %copy-done, f32[3,2,64,1024]{3,2,1,0:T(8,128)S(1)} %copy-done.2, f32[3,2,64,1024]{3,2,1,0:T(8,128)S(1)} %get-tuple-element.24.total_in, ...), custom_call_target="tpu_custom_call", output_to_operand_aliasing={{0}: (2, {})} | custom-call | tf_op jit(solution)/shard_map/pallas_call | solution.py:490
  20.1 0.0 collective-permute-done.4.arrived
  20.1 0.0 collective-permute-done.5.before
  20.1 1.4 %shard_map.90 = (f32[3,2,64,1024]{3,2,1,0:T(8,128)S(1)}, f32[3,2,64,1024]{3,2,1,0:T(8,128)S(1)}, f32[256,1024]{1,0:T(8,128)S(1)}, f32[256,1024]{1,0:T(8,128)S(1)...) custom-call(f32[3,2,64,1024]{3,2,1,0:T(8,128)S(1)} %copy-done, ...), custom_call_target="tpu_custom_call" | custom-call | tf_op jit(solution)/shard_map/pallas_call | solution.py:490
  21.5 0.1 collective-permute-start.6
  21.6 2.5 %collective-permute-start.9 = (f32[256,1024]{1,0:T(8,128)S(1)}, f32[256,1024]{1,0:T(8,128)S(1)}, u32[]{:S(2)}, u32[]{:S(2)}) collective-permute-start(f32[256,1024]{1,0:T(8,128)S(1)} %get-tuple-element.38), channel_id=1, source_target_pairs={{8,16},{16,8},{9,17},{17,9},{10,18},{18,10},{11,19},{19,11},{12,20... | collective-permute-start | bytes 3145736 | tf_op jit(solution)/shard_map/ppermute | solution.py:28
  24.1 0.2 collective-permute-start.7
  24.3 4.3 %collective-permute-start.8 = (f32[16,1024]{1,0:T(8,128)S(1)}, f32[16,1024]{1,0:T(8,128)S(1)}, u32[]{:S(2)}, u32[]{:S(2)}) collective-permute-start(f32[16,1024]{1,0:T(8,128)S(1)} %get-tuple-element.35), channel_id=1, source_target_pairs={{1,2},{2,1},{3,4},{4,3},{5,6},{6,5},{9,10},{10,9},{11,12},{12,11},... | collective-permute-start | bytes 196616 | tf_op jit(solution)/shard_map/ppermute | solution.py:28
  28.6 2.8 %shard_map.91.total_in = f32[3,2,64,1024]{3,2,1,0:T(8,128)S(1)} custom-call(f32[3,2,64,1024]{3,2,1,0:T(8,128)S(1)} %get-tuple-element.31.u, f32[3,2,64,1024]{3,2,1,0:T(8,128)S(1)} %get-tuple-element.32.w, f32[3,2,64,1024]{3,2,1,0:T(8,128)S(1)} %get-tuple-element.25.half, s32[3,2,8,8]{3,2,1,0:T(8,128)S(1)} %copy-done.4, f32[10,8,128]{2,1,0:T(8,128)S(1)} %get-tuple-element.23.splat), custom_call_target="tpu_custom_call" | custom-call | tf_op jit(solution)/shard_map/pallas_call | solution.py:490
  31.4 0.0 collective-permute-done.7.rim_a
  31.4 0.0 collective-permute-done.8.rim_b
  31.4 0.0 collective-permute-done.6.fast
  31.4 1.9 %shard_map.92 = (f32[3,2,64,1024]{3,2,1,0:T(8,128)S(1)}, f32[3,2,64,1024]{3,2,1,0:T(8,128)}, f32[3,2,64,1024]{3,2,1,0:T(8,128)}) custom-call(f32[3,2,64,1024]{3,2,1,0:T(8,128)S(1)} %get-tuple-element.31.u, f32[3,2,64,1024]{3,2,1,0:T(8,128)S(1)} %shard_map.91.total_in, ...), custom_call_target="tpu_custom_call", output_to_operand_aliasing={{0}: (1, {})} | custom-call | tf_op jit(solution)/shard_map/pallas_call | solution.py:490
  33.3 4.4 %collective-permute-done.9.arrived = f32[256,1024]{1,0:T(8,128)S(1)} collective-permute-done((f32[256,1024]{1,0:T(8,128)S(1)}, f32[256,1024]{1,0:T(8,128)S(1)}, u32[]{:S(2)}, u32[]{:S(2)}) %collective-permute-start.9) | collective-permute-done | bytes 1048608 | tf_op jit(solution)/shard_map/ppermute | solution.py:28
  37.7 2.0 %shard_map.93 = (f32[3,2,64,1024]{3,2,1,0:T(8,128)}, f32[3,2,64,1024]{3,2,1,0:T(8,128)}) custom-call(f32[3,2,64,1024]{3,2,1,0:T(8,128)S(1)} %get-tuple-element.31.u, f32[3,2,64,1024]{3,2,1,0:T(8,128)S(1)} %get-tuple-element.37.total, f32[256,1024]{1,0:T(8,128)S(1)} %collective-permute-done.9.arrived, ...), custom_call_target="tpu_custom_call", output_to_operand_aliasing={{0}: (5, {}), {1}: (6, {})} | custom-call | tf_op jit(solution)/shard_map/pallas_call | solution.py:490
Async XLA Ops:
  0.6 1.4 %copy-start = (f32[3,2,64,1024]{3,2,1,0:T(8,128)S(1)}, f32[3,2,64,1024]{3,2,1,0:T(8,128)}, u32[]{:S(2)}) copy-start(f32[3,2,64,1024]{3,2,1,0:T(8,128)} %u.9) | copy-start | bytes 4718596
  2.0 4.1 %copy-start.1 = (s32[3,2,64,1024]{3,2,1,0:T(8,128)S(1)}, s32[3,2,64,1024]{3,2,1,0:T(8,128)}, u32[]{:S(2)}) copy-start(s32[3,2,64,1024]{3,2,1,0:T(8,128)} %cls.3) | copy-start | bytes 4718596
  2.0 4.1 %copy-start.5 = (f32[8]{0:T(128)S(1)}, f32[8]{0:T(128)}, u32[]{:S(2)}) copy-start(f32[8]{0:T(128)} %stiff.1) | copy-start | bytes 100
  2.0 4.1 %copy-start.6 = (f32[2]{0:T(128)S(1)}, f32[2]{0:T(128)}, u32[]{:S(2)}) copy-start(f32[2]{0:T(128)} %cross.1) | copy-start | bytes 28
  2.0 4.1 %copy-start.7 = (s32[3]{0:T(128)S(1)}, s32[3]{0:T(128)}, u32[]{:S(2)}) copy-start(s32[3]{0:T(128)} %fixed.1) | copy-start | bytes 40
  2.2 3.9 %collective-permute-start = (f32[256,1024]{1,0:T(8,128)S(1)}, f32[256,1024]{1,0:T(8,128)S(1)}, u32[]{:S(2)}, u32[]{:S(2)}) collective-permute-start(f32[256,1024]{1,0:T(8,128)S(1)} %get-tuple-element.22), channel_id=1, source_target_pairs={{0,8},{8,0},{16,24},{24,16},{1,9},{9,1},{17,25},{25,17},{2,10},{10... | collective-permute-start | bytes 3145736 | tf_op jit(solution)/shard_map/ppermute | solution.py:28
  3.0 17.2 %collective-permute-start.4 = (f32[256,1024]{1,0:T(8,128)S(1)}, f32[256,1024]{1,0:T(8,128)S(1)}, u32[]{:S(2)}, u32[]{:S(2)}) collective-permute-start(f32[256,1024]{1,0:T(8,128)S(1)} %get-tuple-element.30), channel_id=1, source_target_pairs={{8,16},{16,8},{9,17},{17,9},{10,18},{18,10},{11,19},{19,11},{12,20... | collective-permute-start | bytes 3145736 | tf_op jit(solution)/shard_map/ppermute | solution.py:28
  6.2 0.7 %copy-start.3 = (s32[3,2,8,8]{3,2,1,0:T(8,128)S(1)}, s32[3,2,8,8]{3,2,1,0:T(8,128)}, u32[]{:S(2)}) copy-start(s32[3,2,8,8]{3,2,1,0:T(8,128)} %shift.9) | copy-start | bytes 4612
  6.9 8.3 %copy-start.4 = (s32[3,2,8,8]{3,2,1,0:T(8,128)S(1)}, s32[3,2,8,8]{3,2,1,0:T(8,128)}, u32[]{:S(2)}) copy-start(s32[3,2,8,8]{3,2,1,0:T(8,128)} %shift.9) | copy-start | bytes 4612
  7.6 10.9 %collective-permute-start.1 = (f32[16,1024]{1,0:T(8,128)S(1)}, f32[16,1024]{1,0:T(8,128)S(1)}, u32[]{:S(2)}, u32[]{:S(2)}) collective-permute-start(f32[16,1024]{1,0:T(8,128)S(1)} %get-tuple-element.26), channel_id=1, source_target_pairs={{0,1},{1,0},{2,3},{3,2},{4,5},{5,4},{6,7},{7,6},{8,9},{9,8},{10,11... | collective-permute-start | bytes 196616 | tf_op jit(solution)/shard_map/ppermute | solution.py:28
  7.9 10.6 %collective-permute-start.2 = (f32[16,1024]{1,0:T(8,128)S(1)}, f32[16,1024]{1,0:T(8,128)S(1)}, u32[]{:S(2)}, u32[]{:S(2)}) collective-permute-start(f32[16,1024]{1,0:T(8,128)S(1)} %get-tuple-element.27), channel_id=1, source_target_pairs={{1,2},{2,1},{3,4},{4,3},{5,6},{6,5},{9,10},{10,9},{11,12},{12,11},... | collective-permute-start | bytes 196616 | tf_op jit(solution)/shard_map/ppermute | solution.py:28
  12.1 6.4 %collective-permute-start.3 = (s32[3,2,8,8]{3,2,1,0:T(8,128)S(1)}, s32[3,2,8,8]{3,2,1,0:T(8,128)S(1)}, u32[]{:S(2)}, u32[]{:S(2)}) collective-permute-start(s32[3,2,8,8]{3,2,1,0:T(8,128)S(1)} %get-tuple-element.28), channel_id=1, source_target_pairs={{0,8},{8,0},{16,24},{24,16},{1,9},{9,1},{17,25},{25,17},{2,10},{10... | collective-permute-start | bytes 4616 | tf_op jit(solution)/shard_map/ppermute | solution.py:28
  12.1 8.0 %collective-permute-start.5 = (s32[3,2,8,8]{3,2,1,0:T(8,128)S(1)}, s32[3,2,8,8]{3,2,1,0:T(8,128)S(1)}, u32[]{:S(2)}, u32[]{:S(2)}) collective-permute-start(s32[3,2,8,8]{3,2,1,0:T(8,128)S(1)} %get-tuple-element.28), channel_id=1, source_target_pairs={{8,16},{16,8},{9,17},{17,9},{10,18},{18,10},{11,19},{19,11},{12,20... | collective-permute-start | bytes 4616 | tf_op jit(solution)/shard_map/ppermute | solution.py:28
  15.2 3.3 %copy-start.2 = (f32[3,2,64,1024]{3,2,1,0:T(8,128)S(1)}, f32[3,2,64,1024]{3,2,1,0:T(8,128)}, u32[]{:S(2)}) copy-start(f32[3,2,64,1024]{3,2,1,0:T(8,128)} %w.1) | copy-start | bytes 4718596
  21.5 9.9 %collective-permute-start.6 = (f32[256,1024]{1,0:T(8,128)S(1)}, f32[256,1024]{1,0:T(8,128)S(1)}, u32[]{:S(2)}, u32[]{:S(2)}) collective-permute-start(f32[256,1024]{1,0:T(8,128)S(1)} %get-tuple-element.33), channel_id=1, source_target_pairs={{0,8},{8,0},{16,24},{24,16},{1,9},{9,1},{17,25},{25,17},{2,10},{10... | collective-permute-start | bytes 3145736 | tf_op jit(solution)/shard_map/ppermute | solution.py:28
  21.6 16.1 %collective-permute-start.9 = (f32[256,1024]{1,0:T(8,128)S(1)}, f32[256,1024]{1,0:T(8,128)S(1)}, u32[]{:S(2)}, u32[]{:S(2)}) collective-permute-start(f32[256,1024]{1,0:T(8,128)S(1)} %get-tuple-element.38), channel_id=1, source_target_pairs={{8,16},{16,8},{9,17},{17,9},{10,18},{18,10},{11,19},{19,11},{12,20... | collective-permute-start | bytes 3145736 | tf_op jit(solution)/shard_map/ppermute | solution.py:28
  24.1 7.3 %collective-permute-start.7 = (f32[16,1024]{1,0:T(8,128)S(1)}, f32[16,1024]{1,0:T(8,128)S(1)}, u32[]{:S(2)}, u32[]{:S(2)}) collective-permute-start(f32[16,1024]{1,0:T(8,128)S(1)} %get-tuple-element.34), channel_id=1, source_target_pairs={{0,1},{1,0},{2,3},{3,2},{4,5},{5,4},{6,7},{7,6},{8,9},{9,8},{10,11... | collective-permute-start | bytes 196616 | tf_op jit(solution)/shard_map/ppermute | solution.py:28
  24.3 7.2 %collective-permute-start.8 = (f32[16,1024]{1,0:T(8,128)S(1)}, f32[16,1024]{1,0:T(8,128)S(1)}, u32[]{:S(2)}, u32[]{:S(2)}) collective-permute-start(f32[16,1024]{1,0:T(8,128)S(1)} %get-tuple-element.35), channel_id=1, source_target_pairs={{1,2},{2,1},{3,4},{4,3},{5,6},{6,5},{9,10},{10,9},{11,12},{12,11},... | collective-permute-start | bytes 196616 | tf_op jit(solution)/shard_map/ppermute | solution.py:28

commit v7 on v6

--- a/solution.py
+++ b/solution.py
@@ -171,10 +171,9 @@
     by_side(body)
 
 
-def prepare_kernel(u, cls, shift, arrived, stiff, cross, fixed, rim_a, rim_b, splat, offsets):
+def prepare_kernel(u, cls, arrived, stiff, cross, fixed, rim_a, rim_b, splat):
     sections, _, rows, _ = u.shape
     last = slice(rows - 1, rows)
-    offsets[...] = shift[...]
     put_splat(stiff, cross, fixed, splat)
     table = splat[TABLE]
     put_rims(
@@ -520,14 +519,14 @@
     slow, fast = call(lead_kernel, [two, two], [u])
     slow = exchange(slow, "sec", "b")
     fast = exchange(fast, "sec", "a")
-    rim_a, rim_b, splat, offsets = call(
+    rim_a, rim_b, splat = call(
         prepare_kernel,
-        [rim, rim, splat, array(*shift.shape, dtype=jnp.int32)],
-        [u, cls, shift, fast, stiff, cross, fixed],
-        in_specs=[VMEM] * 3 + [ANY] + [smem] * 3,
-    )
-    before_fast = exchange(offsets, "sec", "a")
-    before_slow = exchange(offsets, "sec", "b")
+        [rim, rim, splat],
+        [u, cls, fast, stiff, cross, fixed],
+        in_specs=[VMEM] * 2 + [ANY] + [smem] * 3,
+    )
+    before_fast = exchange(shift, "sec", "a")
+    before_slow = exchange(shift, "sec", "b")
     rim_a = exchange(rim_a, "strip", "a")
     rim_b = exchange(rim_b, "strip", "b")
     total, half = call(

time: 40.2 us -> 39.7 us (0.988)
  local copies, waits for them, and re-layouts: 2.16 us -> 1.43 us
  starting transfers between devices: 18.5 us -> 19.1 us
  waiting for transfers between devices: 4.42 us -> 3.93 us
    unnamed x16 -> x14, local copies, waits for them, and re-layouts: 2.16 us -> 1.43 us
    ppermute x10, starting transfers between devices: 18.5 us -> 19.1 us  [exchange(): return lax.ppermute(value, axis, route)]
    ppermute x10, waiting for transfers between devices: 4.42 us -> 3.93 us  [exchange(): return lax.ppermute(value, axis, route)]
  transfers between devices with their start and end apart: 10 -> 10, of which waited for: 1 -> 2; matrix products, arithmetic and copies ran while one was open for 0% -> 0% of each run, Pallas kernels for 26% -> 26%
where the time goes in v7:
time: 39.7 us; the launch traced here: 39.2 us
  starting transfers between devices  19.1 us (48%)
  Pallas kernels  13.8 us (35%)
  waiting for transfers between devices  3.93 us (10%)
  local copies, waits for them, and re-layouts  1.43 us (4%)
  between operations  1.03 us (3%)
    ppermute x10, starting transfers between devices, exchange(): return lax.ppermute(value, axis, route)  19.1 us
    pallas_call x8, Pallas kernels, call(): pl.pallas_call(kernel, out_shape=outs, in_specs=in_specs or [VMEM] * len(...  13.8 us
    ppermute x10, waiting for transfers between devices, exchange(): return lax.ppermute(value, axis, route)  3.93 us
    unnamed x14, local copies, waits for them, and re-layouts  1.43 us
  transfers between devices with their start and end apart: 10, of which 2 were waited for; matrix products, arithmetic and copies ran while one was open for 0% of the time, Pallas kernels for 26%

profile of v7, /device:TPU:3, one launch (start us, length us, event | category | flops | bytes accessed | tf_op | source)
XLA Modules:
  0.0 39.2 jit_solution(15689428965367100577)
XLA Ops:
  0.6 0.0 copy-start
  0.6 1.4 %copy-done = f32[3,2,64,1024]{3,2,1,0:T(8,128)S(1)} copy-done((f32[3,2,64,1024]{3,2,1,0:T(8,128)S(1)}, f32[3,2,64,1024]{3,2,1,0:T(8,128)}, u32[]{:S(2)}) %copy-start) | copy-done | bytes 1572888
  2.0 0.0 copy-start.1
  2.0 0.0 copy-start.4
  2.0 0.0 copy-start.5
  2.0 0.0 copy-start.6
  2.1 0.2 shard_map.86
  2.2 0.7 %collective-permute-start = (f32[256,1024]{1,0:T(8,128)S(1)}, f32[256,1024]{1,0:T(8,128)S(1)}, u32[]{:S(2)}, u32[]{:S(2)}) collective-permute-start(f32[256,1024]{1,0:T(8,128)S(1)} %get-tuple-element.21), channel_id=1, source_target_pairs={{0,8},{8,0},{16,24},{24,16},{1,9},{9,1},{17,25},{25,17},{2,10},{10... | collective-permute-start | bytes 3145736 | tf_op jit(solution)/shard_map/ppermute | solution.py:28
  3.0 0.0 copy-start.3
  3.0 3.2 %collective-permute-start.4 = (f32[256,1024]{1,0:T(8,128)S(1)}, f32[256,1024]{1,0:T(8,128)S(1)}, u32[]{:S(2)}, u32[]{:S(2)}) collective-permute-start(f32[256,1024]{1,0:T(8,128)S(1)} %get-tuple-element.28), channel_id=1, source_target_pairs={{8,16},{16,8},{9,17},{17,9},{10,18},{18,10},{11,19},{19,11},{12,20... | collective-permute-start | bytes 3145736 | tf_op jit(solution)/shard_map/ppermute | solution.py:28
  6.2 0.0 collective-permute-done.arrived.fast
  6.2 0.0 copy-done.1
  6.2 0.0 copy-done.4
  6.2 0.0 copy-done.5
  6.2 0.0 copy-done.6
  6.2 0.7 %shard_map.87 = (f32[16,1024]{1,0:T(8,128)S(1)}, f32[16,1024]{1,0:T(8,128)S(1)}, f32[10,8,128]{2,1,0:T(8,128)S(1)}) custom-call(f32[3,2,64,1024]{3,2,1,0:T(8,128)S(1)} %copy-done, s32[3,2,64,1024]{3,2,1,0:T(8,128)S(1)} %copy-done.1, f32[256,1024]{1,0:T(8,128)S(1)} %collective-permute-done.arrived.fast, f32[8]{0:T(128)S(1)} %copy-done.4, f32[2]{0:T(128)S(1)} %copy-done.5, ...), custom_call_target="tpu_custom_call" | custom-call | tf_op jit(solution)/shard_map/pallas_call | solution.py:489
  6.9 0.3 collective-permute-start.1
  7.2 4.1 %collective-permute-start.2 = (f32[16,1024]{1,0:T(8,128)S(1)}, f32[16,1024]{1,0:T(8,128)S(1)}, u32[]{:S(2)}, u32[]{:S(2)}) collective-permute-start(f32[16,1024]{1,0:T(8,128)S(1)} %get-tuple-element.26), channel_id=1, source_target_pairs={{1,2},{2,1},{3,4},{4,3},{5,6},{6,5},{9,10},{10,9},{11,12},{12,11},... | collective-permute-start | bytes 196616 | tf_op jit(solution)/shard_map/ppermute | solution.py:28
  11.3 0.0 copy-done.3
  11.4 0.1 collective-permute-start.3
  11.4 3.1 %collective-permute-start.5 = (s32[3,2,8,8]{3,2,1,0:T(8,128)S(1)}, s32[3,2,8,8]{3,2,1,0:T(8,128)S(1)}, u32[]{:S(2)}, u32[]{:S(2)}) collective-permute-start(s32[3,2,8,8]{3,2,1,0:T(8,128)S(1)} %copy-done.3), channel_id=1, source_target_pairs={{8,16},{16,8},{9,17},{17,9},{10,18},{18,10},{11,19},{19,11},{12,20... | collective-permute-start | bytes 4616 | tf_op jit(solution)/shard_map/ppermute | solution.py:28
  14.5 0.0 copy-start.2
  14.5 3.2 %shard_map.88 = (f32[3,2,64,1024]{3,2,1,0:T(8,128)S(1)}, f32[3,2,64,1024]{3,2,1,0:T(8,128)S(1)}) custom-call(f32[3,2,64,1024]{3,2,1,0:T(8,128)S(1)} %copy-done, s32[3,2,64,1024]{3,2,1,0:T(8,128)S(1)} %copy-done.1, s32[3,2,8,8]{3,2,1,0:T(8,128)S(1)} %copy-done.3, f32[10,8,128]{2,1,0:T(8,128)S(1)} %get-tuple-element.22.splat), custom_call_target="tpu_custom_call" | custom-call | tf_op jit(solution)/shard_map/pallas_call | solution.py:489
  17.8 0.0 collective-permute-done.3.before
  17.8 0.0 collective-permute-done.1.rim_a
  17.8 0.0 collective-permute-done.2.rim_b
  17.8 0.0 copy-done.2
  17.8 1.6 %shard_map.89 = (f32[3,2,64,1024]{3,2,1,0:T(8,128)S(1)}, s32[3,8,1024]{2,1,0:T(8,128)S(1)}) custom-call(f32[3,2,64,1024]{3,2,1,0:T(8,128)S(1)} %copy-done, f32[3,2,64,1024]{3,2,1,0:T(8,128)S(1)} %copy-done.2, f32[3,2,64,1024]{3,2,1,0:T(8,128)S(1)} %get-tuple-element.23.total_in, ...), custom_call_target="tpu_custom_call", output_to_operand_aliasing={{0}: (2, {})} | custom-call | tf_op jit(solution)/shard_map/pallas_call | solution.py:489
  19.4 0.1 collective-permute-done.5.before
  19.5 0.0 collective-permute-done.4.arrived
  19.5 1.3 %shard_map.90 = (f32[3,2,64,1024]{3,2,1,0:T(8,128)S(1)}, f32[3,2,64,1024]{3,2,1,0:T(8,128)S(1)}, f32[256,1024]{1,0:T(8,128)S(1)}, f32[256,1024]{1,0:T(8,128)S(1)...) custom-call(f32[3,2,64,1024]{3,2,1,0:T(8,128)S(1)} %copy-done, ...), custom_call_target="tpu_custom_call" | custom-call | tf_op jit(solution)/shard_map/pallas_call | solution.py:489
  20.8 0.1 collective-permute-start.6
  20.9 3.1 %collective-permute-start.9 = (f32[256,1024]{1,0:T(8,128)S(1)}, f32[256,1024]{1,0:T(8,128)S(1)}, u32[]{:S(2)}, u32[]{:S(2)}) collective-permute-start(f32[256,1024]{1,0:T(8,128)S(1)} %get-tuple-element.36), channel_id=1, source_target_pairs={{8,16},{16,8},{9,17},{17,9},{10,18},{18,10},{11,19},{19,11},{12,20... | collective-permute-start | bytes 3145736 | tf_op jit(solution)/shard_map/ppermute | solution.py:28
  24.0 0.3 collective-permute-start.7
  24.3 4.1 %collective-permute-start.8 = (f32[16,1024]{1,0:T(8,128)S(1)}, f32[16,1024]{1,0:T(8,128)S(1)}, u32[]{:S(2)}, u32[]{:S(2)}) collective-permute-start(f32[16,1024]{1,0:T(8,128)S(1)} %get-tuple-element.33), channel_id=1, source_target_pairs={{1,2},{2,1},{3,4},{4,3},{5,6},{6,5},{9,10},{10,9},{11,12},{12,11},... | collective-permute-start | bytes 196616 | tf_op jit(solution)/shard_map/ppermute | solution.py:28
  28.4 2.8 %shard_map.91.total_in = f32[3,2,64,1024]{3,2,1,0:T(8,128)S(1)} custom-call(f32[3,2,64,1024]{3,2,1,0:T(8,128)S(1)} %get-tuple-element.29.u, f32[3,2,64,1024]{3,2,1,0:T(8,128)S(1)} %get-tuple-element.30.w, f32[3,2,64,1024]{3,2,1,0:T(8,128)S(1)} %get-tuple-element.24.half, s32[3,2,8,8]{3,2,1,0:T(8,128)S(1)} %copy-done.3, f32[10,8,128]{2,1,0:T(8,128)S(1)} %get-tuple-element.22.splat), custom_call_target="tpu_custom_call" | custom-call | tf_op jit(solution)/shard_map/pallas_call | solution.py:489
  31.3 0.0 collective-permute-done.7.rim_a
  31.3 0.0 collective-permute-done.8.rim_b
  31.3 0.0 collective-permute-done.6.fast
  31.3 1.9 %shard_map.92 = (f32[3,2,64,1024]{3,2,1,0:T(8,128)S(1)}, f32[3,2,64,1024]{3,2,1,0:T(8,128)}, f32[3,2,64,1024]{3,2,1,0:T(8,128)}) custom-call(f32[3,2,64,1024]{3,2,1,0:T(8,128)S(1)} %get-tuple-element.29.u, f32[3,2,64,1024]{3,2,1,0:T(8,128)S(1)} %shard_map.91.total_in, ...), custom_call_target="tpu_custom_call", output_to_operand_aliasing={{0}: (1, {})} | custom-call | tf_op jit(solution)/shard_map/pallas_call | solution.py:489
  33.2 3.9 %collective-permute-done.9.arrived = f32[256,1024]{1,0:T(8,128)S(1)} collective-permute-done((f32[256,1024]{1,0:T(8,128)S(1)}, f32[256,1024]{1,0:T(8,128)S(1)}, u32[]{:S(2)}, u32[]{:S(2)}) %collective-permute-start.9) | collective-permute-done | bytes 1048608 | tf_op jit(solution)/shard_map/ppermute | solution.py:28
  37.0 2.0 %shard_map.93 = (f32[3,2,64,1024]{3,2,1,0:T(8,128)}, f32[3,2,64,1024]{3,2,1,0:T(8,128)}) custom-call(f32[3,2,64,1024]{3,2,1,0:T(8,128)S(1)} %get-tuple-element.29.u, f32[3,2,64,1024]{3,2,1,0:T(8,128)S(1)} %get-tuple-element.35.total, f32[256,1024]{1,0:T(8,128)S(1)} %collective-permute-done.9.arrived, ...), custom_call_target="tpu_custom_call", output_to_operand_aliasing={{0}: (5, {}), {1}: (6, {})} | custom-call | tf_op jit(solution)/shard_map/pallas_call | solution.py:489
Async XLA Ops:
  0.6 1.4 %copy-start = (f32[3,2,64,1024]{3,2,1,0:T(8,128)S(1)}, f32[3,2,64,1024]{3,2,1,0:T(8,128)}, u32[]{:S(2)}) copy-start(f32[3,2,64,1024]{3,2,1,0:T(8,128)} %u.9) | copy-start | bytes 4718596
  2.0 4.1 %copy-start.1 = (s32[3,2,64,1024]{3,2,1,0:T(8,128)S(1)}, s32[3,2,64,1024]{3,2,1,0:T(8,128)}, u32[]{:S(2)}) copy-start(s32[3,2,64,1024]{3,2,1,0:T(8,128)} %cls.3) | copy-start | bytes 4718596
  2.0 4.1 %copy-start.4 = (f32[8]{0:T(128)S(1)}, f32[8]{0:T(128)}, u32[]{:S(2)}) copy-start(f32[8]{0:T(128)} %stiff.1) | copy-start | bytes 100
  2.0 4.1 %copy-start.5 = (f32[2]{0:T(128)S(1)}, f32[2]{0:T(128)}, u32[]{:S(2)}) copy-start(f32[2]{0:T(128)} %cross.1) | copy-start | bytes 28
  2.0 4.1 %copy-start.6 = (s32[3]{0:T(128)S(1)}, s32[3]{0:T(128)}, u32[]{:S(2)}) copy-start(s32[3]{0:T(128)} %fixed.1) | copy-start | bytes 40
  2.2 3.9 %collective-permute-start = (f32[256,1024]{1,0:T(8,128)S(1)}, f32[256,1024]{1,0:T(8,128)S(1)}, u32[]{:S(2)}, u32[]{:S(2)}) collective-permute-start(f32[256,1024]{1,0:T(8,128)S(1)} %get-tuple-element.21), channel_id=1, source_target_pairs={{0,8},{8,0},{16,24},{24,16},{1,9},{9,1},{17,25},{25,17},{2,10},{10... | collective-permute-start | bytes 3145736 | tf_op jit(solution)/shard_map/ppermute | solution.py:28
  3.0 8.4 %copy-start.3 = (s32[3,2,8,8]{3,2,1,0:T(8,128)S(1)}, s32[3,2,8,8]{3,2,1,0:T(8,128)}, u32[]{:S(2)}) copy-start(s32[3,2,8,8]{3,2,1,0:T(8,128)} %shift.7) | copy-start | bytes 4612
  3.0 16.5 %collective-permute-start.4 = (f32[256,1024]{1,0:T(8,128)S(1)}, f32[256,1024]{1,0:T(8,128)S(1)}, u32[]{:S(2)}, u32[]{:S(2)}) collective-permute-start(f32[256,1024]{1,0:T(8,128)S(1)} %get-tuple-element.28), channel_id=1, source_target_pairs={{8,16},{16,8},{9,17},{17,9},{10,18},{18,10},{11,19},{19,11},{12,20... | collective-permute-start | bytes 3145736 | tf_op jit(solution)/shard_map/ppermute | solution.py:28
  6.9 10.9 %collective-permute-start.1 = (f32[16,1024]{1,0:T(8,128)S(1)}, f32[16,1024]{1,0:T(8,128)S(1)}, u32[]{:S(2)}, u32[]{:S(2)}) collective-permute-start(f32[16,1024]{1,0:T(8,128)S(1)} %get-tuple-element.25), channel_id=1, source_target_pairs={{0,1},{1,0},{2,3},{3,2},{4,5},{5,4},{6,7},{7,6},{8,9},{9,8},{10,11... | collective-permute-start | bytes 196616 | tf_op jit(solution)/shard_map/ppermute | solution.py:28
  7.2 10.6 %collective-permute-start.2 = (f32[16,1024]{1,0:T(8,128)S(1)}, f32[16,1024]{1,0:T(8,128)S(1)}, u32[]{:S(2)}, u32[]{:S(2)}) collective-permute-start(f32[16,1024]{1,0:T(8,128)S(1)} %get-tuple-element.26), channel_id=1, source_target_pairs={{1,2},{2,1},{3,4},{4,3},{5,6},{6,5},{9,10},{10,9},{11,12},{12,11},... | collective-permute-start | bytes 196616 | tf_op jit(solution)/shard_map/ppermute | solution.py:28
  11.4 6.4 %collective-permute-start.3 = (s32[3,2,8,8]{3,2,1,0:T(8,128)S(1)}, s32[3,2,8,8]{3,2,1,0:T(8,128)S(1)}, u32[]{:S(2)}, u32[]{:S(2)}) collective-permute-start(s32[3,2,8,8]{3,2,1,0:T(8,128)S(1)} %copy-done.3), channel_id=1, source_target_pairs={{0,8},{8,0},{16,24},{24,16},{1,9},{9,1},{17,25},{25,17},{2,10},{10... | collective-permute-start | bytes 4616 | tf_op jit(solution)/shard_map/ppermute | solution.py:28
  11.4 8.0 %collective-permute-start.5 = (s32[3,2,8,8]{3,2,1,0:T(8,128)S(1)}, s32[3,2,8,8]{3,2,1,0:T(8,128)S(1)}, u32[]{:S(2)}, u32[]{:S(2)}) collective-permute-start(s32[3,2,8,8]{3,2,1,0:T(8,128)S(1)} %copy-done.3), channel_id=1, source_target_pairs={{8,16},{16,8},{9,17},{17,9},{10,18},{18,10},{11,19},{19,11},{12,20... | collective-permute-start | bytes 4616 | tf_op jit(solution)/shard_map/ppermute | solution.py:28
  14.5 3.3 %copy-start.2 = (f32[3,2,64,1024]{3,2,1,0:T(8,128)S(1)}, f32[3,2,64,1024]{3,2,1,0:T(8,128)}, u32[]{:S(2)}) copy-start(f32[3,2,64,1024]{3,2,1,0:T(8,128)} %w.1) | copy-start | bytes 4718596
  20.8 10.5 %collective-permute-start.6 = (f32[256,1024]{1,0:T(8,128)S(1)}, f32[256,1024]{1,0:T(8,128)S(1)}, u32[]{:S(2)}, u32[]{:S(2)}) collective-permute-start(f32[256,1024]{1,0:T(8,128)S(1)} %get-tuple-element.31), channel_id=1, source_target_pairs={{0,8},{8,0},{16,24},{24,16},{1,9},{9,1},{17,25},{25,17},{2,10},{10... | collective-permute-start | bytes 3145736 | tf_op jit(solution)/shard_map/ppermute | solution.py:28
  20.9 16.1 %collective-permute-start.9 = (f32[256,1024]{1,0:T(8,128)S(1)}, f32[256,1024]{1,0:T(8,128)S(1)}, u32[]{:S(2)}, u32[]{:S(2)}) collective-permute-start(f32[256,1024]{1,0:T(8,128)S(1)} %get-tuple-element.36), channel_id=1, source_target_pairs={{8,16},{16,8},{9,17},{17,9},{10,18},{18,10},{11,19},{19,11},{12,20... | collective-permute-start | bytes 3145736 | tf_op jit(solution)/shard_map/ppermute | solution.py:28
  24.0 7.3 %collective-permute-start.7 = (f32[16,1024]{1,0:T(8,128)S(1)}, f32[16,1024]{1,0:T(8,128)S(1)}, u32[]{:S(2)}, u32[]{:S(2)}) collective-permute-start(f32[16,1024]{1,0:T(8,128)S(1)} %get-tuple-element.32), channel_id=1, source_target_pairs={{0,1},{1,0},{2,3},{3,2},{4,5},{5,4},{6,7},{7,6},{8,9},{9,8},{10,11... | collective-permute-start | bytes 196616 | tf_op jit(solution)/shard_map/ppermute | solution.py:28
  24.3 7.0 %collective-permute-start.8 = (f32[16,1024]{1,0:T(8,128)S(1)}, f32[16,1024]{1,0:T(8,128)S(1)}, u32[]{:S(2)}, u32[]{:S(2)}) collective-permute-start(f32[16,1024]{1,0:T(8,128)S(1)} %get-tuple-element.33), channel_id=1, source_target_pairs={{1,2},{2,1},{3,4},{4,3},{5,6},{6,5},{9,10},{10,9},{11,12},{12,11},... | collective-permute-start | bytes 196616 | tf_op jit(solution)/shard_map/ppermute | solution.py:28

commit v8 on v7

--- a/solution.py
+++ b/solution.py
@@ -411,9 +411,10 @@
 
 def step_kernel(
     u, total, arrived, half, shift, before, splat,
-    new_u, new_w, slow, fast, index, rim_a, rim_b,
+    new_u, new_w, slow_top, slow_rest, fast, index, rim_a, rim_b,
 ):
     sections, _, rows, width = u.shape
+    top = slow_top.shape[0] // 4
 
     def body(after):
         put_index(after, shift, before, index)
@@ -434,9 +435,14 @@
                     moved = u[s, c, at, :] + STEP * v
                     new_w[s, c, at, :] = v
                     new_u[s, c, at, :] = moved
-                    for edge, out in ((slow_edge, slow), (fast_edge, fast)):
-                        if s in edge:
-                            out[pl.ds((2 * edge.index(s) + c) * rows + row, ROWS), :] = moved
+                    if s in fast_edge:
+                        fast[pl.ds((2 * fast_edge.index(s) + c) * rows + row, ROWS), :] = moved
+                    if s in slow_edge:
+                        k = 2 * slow_edge.index(s) + c
+                        if row < top:
+                            slow_top[pl.ds(k * top + row, ROWS), :] = moved
+                        else:
+                            slow_rest[pl.ds(k * (rows - top) + row - top, ROWS), :] = moved
 
     by_side(body)
     last = slice(rows - 1, rows)
@@ -456,7 +462,7 @@
     sections, _, rows, width = u.shape
     height = arrived.shape[0] // 4
     rbs = height // ROWS
-    part = rbs // 2 if rbs % 2 == 0 else rbs
+    ends = sorted({(rbs + 1) // 2, rbs})
 
     def body(after):
         copies = []
@@ -470,9 +476,11 @@
                     v = value[c] * moving
                     new_w[j, c, rows_of(k), :] = v
                     new_u[j, c, rows_of(k), :] = u[own, c, rows_of(rb), :] + STEP * v
-                if (k + 1) % part == 0:
-                    here = pl.ds((k + 1 - part) * ROWS, part * ROWS)
-                    there = pl.ds(base + (k + 1 - part) * ROWS, part * ROWS)
+                if k + 1 in ends:
+                    first = 0 if k + 1 == ends[0] else ends[0]
+                    size = (k + 1 - first) * ROWS
+                    here = pl.ds(first * ROWS, size)
+                    there = pl.ds(base + first * ROWS, size)
                     for source, target in ((new_u, out_u), (new_w, out_w)):
                         copy = pltpu.make_async_copy(
                             source.at[j, :, here], target.at[own, :, there], sem.at[len(copies)]
@@ -538,12 +546,14 @@
         [u, w, total, half, fast, rim_a, rim_b, shift, before_fast, splat],
         {2: 0},
     )
-    u, w, slow, fast, index, rim_a, rim_b = call(
+    top = max(rows // ROWS * 7 // 8, 1) * ROWS
+    u, w, slow_top, slow_rest, fast, index, rim_a, rim_b = call(
         step_kernel,
-        [full, full, two, two, index, rim, rim],
+        [full, full, array(4 * top, width), array(4 * (rows - top), width), two, index, rim, rim],
         [u, total, slow, half, shift, before_slow, splat],
     )
-    slow = exchange(slow, "sec", "b")
+    slow_top = exchange(slow_top, "sec", "b")
+    slow_rest = exchange(slow_rest, "sec", "b")
     fast = exchange(fast, "sec", "a")
     rim_a = exchange(rim_a, "strip", "a")
     rim_b = exchange(rim_b, "strip", "b")
@@ -559,18 +569,19 @@
         + [pltpu.SemaphoreType.DMA((2 * done,))],
         out_specs=[VMEM, ANY, ANY],
     )
-    return tuple(
-        call(
-            functools.partial(last_kernel, 0),
+    for base, arrived in ((0, slow_top), (top, slow_rest)):
+        height = arrived.shape[0] // 4
+        out_u, out_w = call(
+            functools.partial(last_kernel, base),
             [full, full],
-            [u, total, slow, index, splat, out_u, out_w],
+            [u, total, arrived, index, splat, out_u, out_w],
             {5: 0, 6: 1},
-            scratch=[pltpu.VMEM((2, 2, rows, width), jnp.float32)] * 2
+            scratch=[pltpu.VMEM((2, 2, height, width), jnp.float32)] * 2
             + [pltpu.SemaphoreType.DMA((8,))],
             in_specs=[VMEM] * 5 + [ANY] * 2,
             out_specs=[ANY] * 2,
         )
-    )
+    return out_u, out_w
 
 
 def solution(mesh):

time: 39.7 us -> 39.9 us (level)
  the two profiles are of different devices: /device:TPU:3 before, /device:TPU:12 now
where the time goes in v8:
time: 39.9 us; the launch traced here: 39.6 us
  starting transfers between devices  18.7 us (47%)
  Pallas kernels  14.8 us (37%)
  waiting for transfers between devices  3.63 us (9%)
  local copies, waits for them, and re-layouts  1.43 us (4%)
  between operations  1.06 us (3%)
    ppermute x11, starting transfers between devices, exchange(): return lax.ppermute(value, axis, route)  18.7 us
    pallas_call x9, Pallas kernels, call(): pl.pallas_call(kernel, out_shape=outs, in_specs=in_specs or [VMEM] * len(...  14.8 us
    ppermute x11, waiting for transfers between devices, exchange(): return lax.ppermute(value, axis, route)  3.63 us
    unnamed x14, local copies, waits for them, and re-layouts  1.43 us
  transfers between devices with their start and end apart: 11, of which 2 were waited for; matrix products, arithmetic and copies ran while one was open for 0% of the time, Pallas kernels for 31%

profile of v8, /device:TPU:12, one launch (start us, length us, event | category | flops | bytes accessed | tf_op | source)
XLA Modules:
  0.0 39.6 jit_solution(14161485954464444770)
XLA Ops:
  0.6 0.0 copy-start
  0.6 1.4 %copy-done = f32[3,2,64,1024]{3,2,1,0:T(8,128)S(1)} copy-done((f32[3,2,64,1024]{3,2,1,0:T(8,128)S(1)}, f32[3,2,64,1024]{3,2,1,0:T(8,128)}, u32[]{:S(2)}) %copy-start) | copy-done | bytes 1572888
  2.0 0.0 copy-start.1
  2.0 0.0 copy-start.4
  2.0 0.0 copy-start.5
  2.0 0.0 copy-start.6
  2.1 0.2 shard_map.86
  2.2 0.1 collective-permute-start
  2.3 0.0 copy-start.3
  2.3 2.6 %collective-permute-start.4 = (f32[256,1024]{1,0:T(8,128)S(1)}, f32[256,1024]{1,0:T(8,128)S(1)}, u32[]{:S(2)}, u32[]{:S(2)}) collective-permute-start(f32[256,1024]{1,0:T(8,128)S(1)} %get-tuple-element.31), channel_id=1, source_target_pairs={{8,16},{16,8},{9,17},{17,9},{10,18},{18,10},{11,19},{19,11},{12,20... | collective-permute-start | bytes 3145736 | tf_op jit(solution)/shard_map/ppermute | solution.py:28
  4.9 0.0 collective-permute-done.arrived.fast
  4.9 0.0 copy-done.1
  5.0 0.0 copy-done.4
  5.0 0.0 copy-done.5
  5.0 0.0 copy-done.6
  5.0 0.7 %shard_map.87 = (f32[16,1024]{1,0:T(8,128)S(1)}, f32[16,1024]{1,0:T(8,128)S(1)}, f32[10,8,128]{2,1,0:T(8,128)S(1)}) custom-call(f32[3,2,64,1024]{3,2,1,0:T(8,128)S(1)} %copy-done, s32[3,2,64,1024]{3,2,1,0:T(8,128)S(1)} %copy-done.1, f32[256,1024]{1,0:T(8,128)S(1)} %collective-permute-done.arrived.fast, f32[8]{0:T(128)S(1)} %copy-done.4, f32[2]{0:T(128)S(1)} %copy-done.5, ...), custom_call_target="tpu_custom_call" | custom-call | tf_op jit(solution)/shard_map/pallas_call | solution.py:497
  5.7 1.6 %collective-permute-start.1 = (f32[16,1024]{1,0:T(8,128)S(1)}, f32[16,1024]{1,0:T(8,128)S(1)}, u32[]{:S(2)}, u32[]{:S(2)}) collective-permute-start(f32[16,1024]{1,0:T(8,128)S(1)} %get-tuple-element.28), channel_id=1, source_target_pairs={{0,1},{1,0},{2,3},{3,2},{4,5},{5,4},{6,7},{7,6},{8,9},{9,8},{10,11... | collective-permute-start | bytes 196616 | tf_op jit(solution)/shard_map/ppermute | solution.py:28
  7.2 2.3 %collective-permute-start.2 = (f32[16,1024]{1,0:T(8,128)S(1)}, f32[16,1024]{1,0:T(8,128)S(1)}, u32[]{:S(2)}, u32[]{:S(2)}) collective-permute-start(f32[16,1024]{1,0:T(8,128)S(1)} %get-tuple-element.29), channel_id=1, source_target_pairs={{1,2},{2,1},{3,4},{4,3},{5,6},{6,5},{9,10},{10,9},{11,12},{12,11},... | collective-permute-start | bytes 196616 | tf_op jit(solution)/shard_map/ppermute | solution.py:28
  9.5 0.0 copy-done.3
  9.5 0.1 collective-permute-start.3
  9.6 2.5 %collective-permute-start.5 = (s32[3,2,8,8]{3,2,1,0:T(8,128)S(1)}, s32[3,2,8,8]{3,2,1,0:T(8,128)S(1)}, u32[]{:S(2)}, u32[]{:S(2)}) collective-permute-start(s32[3,2,8,8]{3,2,1,0:T(8,128)S(1)} %copy-done.3), channel_id=1, source_target_pairs={{8,16},{16,8},{9,17},{17,9},{10,18},{18,10},{11,19},{19,11},{12,20... | collective-permute-start | bytes 4616 | tf_op jit(solution)/shard_map/ppermute | solution.py:28
  12.2 0.0 copy-start.2
  12.2 3.2 %shard_map.88 = (f32[3,2,64,1024]{3,2,1,0:T(8,128)S(1)}, f32[3,2,64,1024]{3,2,1,0:T(8,128)S(1)}) custom-call(f32[3,2,64,1024]{3,2,1,0:T(8,128)S(1)} %copy-done, s32[3,2,64,1024]{3,2,1,0:T(8,128)S(1)} %copy-done.1, s32[3,2,8,8]{3,2,1,0:T(8,128)S(1)} %copy-done.3, f32[10,8,128]{2,1,0:T(8,128)S(1)} %get-tuple-element.25.splat), custom_call_target="tpu_custom_call" | custom-call | tf_op jit(solution)/shard_map/pallas_call | solution.py:497
  15.4 0.0 collective-permute-done.3.before
  15.4 0.0 collective-permute-done.1.rim_a
  15.4 0.0 collective-permute-done.2.rim_b
  15.5 0.0 copy-done.2
  15.5 1.6 %shard_map.89 = (f32[3,2,64,1024]{3,2,1,0:T(8,128)S(1)}, s32[3,8,1024]{2,1,0:T(8,128)S(1)}) custom-call(f32[3,2,64,1024]{3,2,1,0:T(8,128)S(1)} %copy-done, f32[3,2,64,1024]{3,2,1,0:T(8,128)S(1)} %copy-done.2, f32[3,2,64,1024]{3,2,1,0:T(8,128)S(1)} %get-tuple-element.26.total_in, ...), custom_call_target="tpu_custom_call", output_to_operand_aliasing={{0}: (2, {})} | custom-call | tf_op jit(solution)/shard_map/pallas_call | solution.py:497
  17.1 1.7 %collective-permute-done.5.before = s32[3,2,8,8]{3,2,1,0:T(8,128)S(1)} collective-permute-done((s32[3,2,8,8]{3,2,1,0:T(8,128)S(1)}, s32[3,2,8,8]{3,2,1,0:T(8,128)S(1)}, u32[]{:S(2)}, u32[]{:S(2)}) %collective-permute-start.5) | collective-permute-done | bytes 1568 | tf_op jit(solution)/shard_map/ppermute | solution.py:28
  18.8 0.0 collective-permute-done.4.arrived
  18.8 1.3 %shard_map.90 = (f32[3,2,64,1024]{3,2,1,0:T(8,128)S(1)}, f32[3,2,64,1024]{3,2,1,0:T(8,128)S(1)}, f32[224,1024]{1,0:T(8,128)S(1)}, f32[32,1024]{1,0:T(8,128)S(1)}...) custom-call(f32[3,2,64,1024]{3,2,1,0:T(8,128)S(1)} %copy-done, ...), custom_call_target="tpu_custom_call" | custom-call | tf_op jit(solution)/shard_map/pallas_call | solution.py:497
  20.2 0.1 collective-permute-start.6
  20.3 2.5 %collective-permute-start.10 = (f32[224,1024]{1,0:T(8,128)S(1)}, f32[224,1024]{1,0:T(8,128)S(1)}, u32[]{:S(2)}, u32[]{:S(2)}) collective-permute-start(f32[224,1024]{1,0:T(8,128)S(1)} %get-tuple-element.41), channel_id=1, source_target_pairs={{8,16},{16,8},{9,17},{17,9},{10,18},{18,10},{11,19},{19,11},{12,20... | collective-permute-start | bytes 2752520 | tf_op jit(solution)/shard_map/ppermute | solution.py:28
  22.8 3.1 %collective-permute-start.9 = (f32[32,1024]{1,0:T(8,128)S(1)}, f32[32,1024]{1,0:T(8,128)S(1)}, u32[]{:S(2)}, u32[]{:S(2)}) collective-permute-start(f32[32,1024]{1,0:T(8,128)S(1)} %get-tuple-element.39), channel_id=1, source_target_pairs={{8,16},{16,8},{9,17},{17,9},{10,18},{18,10},{11,19},{19,11},{12,20... | collective-permute-start | bytes 393224 | tf_op jit(solution)/shard_map/ppermute | solution.py:28
  25.8 1.6 %collective-permute-start.7 = (f32[16,1024]{1,0:T(8,128)S(1)}, f32[16,1024]{1,0:T(8,128)S(1)}, u32[]{:S(2)}, u32[]{:S(2)}) collective-permute-start(f32[16,1024]{1,0:T(8,128)S(1)} %get-tuple-element.35), channel_id=1, source_target_pairs={{0,1},{1,0},{2,3},{3,2},{4,5},{5,4},{6,7},{7,6},{8,9},{9,8},{10,11... | collective-permute-start | bytes 196616 | tf_op jit(solution)/shard_map/ppermute | solution.py:28
  27.4 2.3 %collective-permute-start.8 = (f32[16,1024]{1,0:T(8,128)S(1)}, f32[16,1024]{1,0:T(8,128)S(1)}, u32[]{:S(2)}, u32[]{:S(2)}) collective-permute-start(f32[16,1024]{1,0:T(8,128)S(1)} %get-tuple-element.36), channel_id=1, source_target_pairs={{1,2},{2,1},{3,4},{4,3},{5,6},{6,5},{9,10},{10,9},{11,12},{12,11},... | collective-permute-start | bytes 196616 | tf_op jit(solution)/shard_map/ppermute | solution.py:28
  29.7 2.8 %shard_map.91.total_in = f32[3,2,64,1024]{3,2,1,0:T(8,128)S(1)} custom-call(f32[3,2,64,1024]{3,2,1,0:T(8,128)S(1)} %get-tuple-element.32.u, f32[3,2,64,1024]{3,2,1,0:T(8,128)S(1)} %get-tuple-element.33.w, f32[3,2,64,1024]{3,2,1,0:T(8,128)S(1)} %get-tuple-element.27.half, s32[3,2,8,8]{3,2,1,0:T(8,128)S(1)} %copy-done.3, f32[10,8,128]{2,1,0:T(8,128)S(1)} %get-tuple-element.25.splat), custom_call_target="tpu_custom_call" | custom-call | tf_op jit(solution)/shard_map/pallas_call | solution.py:497
  32.6 0.0 collective-permute-done.7.rim_a
  32.6 1.9 %collective-permute-done.8.rim_b = f32[16,1024]{1,0:T(8,128)S(1)} collective-permute-done((f32[16,1024]{1,0:T(8,128)S(1)}, f32[16,1024]{1,0:T(8,128)S(1)}, u32[]{:S(2)}, u32[]{:S(2)}) %collective-permute-start.8) | collective-permute-done | bytes 65568 | tf_op jit(solution)/shard_map/ppermute | solution.py:28
  34.4 0.0 collective-permute-done.6.fast
  34.4 2.1 %shard_map.92 = (f32[3,2,64,1024]{3,2,1,0:T(8,128)S(1)}, f32[3,2,64,1024]{3,2,1,0:T(8,128)}, f32[3,2,64,1024]{3,2,1,0:T(8,128)}) custom-call(f32[3,2,64,1024]{3,2,1,0:T(8,128)S(1)} %get-tuple-element.32.u, f32[3,2,64,1024]{3,2,1,0:T(8,128)S(1)} %shard_map.91.total_in, ...), custom_call_target="tpu_custom_call", output_to_operand_aliasing={{0}: (1, {})} | custom-call | tf_op jit(solution)/shard_map/pallas_call | solution.py:497
  36.5 0.0 collective-permute-done.10.arrived
  36.5 1.9 %shard_map.93 = (f32[3,2,64,1024]{3,2,1,0:T(8,128)}, f32[3,2,64,1024]{3,2,1,0:T(8,128)}) custom-call(f32[3,2,64,1024]{3,2,1,0:T(8,128)S(1)} %get-tuple-element.32.u, f32[3,2,64,1024]{3,2,1,0:T(8,128)S(1)} %get-tuple-element.38.total, f32[224,1024]{1,0:T(8,128)S(1)} %collective-permute-done.10.arrived, ...), custom_call_target="tpu_custom_call", output_to_operand_aliasing={{0}: (5, {}), {1}: (6, {})} | custom-call | tf_op jit(solution)/shard_map/pallas_call | solution.py:497
  38.5 0.0 collective-permute-done.9.arrived
  38.5 1.0 %shard_map.94 = (f32[3,2,64,1024]{3,2,1,0:T(8,128)}, f32[3,2,64,1024]{3,2,1,0:T(8,128)}) custom-call(f32[3,2,64,1024]{3,2,1,0:T(8,128)S(1)} %get-tuple-element.32.u, f32[3,2,64,1024]{3,2,1,0:T(8,128)S(1)} %get-tuple-element.38.total, f32[32,1024]{1,0:T(8,128)S(1)} %collective-permute-done.9.arrived, ...), custom_call_target="tpu_custom_call", output_to_operand_aliasing={{0}: (5, {}), {1}: (6, {})} | custom-call | tf_op jit(solution)/shard_map/pallas_call | solution.py:497
Async XLA Ops:
  0.6 1.4 %copy-start = (f32[3,2,64,1024]{3,2,1,0:T(8,128)S(1)}, f32[3,2,64,1024]{3,2,1,0:T(8,128)}, u32[]{:S(2)}) copy-start(f32[3,2,64,1024]{3,2,1,0:T(8,128)} %u.9) | copy-start | bytes 4718596
  2.0 2.9 %copy-start.1 = (s32[3,2,64,1024]{3,2,1,0:T(8,128)S(1)}, s32[3,2,64,1024]{3,2,1,0:T(8,128)}, u32[]{:S(2)}) copy-start(s32[3,2,64,1024]{3,2,1,0:T(8,128)} %cls.3) | copy-start | bytes 4718596
  2.0 2.9 %copy-start.4 = (f32[8]{0:T(128)S(1)}, f32[8]{0:T(128)}, u32[]{:S(2)}) copy-start(f32[8]{0:T(128)} %stiff.1) | copy-start | bytes 100
  2.0 2.9 %copy-start.5 = (f32[2]{0:T(128)S(1)}, f32[2]{0:T(128)}, u32[]{:S(2)}) copy-start(f32[2]{0:T(128)} %cross.1) | copy-start | bytes 28
  2.0 2.9 %copy-start.6 = (s32[3]{0:T(128)S(1)}, s32[3]{0:T(128)}, u32[]{:S(2)}) copy-start(s32[3]{0:T(128)} %fixed.1) | copy-start | bytes 40
  2.2 2.7 %collective-permute-start = (f32[256,1024]{1,0:T(8,128)S(1)}, f32[256,1024]{1,0:T(8,128)S(1)}, u32[]{:S(2)}, u32[]{:S(2)}) collective-permute-start(f32[256,1024]{1,0:T(8,128)S(1)} %get-tuple-element.24), channel_id=1, source_target_pairs={{0,8},{8,0},{16,24},{24,16},{1,9},{9,1},{17,25},{25,17},{2,10},{10... | collective-permute-start | bytes 3145736 | tf_op jit(solution)/shard_map/ppermute | solution.py:28
  2.3 7.2 %copy-start.3 = (s32[3,2,8,8]{3,2,1,0:T(8,128)S(1)}, s32[3,2,8,8]{3,2,1,0:T(8,128)}, u32[]{:S(2)}) copy-start(s32[3,2,8,8]{3,2,1,0:T(8,128)} %shift.7) | copy-start | bytes 4612
  2.3 16.5 %collective-permute-start.4 = (f32[256,1024]{1,0:T(8,128)S(1)}, f32[256,1024]{1,0:T(8,128)S(1)}, u32[]{:S(2)}, u32[]{:S(2)}) collective-permute-start(f32[256,1024]{1,0:T(8,128)S(1)} %get-tuple-element.31), channel_id=1, source_target_pairs={{8,16},{16,8},{9,17},{17,9},{10,18},{18,10},{11,19},{19,11},{12,20... | collective-permute-start | bytes 3145736 | tf_op jit(solution)/shard_map/ppermute | solution.py:28
  5.7 9.8 %collective-permute-start.1 = (f32[16,1024]{1,0:T(8,128)S(1)}, f32[16,1024]{1,0:T(8,128)S(1)}, u32[]{:S(2)}, u32[]{:S(2)}) collective-permute-start(f32[16,1024]{1,0:T(8,128)S(1)} %get-tuple-element.28), channel_id=1, source_target_pairs={{0,1},{1,0},{2,3},{3,2},{4,5},{5,4},{6,7},{7,6},{8,9},{9,8},{10,11... | collective-permute-start | bytes 196616 | tf_op jit(solution)/shard_map/ppermute | solution.py:28
  7.2 8.2 %collective-permute-start.2 = (f32[16,1024]{1,0:T(8,128)S(1)}, f32[16,1024]{1,0:T(8,128)S(1)}, u32[]{:S(2)}, u32[]{:S(2)}) collective-permute-start(f32[16,1024]{1,0:T(8,128)S(1)} %get-tuple-element.29), channel_id=1, source_target_pairs={{1,2},{2,1},{3,4},{4,3},{5,6},{6,5},{9,10},{10,9},{11,12},{12,11},... | collective-permute-start | bytes 196616 | tf_op jit(solution)/shard_map/ppermute | solution.py:28
  9.5 5.9 %collective-permute-start.3 = (s32[3,2,8,8]{3,2,1,0:T(8,128)S(1)}, s32[3,2,8,8]{3,2,1,0:T(8,128)S(1)}, u32[]{:S(2)}, u32[]{:S(2)}) collective-permute-start(s32[3,2,8,8]{3,2,1,0:T(8,128)S(1)} %copy-done.3), channel_id=1, source_target_pairs={{0,8},{8,0},{16,24},{24,16},{1,9},{9,1},{17,25},{25,17},{2,10},{10... | collective-permute-start | bytes 4616 | tf_op jit(solution)/shard_map/ppermute | solution.py:28
  9.6 9.2 %collective-permute-start.5 = (s32[3,2,8,8]{3,2,1,0:T(8,128)S(1)}, s32[3,2,8,8]{3,2,1,0:T(8,128)S(1)}, u32[]{:S(2)}, u32[]{:S(2)}) collective-permute-start(s32[3,2,8,8]{3,2,1,0:T(8,128)S(1)} %copy-done.3), channel_id=1, source_target_pairs={{8,16},{16,8},{9,17},{17,9},{10,18},{18,10},{11,19},{19,11},{12,20... | collective-permute-start | bytes 4616 | tf_op jit(solution)/shard_map/ppermute | solution.py:28
  12.2 3.3 %copy-start.2 = (f32[3,2,64,1024]{3,2,1,0:T(8,128)S(1)}, f32[3,2,64,1024]{3,2,1,0:T(8,128)}, u32[]{:S(2)}) copy-start(f32[3,2,64,1024]{3,2,1,0:T(8,128)} %w.1) | copy-start | bytes 4718596
  20.2 14.3 %collective-permute-start.6 = (f32[256,1024]{1,0:T(8,128)S(1)}, f32[256,1024]{1,0:T(8,128)S(1)}, u32[]{:S(2)}, u32[]{:S(2)}) collective-permute-start(f32[256,1024]{1,0:T(8,128)S(1)} %get-tuple-element.34), channel_id=1, source_target_pairs={{0,8},{8,0},{16,24},{24,16},{1,9},{9,1},{17,25},{25,17},{2,10},{10... | collective-permute-start | bytes 3145736 | tf_op jit(solution)/shard_map/ppermute | solution.py:28
  20.3 16.3 %collective-permute-start.10 = (f32[224,1024]{1,0:T(8,128)S(1)}, f32[224,1024]{1,0:T(8,128)S(1)}, u32[]{:S(2)}, u32[]{:S(2)}) collective-permute-start(f32[224,1024]{1,0:T(8,128)S(1)} %get-tuple-element.41), channel_id=1, source_target_pairs={{8,16},{16,8},{9,17},{17,9},{10,18},{18,10},{11,19},{19,11},{12,20... | collective-permute-start | bytes 2752520 | tf_op jit(solution)/shard_map/ppermute | solution.py:28
  22.8 15.7 %collective-permute-start.9 = (f32[32,1024]{1,0:T(8,128)S(1)}, f32[32,1024]{1,0:T(8,128)S(1)}, u32[]{:S(2)}, u32[]{:S(2)}) collective-permute-start(f32[32,1024]{1,0:T(8,128)S(1)} %get-tuple-element.39), channel_id=1, source_target_pairs={{8,16},{16,8},{9,17},{17,9},{10,18},{18,10},{11,19},{19,11},{12,20... | collective-permute-start | bytes 393224 | tf_op jit(solution)/shard_map/ppermute | solution.py:28
  25.8 6.7 %collective-permute-start.7 = (f32[16,1024]{1,0:T(8,128)S(1)}, f32[16,1024]{1,0:T(8,128)S(1)}, u32[]{:S(2)}, u32[]{:S(2)}) collective-permute-start(f32[16,1024]{1,0:T(8,128)S(1)} %get-tuple-element.35), channel_id=1, source_target_pairs={{0,1},{1,0},{2,3},{3,2},{4,5},{5,4},{6,7},{7,6},{8,9},{9,8},{10,11... | collective-permute-start | bytes 196616 | tf_op jit(solution)/shard_map/ppermute | solution.py:28
  27.4 7.0 %collective-permute-start.8 = (f32[16,1024]{1,0:T(8,128)S(1)}, f32[16,1024]{1,0:T(8,128)S(1)}, u32[]{:S(2)}, u32[]{:S(2)}) collective-permute-start(f32[16,1024]{1,0:T(8,128)S(1)} %get-tuple-element.36), channel_id=1, source_target_pairs={{1,2},{2,1},{3,4},{4,3},{5,6},{6,5},{9,10},{10,9},{11,12},{12,11},... | collective-permute-start | bytes 196616 | tf_op jit(solution)/shard_map/ppermute | solution.py:28

commit v9 on v7

--- a/solution.py
+++ b/solution.py
@@ -342,7 +342,8 @@
 
 
 def first_rims_kernel(
-    u, w, total_in, half, fast, rim_a, rim_b, shift, before, splat, total, index
+    u, w, total_in, half, fast, rim_a, rim_b, shift, before, splat,
+    total, index, new_u, new_w, sent,
 ):
     sections, _, rows, _ = u.shape
 
@@ -361,6 +362,25 @@
 
     by_side(body)
     rim_flows(u, half, rim_a, rim_b, total, range(sections))
+
+    def settle(after):
+        slow_edge = (near_of(after, sections), second_of(after, sections))
+        fast_edge = (near_of(not after, sections), second_of(not after, sections))
+        for s in range(sections):
+            if s in slow_edge:
+                continue
+            moving = wide_splat(splat, MOVING + s, u.shape[3])
+            for row in range(0, rows, ROWS):
+                at = pl.ds(row, ROWS)
+                for c in range(2):
+                    v = total[s, c, at, :] * moving
+                    moved = u[s, c, at, :] + STEP * v
+                    new_w[s, c, at, :] = v
+                    new_u[s, c, at, :] = moved
+                    if s in fast_edge:
+                        sent[pl.ds((2 * fast_edge.index(s) + c) * rows + row, ROWS), :] = moved
+
+    by_side(settle)
 
 
 def later_rims_kernel(
@@ -410,7 +430,7 @@
 
 
 def step_kernel(
-    u, total, arrived, half, shift, before, splat,
+    u, total, arrived, half, shift, before, splat, new_u_in, new_w_in, fast_in,
     new_u, new_w, slow, fast, index, rim_a, rim_b,
 ):
     sections, _, rows, width = u.shape
@@ -419,16 +439,11 @@
         put_index(after, shift, before, index)
         slow_edge = (near_of(after, sections), second_of(after, sections))
         fast_edge = (near_of(not after, sections), second_of(not after, sections))
-        for s in range(sections):
+        for j, s in enumerate(slow_edge):
             moving = wide_splat(splat, MOVING + s, width)
             for rb in range(rows // ROWS):
                 at, row = rows_of(rb), rb * ROWS
-                if s in slow_edge:
-                    value = slow_values(
-                        u, after, arrived, rows, 0, index, splat, total, slow_edge.index(s), rb
-                    )
-                else:
-                    value = [total[s, c, at, :] for c in range(2)]
+                value = slow_values(u, after, arrived, rows, 0, index, splat, total, j, rb)
                 for c in range(2):
                     v = value[c] * moving
                     moved = u[s, c, at, :] + STEP * v
@@ -532,16 +547,17 @@
     total, half = call(
         first_inside_kernel, [full, full], [u, cls, shift, splat], scratch=scalars
     )
-    total, fast_index = call(
+    total, fast_index, new_u, new_w, fast = call(
         first_rims_kernel,
-        [full, index],
+        [full, index, full, full, two],
         [u, w, total, half, fast, rim_a, rim_b, shift, before_fast, splat],
         {2: 0},
     )
     u, w, slow, fast, index, rim_a, rim_b = call(
         step_kernel,
         [full, full, two, two, index, rim, rim],
-        [u, total, slow, half, shift, before_slow, splat],
+        [u, total, slow, half, shift, before_slow, splat, new_u, new_w, fast],
+        {7: 0, 8: 1, 9: 3},
     )
     slow = exchange(slow, "sec", "b")
     fast = exchange(fast, "sec", "a")

time: 39.7 us -> 39.7 us (level)
  transfers between devices with their start and end apart: 10 -> 10, of which waited for: 2 -> 1; matrix products, arithmetic and copies ran while one was open for 0% -> 0% of each run, Pallas kernels for 26% -> 27%
where the time goes in v9:
time: 39.7 us; the launch traced here: 39.2 us
  starting transfers between devices  19 us (48%)
  Pallas kernels  14 us (35%)
  waiting for transfers between devices  3.8 us (10%)
  local copies, waits for them, and re-layouts  1.43 us (4%)
  between operations  1.04 us (3%)
    ppermute x10, starting transfers between devices, exchange(): return lax.ppermute(value, axis, route)  19 us
    pallas_call x8, Pallas kernels, call(): pl.pallas_call(kernel, out_shape=outs, in_specs=in_specs or [VMEM] * len(...  14 us
    ppermute x10, waiting for transfers between devices, exchange(): return lax.ppermute(value, axis, route)  3.8 us
    unnamed x14, local copies, waits for them, and re-layouts  1.43 us
  transfers between devices with their start and end apart: 10, of which 1 were waited for; matrix products, arithmetic and copies ran while one was open for 0% of the time, Pallas kernels for 27%

profile of v9, /device:TPU:3, one launch (start us, length us, event | category | flops | bytes accessed | tf_op | source)
XLA Modules:
  0.0 39.2 jit_solution(652575132111999512)
XLA Ops:
  0.6 0.0 copy-start
  0.6 1.4 %copy-done = f32[3,2,64,1024]{3,2,1,0:T(8,128)S(1)} copy-done((f32[3,2,64,1024]{3,2,1,0:T(8,128)S(1)}, f32[3,2,64,1024]{3,2,1,0:T(8,128)}, u32[]{:S(2)}) %copy-start) | copy-done | bytes 1572888
  2.0 0.0 copy-start.1
  2.0 0.0 copy-start.4
  2.0 0.0 copy-start.5
  2.0 0.0 copy-start.6
  2.1 0.2 shard_map.86
  2.2 0.7 %collective-permute-start = (f32[256,1024]{1,0:T(8,128)S(1)}, f32[256,1024]{1,0:T(8,128)S(1)}, u32[]{:S(2)}, u32[]{:S(2)}) collective-permute-start(f32[256,1024]{1,0:T(8,128)S(1)} %get-tuple-element.24), channel_id=1, source_target_pairs={{0,8},{8,0},{16,24},{24,16},{1,9},{9,1},{17,25},{25,17},{2,10},{10... | collective-permute-start | bytes 3145736 | tf_op jit(solution)/shard_map/ppermute | solution.py:28
  3.0 0.0 copy-start.3
  3.0 3.2 %collective-permute-start.4 = (f32[256,1024]{1,0:T(8,128)S(1)}, f32[256,1024]{1,0:T(8,128)S(1)}, u32[]{:S(2)}, u32[]{:S(2)}) collective-permute-start(f32[256,1024]{1,0:T(8,128)S(1)} %get-tuple-element.31), channel_id=1, source_target_pairs={{8,16},{16,8},{9,17},{17,9},{10,18},{18,10},{11,19},{19,11},{12,20... | collective-permute-start | bytes 3145736 | tf_op jit(solution)/shard_map/ppermute | solution.py:28
  6.2 0.0 collective-permute-done.arrived.fast
  6.2 0.0 copy-done.1
  6.2 0.0 copy-done.4
  6.2 0.0 copy-done.5
  6.2 0.0 copy-done.6
  6.2 0.7 %shard_map.87 = (f32[16,1024]{1,0:T(8,128)S(1)}, f32[16,1024]{1,0:T(8,128)S(1)}, f32[10,8,128]{2,1,0:T(8,128)S(1)}) custom-call(f32[3,2,64,1024]{3,2,1,0:T(8,128)S(1)} %copy-done, s32[3,2,64,1024]{3,2,1,0:T(8,128)S(1)} %copy-done.1, f32[256,1024]{1,0:T(8,128)S(1)} %collective-permute-done.arrived.fast, f32[8]{0:T(128)S(1)} %copy-done.4, f32[2]{0:T(128)S(1)} %copy-done.5, ...), custom_call_target="tpu_custom_call" | custom-call | tf_op jit(solution)/shard_map/pallas_call | solution.py:504
  6.9 0.3 collective-permute-start.1
  7.2 4.1 %collective-permute-start.2 = (f32[16,1024]{1,0:T(8,128)S(1)}, f32[16,1024]{1,0:T(8,128)S(1)}, u32[]{:S(2)}, u32[]{:S(2)}) collective-permute-start(f32[16,1024]{1,0:T(8,128)S(1)} %get-tuple-element.29), channel_id=1, source_target_pairs={{1,2},{2,1},{3,4},{4,3},{5,6},{6,5},{9,10},{10,9},{11,12},{12,11},... | collective-permute-start | bytes 196616 | tf_op jit(solution)/shard_map/ppermute | solution.py:28
  11.3 0.0 copy-done.3
  11.4 0.1 collective-permute-start.3
  11.4 3.1 %collective-permute-start.5 = (s32[3,2,8,8]{3,2,1,0:T(8,128)S(1)}, s32[3,2,8,8]{3,2,1,0:T(8,128)S(1)}, u32[]{:S(2)}, u32[]{:S(2)}) collective-permute-start(s32[3,2,8,8]{3,2,1,0:T(8,128)S(1)} %copy-done.3), channel_id=1, source_target_pairs={{8,16},{16,8},{9,17},{17,9},{10,18},{18,10},{11,19},{19,11},{12,20... | collective-permute-start | bytes 4616 | tf_op jit(solution)/shard_map/ppermute | solution.py:28
  14.5 0.0 copy-start.2
  14.5 3.2 %shard_map.88 = (f32[3,2,64,1024]{3,2,1,0:T(8,128)S(1)}, f32[3,2,64,1024]{3,2,1,0:T(8,128)S(1)}) custom-call(f32[3,2,64,1024]{3,2,1,0:T(8,128)S(1)} %copy-done, s32[3,2,64,1024]{3,2,1,0:T(8,128)S(1)} %copy-done.1, s32[3,2,8,8]{3,2,1,0:T(8,128)S(1)} %copy-done.3, f32[10,8,128]{2,1,0:T(8,128)S(1)} %get-tuple-element.25.splat), custom_call_target="tpu_custom_call" | custom-call | tf_op jit(solution)/shard_map/pallas_call | solution.py:504
  17.8 0.0 collective-permute-done.3.before
  17.8 0.0 collective-permute-done.1.rim_a
  17.8 0.0 collective-permute-done.2.rim_b
  17.8 0.0 copy-done.2
  17.8 1.7 %shard_map.89 = (f32[3,2,64,1024]{3,2,1,0:T(8,128)S(1)}, s32[3,8,1024]{2,1,0:T(8,128)S(1)}, f32[3,2,64,1024]{3,2,1,0:T(8,128)S(1)}, f32[3,2,64,1024]{3,2,1,0:T(8,128)S(1)}, f32[256,1024]{1,0:T(8,128)S(1)}) custom-call(f32[3,2,64,1024]{3,2,1,0:T(8,128)S(1)} %copy-done, f32[3,2,64,1024]{3,2,1,0:T(8,128)S(1)} %copy-done.2, ...), custom_call_target="tpu_custom_call", output_to_operand_aliasing={{0}: (2, {})} | custom-call | tf_op jit(solution)/shard_map/pallas_call | solution.py:504
  19.5 0.0 collective-permute-done.5.before
  19.5 0.0 collective-permute-done.4.arrived
  19.5 1.3 %shard_map.90 = (f32[3,2,64,1024]{3,2,1,0:T(8,128)S(1)}, f32[3,2,64,1024]{3,2,1,0:T(8,128)S(1)}, f32[256,1024]{1,0:T(8,128)S(1)}, f32[256,1024]{1,0:T(8,128)S(1)...) custom-call(f32[3,2,64,1024]{3,2,1,0:T(8,128)S(1)} %copy-done, ...), custom_call_target="tpu_custom_call", output_to_operand_aliasing={{0}: (7, {}), {1}: (8, {}), {3}: (9, {})} | custom-call | tf_op jit(solution)/shard_map/pallas_call | solution.py:504
  20.8 0.1 collective-permute-start.6
  20.9 3.0 %collective-permute-start.9 = (f32[256,1024]{1,0:T(8,128)S(1)}, f32[256,1024]{1,0:T(8,128)S(1)}, u32[]{:S(2)}, u32[]{:S(2)}) collective-permute-start(f32[256,1024]{1,0:T(8,128)S(1)} %get-tuple-element.42), channel_id=1, source_target_pairs={{8,16},{16,8},{9,17},{17,9},{10,18},{18,10},{11,19},{19,11},{12,20... | collective-permute-start | bytes 3145736 | tf_op jit(solution)/shard_map/ppermute | solution.py:28
  23.9 0.3 collective-permute-start.7
  24.2 4.1 %collective-permute-start.8 = (f32[16,1024]{1,0:T(8,128)S(1)}, f32[16,1024]{1,0:T(8,128)S(1)}, u32[]{:S(2)}, u32[]{:S(2)}) collective-permute-start(f32[16,1024]{1,0:T(8,128)S(1)} %get-tuple-element.39), channel_id=1, source_target_pairs={{1,2},{2,1},{3,4},{4,3},{5,6},{6,5},{9,10},{10,9},{11,12},{12,11},... | collective-permute-start | bytes 196616 | tf_op jit(solution)/shard_map/ppermute | solution.py:28
  28.4 2.8 %shard_map.91.total_in = f32[3,2,64,1024]{3,2,1,0:T(8,128)S(1)} custom-call(f32[3,2,64,1024]{3,2,1,0:T(8,128)S(1)} %get-tuple-element.35.u, f32[3,2,64,1024]{3,2,1,0:T(8,128)S(1)} %get-tuple-element.36.w, f32[3,2,64,1024]{3,2,1,0:T(8,128)S(1)} %get-tuple-element.27.half, s32[3,2,8,8]{3,2,1,0:T(8,128)S(1)} %copy-done.3, f32[10,8,128]{2,1,0:T(8,128)S(1)} %get-tuple-element.25.splat), custom_call_target="tpu_custom_call" | custom-call | tf_op jit(solution)/shard_map/pallas_call | solution.py:504
  31.2 0.0 collective-permute-done.7.rim_a
  31.2 0.0 collective-permute-done.8.rim_b
  31.2 0.0 collective-permute-done.6.fast
  31.2 2.0 %shard_map.92 = (f32[3,2,64,1024]{3,2,1,0:T(8,128)S(1)}, f32[3,2,64,1024]{3,2,1,0:T(8,128)}, f32[3,2,64,1024]{3,2,1,0:T(8,128)}) custom-call(f32[3,2,64,1024]{3,2,1,0:T(8,128)S(1)} %get-tuple-element.35.u, f32[3,2,64,1024]{3,2,1,0:T(8,128)S(1)} %shard_map.91.total_in, ...), custom_call_target="tpu_custom_call", output_to_operand_aliasing={{0}: (1, {})} | custom-call | tf_op jit(solution)/shard_map/pallas_call | solution.py:504
  33.3 3.8 %collective-permute-done.9.arrived = f32[256,1024]{1,0:T(8,128)S(1)} collective-permute-done((f32[256,1024]{1,0:T(8,128)S(1)}, f32[256,1024]{1,0:T(8,128)S(1)}, u32[]{:S(2)}, u32[]{:S(2)}) %collective-permute-start.9) | collective-permute-done | bytes 1048608 | tf_op jit(solution)/shard_map/ppermute | solution.py:28
  37.0 2.0 %shard_map.93 = (f32[3,2,64,1024]{3,2,1,0:T(8,128)}, f32[3,2,64,1024]{3,2,1,0:T(8,128)}) custom-call(f32[3,2,64,1024]{3,2,1,0:T(8,128)S(1)} %get-tuple-element.35.u, f32[3,2,64,1024]{3,2,1,0:T(8,128)S(1)} %get-tuple-element.41.total, f32[256,1024]{1,0:T(8,128)S(1)} %collective-permute-done.9.arrived, ...), custom_call_target="tpu_custom_call", output_to_operand_aliasing={{0}: (5, {}), {1}: (6, {})} | custom-call | tf_op jit(solution)/shard_map/pallas_call | solution.py:504
Async XLA Ops:
  0.6 1.4 %copy-start = (f32[3,2,64,1024]{3,2,1,0:T(8,128)S(1)}, f32[3,2,64,1024]{3,2,1,0:T(8,128)}, u32[]{:S(2)}) copy-start(f32[3,2,64,1024]{3,2,1,0:T(8,128)} %u.9) | copy-start | bytes 4718596
  2.0 4.1 %copy-start.1 = (s32[3,2,64,1024]{3,2,1,0:T(8,128)S(1)}, s32[3,2,64,1024]{3,2,1,0:T(8,128)}, u32[]{:S(2)}) copy-start(s32[3,2,64,1024]{3,2,1,0:T(8,128)} %cls.3) | copy-start | bytes 4718596
  2.0 4.1 %copy-start.4 = (f32[8]{0:T(128)S(1)}, f32[8]{0:T(128)}, u32[]{:S(2)}) copy-start(f32[8]{0:T(128)} %stiff.1) | copy-start | bytes 100
  2.0 4.1 %copy-start.5 = (f32[2]{0:T(128)S(1)}, f32[2]{0:T(128)}, u32[]{:S(2)}) copy-start(f32[2]{0:T(128)} %cross.1) | copy-start | bytes 28
  2.0 4.1 %copy-start.6 = (s32[3]{0:T(128)S(1)}, s32[3]{0:T(128)}, u32[]{:S(2)}) copy-start(s32[3]{0:T(128)} %fixed.1) | copy-start | bytes 40
  2.2 3.9 %collective-permute-start = (f32[256,1024]{1,0:T(8,128)S(1)}, f32[256,1024]{1,0:T(8,128)S(1)}, u32[]{:S(2)}, u32[]{:S(2)}) collective-permute-start(f32[256,1024]{1,0:T(8,128)S(1)} %get-tuple-element.24), channel_id=1, source_target_pairs={{0,8},{8,0},{16,24},{24,16},{1,9},{9,1},{17,25},{25,17},{2,10},{10... | collective-permute-start | bytes 3145736 | tf_op jit(solution)/shard_map/ppermute | solution.py:28
  3.0 8.4 %copy-start.3 = (s32[3,2,8,8]{3,2,1,0:T(8,128)S(1)}, s32[3,2,8,8]{3,2,1,0:T(8,128)}, u32[]{:S(2)}) copy-start(s32[3,2,8,8]{3,2,1,0:T(8,128)} %shift.7) | copy-start | bytes 4612
  3.0 16.6 %collective-permute-start.4 = (f32[256,1024]{1,0:T(8,128)S(1)}, f32[256,1024]{1,0:T(8,128)S(1)}, u32[]{:S(2)}, u32[]{:S(2)}) collective-permute-start(f32[256,1024]{1,0:T(8,128)S(1)} %get-tuple-element.31), channel_id=1, source_target_pairs={{8,16},{16,8},{9,17},{17,9},{10,18},{18,10},{11,19},{19,11},{12,20... | collective-permute-start | bytes 3145736 | tf_op jit(solution)/shard_map/ppermute | solution.py:28
  6.9 10.9 %collective-permute-start.1 = (f32[16,1024]{1,0:T(8,128)S(1)}, f32[16,1024]{1,0:T(8,128)S(1)}, u32[]{:S(2)}, u32[]{:S(2)}) collective-permute-start(f32[16,1024]{1,0:T(8,128)S(1)} %get-tuple-element.28), channel_id=1, source_target_pairs={{0,1},{1,0},{2,3},{3,2},{4,5},{5,4},{6,7},{7,6},{8,9},{9,8},{10,11... | collective-permute-start | bytes 196616 | tf_op jit(solution)/shard_map/ppermute | solution.py:28
  7.2 10.6 %collective-permute-start.2 = (f32[16,1024]{1,0:T(8,128)S(1)}, f32[16,1024]{1,0:T(8,128)S(1)}, u32[]{:S(2)}, u32[]{:S(2)}) collective-permute-start(f32[16,1024]{1,0:T(8,128)S(1)} %get-tuple-element.29), channel_id=1, source_target_pairs={{1,2},{2,1},{3,4},{4,3},{5,6},{6,5},{9,10},{10,9},{11,12},{12,11},... | collective-permute-start | bytes 196616 | tf_op jit(solution)/shard_map/ppermute | solution.py:28
  11.4 6.4 %collective-permute-start.3 = (s32[3,2,8,8]{3,2,1,0:T(8,128)S(1)}, s32[3,2,8,8]{3,2,1,0:T(8,128)S(1)}, u32[]{:S(2)}, u32[]{:S(2)}) collective-permute-start(s32[3,2,8,8]{3,2,1,0:T(8,128)S(1)} %copy-done.3), channel_id=1, source_target_pairs={{0,8},{8,0},{16,24},{24,16},{1,9},{9,1},{17,25},{25,17},{2,10},{10... | collective-permute-start | bytes 4616 | tf_op jit(solution)/shard_map/ppermute | solution.py:28
  11.4 8.1 %collective-permute-start.5 = (s32[3,2,8,8]{3,2,1,0:T(8,128)S(1)}, s32[3,2,8,8]{3,2,1,0:T(8,128)S(1)}, u32[]{:S(2)}, u32[]{:S(2)}) collective-permute-start(s32[3,2,8,8]{3,2,1,0:T(8,128)S(1)} %copy-done.3), channel_id=1, source_target_pairs={{8,16},{16,8},{9,17},{17,9},{10,18},{18,10},{11,19},{19,11},{12,20... | collective-permute-start | bytes 4616 | tf_op jit(solution)/shard_map/ppermute | solution.py:28
  14.5 3.3 %copy-start.2 = (f32[3,2,64,1024]{3,2,1,0:T(8,128)S(1)}, f32[3,2,64,1024]{3,2,1,0:T(8,128)}, u32[]{:S(2)}) copy-start(f32[3,2,64,1024]{3,2,1,0:T(8,128)} %w.1) | copy-start | bytes 4718596
  20.8 10.4 %collective-permute-start.6 = (f32[256,1024]{1,0:T(8,128)S(1)}, f32[256,1024]{1,0:T(8,128)S(1)}, u32[]{:S(2)}, u32[]{:S(2)}) collective-permute-start(f32[256,1024]{1,0:T(8,128)S(1)} %get-tuple-element.37), channel_id=1, source_target_pairs={{0,8},{8,0},{16,24},{24,16},{1,9},{9,1},{17,25},{25,17},{2,10},{10... | collective-permute-start | bytes 3145736 | tf_op jit(solution)/shard_map/ppermute | solution.py:28
  20.9 16.1 %collective-permute-start.9 = (f32[256,1024]{1,0:T(8,128)S(1)}, f32[256,1024]{1,0:T(8,128)S(1)}, u32[]{:S(2)}, u32[]{:S(2)}) collective-permute-start(f32[256,1024]{1,0:T(8,128)S(1)} %get-tuple-element.42), channel_id=1, source_target_pairs={{8,16},{16,8},{9,17},{17,9},{10,18},{18,10},{11,19},{19,11},{12,20... | collective-permute-start | bytes 3145736 | tf_op jit(solution)/shard_map/ppermute | solution.py:28
  23.9 7.3 %collective-permute-start.7 = (f32[16,1024]{1,0:T(8,128)S(1)}, f32[16,1024]{1,0:T(8,128)S(1)}, u32[]{:S(2)}, u32[]{:S(2)}) collective-permute-start(f32[16,1024]{1,0:T(8,128)S(1)} %get-tuple-element.38), channel_id=1, source_target_pairs={{0,1},{1,0},{2,3},{3,2},{4,5},{5,4},{6,7},{7,6},{8,9},{9,8},{10,11... | collective-permute-start | bytes 196616 | tf_op jit(solution)/shard_map/ppermute | solution.py:28
  24.2 7.0 %collective-permute-start.8 = (f32[16,1024]{1,0:T(8,128)S(1)}, f32[16,1024]{1,0:T(8,128)S(1)}, u32[]{:S(2)}, u32[]{:S(2)}) collective-permute-start(f32[16,1024]{1,0:T(8,128)S(1)} %get-tuple-element.39), channel_id=1, source_target_pairs={{1,2},{2,1},{3,4},{4,3},{5,6},{6,5},{9,10},{10,9},{11,12},{12,11},... | collective-permute-start | bytes 196616 | tf_op jit(solution)/shard_map/ppermute | solution.py:28

commit v10 on v7

--- a/solution.py
+++ b/solution.py
@@ -456,7 +456,7 @@
     sections, _, rows, width = u.shape
     height = arrived.shape[0] // 4
     rbs = height // ROWS
-    part = rbs // 2 if rbs % 2 == 0 else rbs
+    part = max(rbs // 4, 1) if rbs % max(rbs // 4, 1) == 0 else rbs
 
     def body(after):
         copies = []
@@ -566,7 +566,7 @@
             [u, total, slow, index, splat, out_u, out_w],
             {5: 0, 6: 1},
             scratch=[pltpu.VMEM((2, 2, rows, width), jnp.float32)] * 2
-            + [pltpu.SemaphoreType.DMA((8,))],
+            + [pltpu.SemaphoreType.DMA((4 * (rows // ROWS),))],
             in_specs=[VMEM] * 5 + [ANY] * 2,
             out_specs=[ANY] * 2,
         )

time: 39.7 us -> 39.9 us (level)
  no operation moved by 1% of the time
where the time goes in v10:
time: 39.9 us; the launch traced here: 39.3 us
  starting transfers between devices  19.1 us (48%)
  Pallas kernels  13.9 us (35%)
  waiting for transfers between devices  3.93 us (10%)
  local copies, waits for them, and re-layouts  1.43 us (4%)
  between operations  1.03 us (3%)
    ppermute x10, starting transfers between devices, exchange(): return lax.ppermute(value, axis, route)  19.1 us
    pallas_call x8, Pallas kernels, call(): pl.pallas_call(kernel, out_shape=outs, in_specs=in_specs or [VMEM] * len(...  13.9 us
    ppermute x10, waiting for transfers between devices, exchange(): return lax.ppermute(value, axis, route)  3.93 us
    unnamed x14, local copies, waits for them, and re-layouts  1.43 us
  transfers between devices with their start and end apart: 10, of which 2 were waited for; matrix products, arithmetic and copies ran while one was open for 0% of the time, Pallas kernels for 26%

profile of v10, /device:TPU:3, one launch (start us, length us, event | category | flops | bytes accessed | tf_op | source)
XLA Modules:
  0.0 39.3 jit_solution(11780358086827442049)
XLA Ops:
  0.6 0.0 copy-start
  0.6 1.4 %copy-done = f32[3,2,64,1024]{3,2,1,0:T(8,128)S(1)} copy-done((f32[3,2,64,1024]{3,2,1,0:T(8,128)S(1)}, f32[3,2,64,1024]{3,2,1,0:T(8,128)}, u32[]{:S(2)}) %copy-start) | copy-done | bytes 1572888
  2.0 0.0 copy-start.1
  2.0 0.0 copy-start.4
  2.0 0.0 copy-start.5
  2.0 0.0 copy-start.6
  2.1 0.2 shard_map.86
  2.2 0.7 %collective-permute-start = (f32[256,1024]{1,0:T(8,128)S(1)}, f32[256,1024]{1,0:T(8,128)S(1)}, u32[]{:S(2)}, u32[]{:S(2)}) collective-permute-start(f32[256,1024]{1,0:T(8,128)S(1)} %get-tuple-element.21), channel_id=1, source_target_pairs={{0,8},{8,0},{16,24},{24,16},{1,9},{9,1},{17,25},{25,17},{2,10},{10... | collective-permute-start | bytes 3145736 | tf_op jit(solution)/shard_map/ppermute | solution.py:28
  3.0 0.0 copy-start.3
  3.0 3.2 %collective-permute-start.4 = (f32[256,1024]{1,0:T(8,128)S(1)}, f32[256,1024]{1,0:T(8,128)S(1)}, u32[]{:S(2)}, u32[]{:S(2)}) collective-permute-start(f32[256,1024]{1,0:T(8,128)S(1)} %get-tuple-element.28), channel_id=1, source_target_pairs={{8,16},{16,8},{9,17},{17,9},{10,18},{18,10},{11,19},{19,11},{12,20... | collective-permute-start | bytes 3145736 | tf_op jit(solution)/shard_map/ppermute | solution.py:28
  6.2 0.0 collective-permute-done.arrived.fast
  6.2 0.0 copy-done.1
  6.2 0.0 copy-done.4
  6.2 0.0 copy-done.5
  6.2 0.0 copy-done.6
  6.2 0.7 %shard_map.87 = (f32[16,1024]{1,0:T(8,128)S(1)}, f32[16,1024]{1,0:T(8,128)S(1)}, f32[10,8,128]{2,1,0:T(8,128)S(1)}) custom-call(f32[3,2,64,1024]{3,2,1,0:T(8,128)S(1)} %copy-done, s32[3,2,64,1024]{3,2,1,0:T(8,128)S(1)} %copy-done.1, f32[256,1024]{1,0:T(8,128)S(1)} %collective-permute-done.arrived.fast, f32[8]{0:T(128)S(1)} %copy-done.4, f32[2]{0:T(128)S(1)} %copy-done.5, ...), custom_call_target="tpu_custom_call" | custom-call | tf_op jit(solution)/shard_map/pallas_call | solution.py:489
  6.9 0.3 collective-permute-start.1
  7.2 4.1 %collective-permute-start.2 = (f32[16,1024]{1,0:T(8,128)S(1)}, f32[16,1024]{1,0:T(8,128)S(1)}, u32[]{:S(2)}, u32[]{:S(2)}) collective-permute-start(f32[16,1024]{1,0:T(8,128)S(1)} %get-tuple-element.26), channel_id=1, source_target_pairs={{1,2},{2,1},{3,4},{4,3},{5,6},{6,5},{9,10},{10,9},{11,12},{12,11},... | collective-permute-start | bytes 196616 | tf_op jit(solution)/shard_map/ppermute | solution.py:28
  11.3 0.0 copy-done.3
  11.4 0.1 collective-permute-start.3
  11.4 3.1 %collective-permute-start.5 = (s32[3,2,8,8]{3,2,1,0:T(8,128)S(1)}, s32[3,2,8,8]{3,2,1,0:T(8,128)S(1)}, u32[]{:S(2)}, u32[]{:S(2)}) collective-permute-start(s32[3,2,8,8]{3,2,1,0:T(8,128)S(1)} %copy-done.3), channel_id=1, source_target_pairs={{8,16},{16,8},{9,17},{17,9},{10,18},{18,10},{11,19},{19,11},{12,20... | collective-permute-start | bytes 4616 | tf_op jit(solution)/shard_map/ppermute | solution.py:28
  14.5 0.0 copy-start.2
  14.5 3.2 %shard_map.88 = (f32[3,2,64,1024]{3,2,1,0:T(8,128)S(1)}, f32[3,2,64,1024]{3,2,1,0:T(8,128)S(1)}) custom-call(f32[3,2,64,1024]{3,2,1,0:T(8,128)S(1)} %copy-done, s32[3,2,64,1024]{3,2,1,0:T(8,128)S(1)} %copy-done.1, s32[3,2,8,8]{3,2,1,0:T(8,128)S(1)} %copy-done.3, f32[10,8,128]{2,1,0:T(8,128)S(1)} %get-tuple-element.22.splat), custom_call_target="tpu_custom_call" | custom-call | tf_op jit(solution)/shard_map/pallas_call | solution.py:489
  17.8 0.0 collective-permute-done.3.before
  17.8 0.0 collective-permute-done.1.rim_a
  17.8 0.0 collective-permute-done.2.rim_b
  17.8 0.0 copy-done.2
  17.8 1.6 %shard_map.89 = (f32[3,2,64,1024]{3,2,1,0:T(8,128)S(1)}, s32[3,8,1024]{2,1,0:T(8,128)S(1)}) custom-call(f32[3,2,64,1024]{3,2,1,0:T(8,128)S(1)} %copy-done, f32[3,2,64,1024]{3,2,1,0:T(8,128)S(1)} %copy-done.2, f32[3,2,64,1024]{3,2,1,0:T(8,128)S(1)} %get-tuple-element.23.total_in, ...), custom_call_target="tpu_custom_call", output_to_operand_aliasing={{0}: (2, {})} | custom-call | tf_op jit(solution)/shard_map/pallas_call | solution.py:489
  19.4 0.1 collective-permute-done.5.before
  19.5 0.0 collective-permute-done.4.arrived
  19.5 1.3 %shard_map.90 = (f32[3,2,64,1024]{3,2,1,0:T(8,128)S(1)}, f32[3,2,64,1024]{3,2,1,0:T(8,128)S(1)}, f32[256,1024]{1,0:T(8,128)S(1)}, f32[256,1024]{1,0:T(8,128)S(1)...) custom-call(f32[3,2,64,1024]{3,2,1,0:T(8,128)S(1)} %copy-done, ...), custom_call_target="tpu_custom_call" | custom-call | tf_op jit(solution)/shard_map/pallas_call | solution.py:489
  20.8 0.1 collective-permute-start.6
  20.9 3.1 %collective-permute-start.9 = (f32[256,1024]{1,0:T(8,128)S(1)}, f32[256,1024]{1,0:T(8,128)S(1)}, u32[]{:S(2)}, u32[]{:S(2)}) collective-permute-start(f32[256,1024]{1,0:T(8,128)S(1)} %get-tuple-element.36), channel_id=1, source_target_pairs={{8,16},{16,8},{9,17},{17,9},{10,18},{18,10},{11,19},{19,11},{12,20... | collective-permute-start | bytes 3145736 | tf_op jit(solution)/shard_map/ppermute | solution.py:28
  24.0 0.3 collective-permute-start.7
  24.3 4.1 %collective-permute-start.8 = (f32[16,1024]{1,0:T(8,128)S(1)}, f32[16,1024]{1,0:T(8,128)S(1)}, u32[]{:S(2)}, u32[]{:S(2)}) collective-permute-start(f32[16,1024]{1,0:T(8,128)S(1)} %get-tuple-element.33), channel_id=1, source_target_pairs={{1,2},{2,1},{3,4},{4,3},{5,6},{6,5},{9,10},{10,9},{11,12},{12,11},... | collective-permute-start | bytes 196616 | tf_op jit(solution)/shard_map/ppermute | solution.py:28
  28.4 2.8 %shard_map.91.total_in = f32[3,2,64,1024]{3,2,1,0:T(8,128)S(1)} custom-call(f32[3,2,64,1024]{3,2,1,0:T(8,128)S(1)} %get-tuple-element.29.u, f32[3,2,64,1024]{3,2,1,0:T(8,128)S(1)} %get-tuple-element.30.w, f32[3,2,64,1024]{3,2,1,0:T(8,128)S(1)} %get-tuple-element.24.half, s32[3,2,8,8]{3,2,1,0:T(8,128)S(1)} %copy-done.3, f32[10,8,128]{2,1,0:T(8,128)S(1)} %get-tuple-element.22.splat), custom_call_target="tpu_custom_call" | custom-call | tf_op jit(solution)/shard_map/pallas_call | solution.py:489
  31.3 0.0 collective-permute-done.7.rim_a
  31.3 0.0 collective-permute-done.8.rim_b
  31.3 0.0 collective-permute-done.6.fast
  31.3 1.9 %shard_map.92 = (f32[3,2,64,1024]{3,2,1,0:T(8,128)S(1)}, f32[3,2,64,1024]{3,2,1,0:T(8,128)}, f32[3,2,64,1024]{3,2,1,0:T(8,128)}) custom-call(f32[3,2,64,1024]{3,2,1,0:T(8,128)S(1)} %get-tuple-element.29.u, f32[3,2,64,1024]{3,2,1,0:T(8,128)S(1)} %shard_map.91.total_in, ...), custom_call_target="tpu_custom_call", output_to_operand_aliasing={{0}: (1, {})} | custom-call | tf_op jit(solution)/shard_map/pallas_call | solution.py:489
  33.2 3.9 %collective-permute-done.9.arrived = f32[256,1024]{1,0:T(8,128)S(1)} collective-permute-done((f32[256,1024]{1,0:T(8,128)S(1)}, f32[256,1024]{1,0:T(8,128)S(1)}, u32[]{:S(2)}, u32[]{:S(2)}) %collective-permute-start.9) | collective-permute-done | bytes 1048608 | tf_op jit(solution)/shard_map/ppermute | solution.py:28
  37.0 2.2 %shard_map.93 = (f32[3,2,64,1024]{3,2,1,0:T(8,128)}, f32[3,2,64,1024]{3,2,1,0:T(8,128)}) custom-call(f32[3,2,64,1024]{3,2,1,0:T(8,128)S(1)} %get-tuple-element.29.u, f32[3,2,64,1024]{3,2,1,0:T(8,128)S(1)} %get-tuple-element.35.total, f32[256,1024]{1,0:T(8,128)S(1)} %collective-permute-done.9.arrived, ...), custom_call_target="tpu_custom_call", output_to_operand_aliasing={{0}: (5, {}), {1}: (6, {})} | custom-call | tf_op jit(solution)/shard_map/pallas_call | solution.py:489
Async XLA Ops:
  0.6 1.4 %copy-start = (f32[3,2,64,1024]{3,2,1,0:T(8,128)S(1)}, f32[3,2,64,1024]{3,2,1,0:T(8,128)}, u32[]{:S(2)}) copy-start(f32[3,2,64,1024]{3,2,1,0:T(8,128)} %u.9) | copy-start | bytes 4718596
  2.0 4.1 %copy-start.1 = (s32[3,2,64,1024]{3,2,1,0:T(8,128)S(1)}, s32[3,2,64,1024]{3,2,1,0:T(8,128)}, u32[]{:S(2)}) copy-start(s32[3,2,64,1024]{3,2,1,0:T(8,128)} %cls.3) | copy-start | bytes 4718596
  2.0 4.1 %copy-start.4 = (f32[8]{0:T(128)S(1)}, f32[8]{0:T(128)}, u32[]{:S(2)}) copy-start(f32[8]{0:T(128)} %stiff.1) | copy-start | bytes 100
  2.0 4.1 %copy-start.5 = (f32[2]{0:T(128)S(1)}, f32[2]{0:T(128)}, u32[]{:S(2)}) copy-start(f32[2]{0:T(128)} %cross.1) | copy-start | bytes 28
  2.0 4.1 %copy-start.6 = (s32[3]{0:T(128)S(1)}, s32[3]{0:T(128)}, u32[]{:S(2)}) copy-start(s32[3]{0:T(128)} %fixed.1) | copy-start | bytes 40
  2.2 3.9 %collective-permute-start = (f32[256,1024]{1,0:T(8,128)S(1)}, f32[256,1024]{1,0:T(8,128)S(1)}, u32[]{:S(2)}, u32[]{:S(2)}) collective-permute-start(f32[256,1024]{1,0:T(8,128)S(1)} %get-tuple-element.21), channel_id=1, source_target_pairs={{0,8},{8,0},{16,24},{24,16},{1,9},{9,1},{17,25},{25,17},{2,10},{10... | collective-permute-start | bytes 3145736 | tf_op jit(solution)/shard_map/ppermute | solution.py:28
  3.0 8.4 %copy-start.3 = (s32[3,2,8,8]{3,2,1,0:T(8,128)S(1)}, s32[3,2,8,8]{3,2,1,0:T(8,128)}, u32[]{:S(2)}) copy-start(s32[3,2,8,8]{3,2,1,0:T(8,128)} %shift.7) | copy-start | bytes 4612
  3.0 16.5 %collective-permute-start.4 = (f32[256,1024]{1,0:T(8,128)S(1)}, f32[256,1024]{1,0:T(8,128)S(1)}, u32[]{:S(2)}, u32[]{:S(2)}) collective-permute-start(f32[256,1024]{1,0:T(8,128)S(1)} %get-tuple-element.28), channel_id=1, source_target_pairs={{8,16},{16,8},{9,17},{17,9},{10,18},{18,10},{11,19},{19,11},{12,20... | collective-permute-start | bytes 3145736 | tf_op jit(solution)/shard_map/ppermute | solution.py:28
  6.9 10.9 %collective-permute-start.1 = (f32[16,1024]{1,0:T(8,128)S(1)}, f32[16,1024]{1,0:T(8,128)S(1)}, u32[]{:S(2)}, u32[]{:S(2)}) collective-permute-start(f32[16,1024]{1,0:T(8,128)S(1)} %get-tuple-element.25), channel_id=1, source_target_pairs={{0,1},{1,0},{2,3},{3,2},{4,5},{5,4},{6,7},{7,6},{8,9},{9,8},{10,11... | collective-permute-start | bytes 196616 | tf_op jit(solution)/shard_map/ppermute | solution.py:28
  7.2 10.6 %collective-permute-start.2 = (f32[16,1024]{1,0:T(8,128)S(1)}, f32[16,1024]{1,0:T(8,128)S(1)}, u32[]{:S(2)}, u32[]{:S(2)}) collective-permute-start(f32[16,1024]{1,0:T(8,128)S(1)} %get-tuple-element.26), channel_id=1, source_target_pairs={{1,2},{2,1},{3,4},{4,3},{5,6},{6,5},{9,10},{10,9},{11,12},{12,11},... | collective-permute-start | bytes 196616 | tf_op jit(solution)/shard_map/ppermute | solution.py:28
  11.4 6.4 %collective-permute-start.3 = (s32[3,2,8,8]{3,2,1,0:T(8,128)S(1)}, s32[3,2,8,8]{3,2,1,0:T(8,128)S(1)}, u32[]{:S(2)}, u32[]{:S(2)}) collective-permute-start(s32[3,2,8,8]{3,2,1,0:T(8,128)S(1)} %copy-done.3), channel_id=1, source_target_pairs={{0,8},{8,0},{16,24},{24,16},{1,9},{9,1},{17,25},{25,17},{2,10},{10... | collective-permute-start | bytes 4616 | tf_op jit(solution)/shard_map/ppermute | solution.py:28
  11.4 8.0 %collective-permute-start.5 = (s32[3,2,8,8]{3,2,1,0:T(8,128)S(1)}, s32[3,2,8,8]{3,2,1,0:T(8,128)S(1)}, u32[]{:S(2)}, u32[]{:S(2)}) collective-permute-start(s32[3,2,8,8]{3,2,1,0:T(8,128)S(1)} %copy-done.3), channel_id=1, source_target_pairs={{8,16},{16,8},{9,17},{17,9},{10,18},{18,10},{11,19},{19,11},{12,20... | collective-permute-start | bytes 4616 | tf_op jit(solution)/shard_map/ppermute | solution.py:28
  14.5 3.3 %copy-start.2 = (f32[3,2,64,1024]{3,2,1,0:T(8,128)S(1)}, f32[3,2,64,1024]{3,2,1,0:T(8,128)}, u32[]{:S(2)}) copy-start(f32[3,2,64,1024]{3,2,1,0:T(8,128)} %w.1) | copy-start | bytes 4718596
  20.8 10.5 %collective-permute-start.6 = (f32[256,1024]{1,0:T(8,128)S(1)}, f32[256,1024]{1,0:T(8,128)S(1)}, u32[]{:S(2)}, u32[]{:S(2)}) collective-permute-start(f32[256,1024]{1,0:T(8,128)S(1)} %get-tuple-element.31), channel_id=1, source_target_pairs={{0,8},{8,0},{16,24},{24,16},{1,9},{9,1},{17,25},{25,17},{2,10},{10... | collective-permute-start | bytes 3145736 | tf_op jit(solution)/shard_map/ppermute | solution.py:28
  20.9 16.1 %collective-permute-start.9 = (f32[256,1024]{1,0:T(8,128)S(1)}, f32[256,1024]{1,0:T(8,128)S(1)}, u32[]{:S(2)}, u32[]{:S(2)}) collective-permute-start(f32[256,1024]{1,0:T(8,128)S(1)} %get-tuple-element.36), channel_id=1, source_target_pairs={{8,16},{16,8},{9,17},{17,9},{10,18},{18,10},{11,19},{19,11},{12,20... | collective-permute-start | bytes 3145736 | tf_op jit(solution)/shard_map/ppermute | solution.py:28
  24.0 7.3 %collective-permute-start.7 = (f32[16,1024]{1,0:T(8,128)S(1)}, f32[16,1024]{1,0:T(8,128)S(1)}, u32[]{:S(2)}, u32[]{:S(2)}) collective-permute-start(f32[16,1024]{1,0:T(8,128)S(1)} %get-tuple-element.32), channel_id=1, source_target_pairs={{0,1},{1,0},{2,3},{3,2},{4,5},{5,4},{6,7},{7,6},{8,9},{9,8},{10,11... | collective-permute-start | bytes 196616 | tf_op jit(solution)/shard_map/ppermute | solution.py:28
  24.3 7.0 %collective-permute-start.8 = (f32[16,1024]{1,0:T(8,128)S(1)}, f32[16,1024]{1,0:T(8,128)S(1)}, u32[]{:S(2)}, u32[]{:S(2)}) collective-permute-start(f32[16,1024]{1,0:T(8,128)S(1)} %get-tuple-element.33), channel_id=1, source_target_pairs={{1,2},{2,1},{3,4},{4,3},{5,6},{6,5},{9,10},{10,9},{11,12},{12,11},... | collective-permute-start | bytes 196616 | tf_op jit(solution)/shard_map/ppermute | solution.py:28
